TPU v7x, 512 devices: a whole 4x4x16 slice. The times are simulated.
512 devices in a mesh: gx: 64 (over x, z), gy: 8 (over y, core).
Axes of the slice: x: 4, y: 4, z: 16, core: 2. Of those that a mesh axis runs over, the one named last changes fastest.
Arguments:
- residual: float32 [1, 2048, 128, 128], P(None, 'gx', 'gy'), may hold values from -6 to 6
- elem_class: int32 [256, 16, 16], P('gx', 'gy'), may hold values from 0 to 7
- basis: float32 [8, 3, 10, 10], replicated, may hold values from -2 to 2
- eigenvalues: float32 [8, 3, 10], replicated, may hold values from 0.1 to 3
- vertex_number: int32 [320, 24, 17], P('gx', 'gy'), may hold values from 0 to 254, as said below
- panels: float32 [16320, 23544], P('gx', 'gy'), may hold values from -1 to 1
Outputs:
- correction: float32 [1, 2048, 128, 128], P(None, 'gx', 'gy')
Inputs may be any that keep to these rules, and one draw needn't show every extreme that they name: `vertex_number`: within each block of (5) x (3) x (17) entries, the block (p, q) starting at (5) p and (3) q, every number 0 to 254 appears once.
All inputs are finite; a program needn't handle non-finite values.
Results may differ from a plain program's by a relative error of at most 0.0001.
Values sent between devices are 32-bit elements; how exact they have to be, the bound alone decides.
No kernel may reach another device: no remote copies, remote signals or barrier semaphores. Data moves between devices by JAX's collectives and lax.ppermute only.
A program may use at most 128 MiB of HBM per device.

v0:
```python
import functools

import jax
import jax.numpy as jnp
from jax import lax
from jax.experimental import pallas as pl
from jax.experimental.pallas import tpu as pltpu
from jax.sharding import PartitionSpec as P

NPR = 8
NEXT = 10
NCLASS = 8
LANES = 128
HALO = NPR + 1
F32 = jnp.float32
exact = lax.Precision.HIGHEST
ORDER = (1, 2, 3, 4, 5, 6, 7, 8, 0, 9)


def iota(shape, axis):
    return lax.broadcasted_iota(jnp.int32, shape, axis)


def hat(point, vertex):
    place = (point.astype(F32) + 0.5) / NPR
    return jnp.maximum(0.0, 1.0 - jnp.abs(place - vertex.astype(F32)))


def plane_hat(point, vertex):
    third = (vertex.astype(F32) + 0.5) / 3.0
    big = third.astype(jnp.int32)
    return hat(point >> 4, big) * hat(point & 15, vertex - 3 * big)


def down_kernel(res_ref, num_ref, pan_ref, pay_ref, own_ref, line_ref):
    q = lax.axis_index("gy")
    plane = plane_hat(iota((16, 512), 1), iota((16, 512), 0))
    depth = hat(iota((128, 17), 0), iota((128, 17), 1))
    half = jnp.dot(plane, res_ref[...], precision=exact)
    vertex = jnp.dot(half, depth, precision=exact)
    rows = iota((256, 17), 0)
    spread = jnp.zeros((256, 17), F32)
    for i in range(5):
        for j in range(3):
            k = 3 * i + j
            spread = spread + jnp.where(num_ref[i, j : j + 1, :] == rows, vertex[k : k + 1, :], 0.0)
    ordered = jnp.broadcast_to(jnp.sum(spread, axis=1, keepdims=True), (256, LANES))
    line_ref[...] = jnp.zeros((40, LANES), F32)
    for c in range(23):
        low = c * LANES
        width = min(LANES, 2943 - low)
        piece = jnp.sum(pan_ref[:, low : low + width] * ordered[:255, :width], axis=0, keepdims=True)
        line_ref[8 + c : 9 + c, :width] = piece
    here = pltpu.roll(line_ref[8:32], 1, 1)
    before = pltpu.roll(line_ref[7:31], 1, 1)
    own_ref[...] = jnp.where(iota((24, LANES), 1) == 0, before, here)
    low_face = res_ref[pl.ds(0, 32, stride=16), :]
    high_face = res_ref[pl.ds(15, 32, stride=16), :]
    for peer in range(8):
        pay_ref[peer, 0:32, :] = jnp.where(peer < q, low_face, high_face)
        pay_ref[peer, 32:35, :] = own_ref[2:5, :]
        if peer < 6:
            pay_ref[peer, 35:38, :] = own_ref[5 + 3 * peer : 8 + 3 * peer, :]
            pay_ref[peer, 38:40, :] = jnp.zeros((2, LANES), F32)
        else:
            pay_ref[peer, 35:40, :] = jnp.zeros((5, LANES), F32)


def share_kernel(got_ref, res_ref, cls_ref, right_ref, left_ref, tree_ref, face_ref):
    q = lax.axis_index("gy")
    face_ref[0:32, :] = jnp.where(q > 0, got_ref[jnp.maximum(q - 1, 0), 0:32, :], 0.0)
    face_ref[32:64, :] = jnp.where(q < 7, got_ref[jnp.minimum(q + 1, 7), 0:32, :], 0.0)
    for ref, column, first in ((right_ref, 3, 23), (left_ref, 0, 0)):
        ref[0:144, :] = res_ref[16 * first : 16 * first + 144, :]
        ref[144:153, :] = face_ref[first : first + 9, :]
        ref[153:162, :] = face_ref[32 + first : 41 + first, :]
        ref[162:168, :] = jnp.zeros((6, LANES), F32)
        ref[162:164, 0:16] = (cls_ref[column] + 1).astype(F32)
    total = got_ref[0, 35:38, :]
    for peer in range(1, 8):
        total = total + got_ref[peer, 35:38, :]
    line = jnp.concatenate([total[0:1], total[1:2], total[2:3]], axis=1)
    for t in range(64):
        tree_ref[t] = line


def shuffled(tile, first, second, third):
    tile = jnp.take_along_axis(tile, first, axis=1, mode="promise_in_bounds")
    tile = jnp.take_along_axis(tile, second, axis=0, mode="promise_in_bounds")
    return jnp.take_along_axis(tile, third, axis=1, mode="promise_in_bounds")


def fine_kernel(
    res_ref, face_ref, from_left, from_right, cls_ref, basis_ref, value_ref,
    fine_ref, rim_ref,
    rows_m, rows_e, win_m, win_e, pick_m, pick_e, eig_m, eig_e, zfwd_m, zback_m, zfwd_e, zback_e,
    half_e, lxe, work, tmp_a, tmp_b, tmp_c, edge, out_rows, rim_rows,
):
    sub = iota((8, LANES), 0)
    lane = iota((8, LANES), 1)
    wide = iota((16, LANES), 1)
    kz = lane & 15

    for ix in range(4):
        for jy in range(2):
            r = 2 * ix + jy
            for i in range(8):
                rows_m[pl.ds(i * 8 + r, 8, stride=64), :] = res_ref[pl.ds(128 * ix + 16 * i + 8 * jy, 8), :]
            rows_m[pl.ds(512 + r, 8, stride=8), :] = face_ref[pl.ds(32 * jy + 8 * ix, 8), :]
    for side, ref in ((0, from_left), (1, from_right)):
        for layer in range(9):
            i = (layer + 8) % 9 if side == 0 else layer
            for jy in range(2):
                part = ref[pl.ds(16 * layer + 8 * jy, 8), :]
                outer = ref[pl.ds(144 + 9 * jy + layer, 1), :]
                for r in (2 * side + jy, 4 + 2 * side + jy):
                    rows_e[pl.ds(i * 8 + r, 8, stride=72), :] = part
                    rows_e[pl.ds((72 + i) * 8 + r, 1), :] = outer

    group = iota((8, LANES), 0)
    spread = (iota((16, LANES), 0) == (iota((16, LANES), 1) & 15)).astype(F32)
    kinds = jnp.concatenate([cls_ref[ix].astype(F32) + 1.0 for ix in range(4)], axis=0)
    near = [from_left[162:164, 0:16], from_right[162:164, 0:16]]
    kinds_e = jnp.concatenate(near + near, axis=0)
    for kind, pick, eig in ((kinds, pick_m, eig_m), (kinds_e, pick_e, eig_e)):
        laid = jnp.dot(kind, spread, precision=exact)
        laid = jnp.sum(jnp.where(group == (lane >> 4), laid, 0.0), axis=0, keepdims=True)
        onehot = (laid == (group + 1).astype(F32)).astype(F32)
        dims = (((0,), (0,)), ((), ()))
        pick[0:300, :] = lax.dot_general(basis_ref[...], onehot, dims, precision=exact, preferred_element_type=F32)
        eig[0:30, :] = lax.dot_general(value_ref[...], onehot, dims, precision=exact, preferred_element_type=F32)
        empty = jnp.where(laid == 0.0, 1.0, 0.0)
        eig[20:30, :] = eig[20:30, :] + empty
        eig[30:36, :] = jnp.ones((6, LANES), F32)
    for pick, zfwd, zback in ((pick_m, zfwd_m, zback_m), (pick_e, zfwd_e, zback_e)):
        for n, k in enumerate(ORDER):
            zfwd[n, 0:10, :] = pick[200 + 10 * k : 210 + 10 * k, :]
            zfwd[n, 10:16, :] = jnp.zeros((6, LANES), F32)
        for c in range(10):
            zback[c, 0:8, :] = pick[pl.ds(210 + c, 8, stride=10), :]
            zback[c, 8:16, :] = jnp.zeros((8, LANES), F32)
            zback[c, 8:9, :] = pick[200 + c : 201 + c, :]
            zback[c, 9:10, :] = pick[290 + c : 291 + c, :]
    low_half = iota((5, LANES), 1) < 64
    for i in range(10):
        half_e[5 * i : 5 * i + 5, :] = jnp.where(low_half, pick_e[10 * i : 10 * i + 5, :], pick_e[10 * i + 5 : 10 * i + 10, :])
    half_e[50:55, :] = jnp.where((iota((5, LANES), 1) & 32) == 0, half_e[45:50, :], half_e[0:5, :])
    lxe[0:5, :] = jnp.where(low_half, eig_e[0:5, :], eig_e[5:10, :])

    turn_a = (lane & ~7) | ((lane - sub) & 7)
    turn_b = (lane - sub) & 7
    turn_c = ((lane & 15) << 3) | ((sub + (lane >> 4)) & 7)

    def place(tile):
        main = shuffled(tile, turn_a, turn_b, turn_c)
        before = jnp.where(kz == 0, 0.0, pltpu.roll(main, 1, 1))
        after = jnp.where(kz == 15, 0.0, pltpu.roll(main, 127, 1))
        tail = pltpu.roll(jnp.where(sub == 7, before, after), 1, 0)
        return main, jnp.where(sub < 2, tail, 0.0)

    def fill(rows, win, count):
        def step(j, _):
            for i in range(count):
                tile = rows[pl.ds(pl.multiple_of((j * count + i) * 8, 8), 8), :]
                main, tail = place(tile)
                dest = jnp.where(j == 8, 10, j + 1)
                win[i + 1, dest, 0:8, :] = main
                win[i + 1, dest, 8:16, :] = tail
            return 0
        lax.fori_loop(0, 9, step, 0)

    fill(rows_m, win_m, 8)
    fill(rows_e, win_e, 9)

    def x_halo(j, _):
        ahead = win_m[8, j]
        back = win_m[1, j]
        extra = win_e[9, j]
        win_m[0, j] = jnp.where(wide >= 32, pltpu.roll(ahead, 32, 1), win_e[8, j])
        win_m[9, j] = jnp.where(wide < 96, pltpu.roll(back, 96, 1), win_e[1, j])
        ahead = jnp.where(wide >= 64, ahead, pltpu.roll(ahead, 64, 1))
        back = jnp.where(wide < 64, back, pltpu.roll(back, 64, 1))
        second = (wide & 32) != 0
        win_e[0, j] = jnp.where(second, ahead, extra)
        win_e[9, j] = jnp.where(second, extra, back)
        return 0

    lax.fori_loop(1, 11, x_halo, 0)

    def y_halo(i, _):
        for win in (win_m, win_e):
            outer = win[i, 10]
            upper = (wide & 16) != 0
            win[i, 0] = jnp.where(upper, pltpu.roll(win[i, 8], 16, 1), outer)
            win[i, 9] = jnp.where(upper, outer, pltpu.roll(win[i, 1], 112, 1))
        return 0

    lax.fori_loop(0, 10, y_halo, 0)

    def row(ref, n):
        return jnp.broadcast_to(ref[pl.ds(n, 1), :], (16, LANES))

    def dot_rows(pairs):
        total = None
        for a, b in pairs:
            total = a * b if total is None else total + a * b
        return total

    def x_forward(win, table, count):
        def step(j, _):
            column = [win[i, j] for i in range(10)]
            for a in range(count):
                work[a, j] = dot_rows([(row(table, count * i + a), column[i]) for i in range(10)])
            return 0
        lax.fori_loop(0, 10, step, 0)

    def through_z(source, target, zfwd):
        table = [zfwd[k] for k in range(10)]
        for b in range(10):
            target[b] = dot_rows([(table[k], jnp.broadcast_to(source[b, k : k + 1, :], (16, LANES))) for k in range(10)])

    def y_forward(a, pick):
        column = [work[a, j] for j in range(10)]
        for b in range(10):
            tmp_a[b] = dot_rows([(row(pick, 100 + 10 * j + b), column[j]) for j in range(10)])

    def scale(a, eig, lx):
        level = row(lx, a) + eig[20:36, :]
        for b in range(10):
            tmp_b[b] = tmp_b[b] / (level + row(eig, 10 + b))

    def y_back(source, pick, store):
        column = [source[b] for b in range(10)]
        for j in range(10):
            store(j, dot_rows([(row(pick, 100 + 10 * j + b), column[b]) for b in range(10)]))

    x_forward(win_e, half_e, 5)
    for b in range(10):
        edge[b] = jnp.zeros((16, LANES), F32)

    def edge_step(a, _):
        y_forward(a, pick_e)
        through_z(tmp_a, tmp_b, zfwd_e)
        scale(a, eig_e, lxe)
        weight = row(half_e, 50 + a)
        for b in range(10):
            edge[b] = edge[b] + weight * tmp_b[b]
        return 0

    lax.fori_loop(0, 5, edge_step, 0)
    for b in range(10):
        tmp_b[b] = edge[b] + pltpu.roll(edge[b], 64, 1)
    through_z(tmp_b, tmp_c, zback_e)

    def put_edge(j, value):
        edge[j] = value

    y_back(tmp_c, pick_e, put_edge)

    x_forward(win_m, pick_m, 10)

    def main_step(a, _):
        y_forward(a, pick_m)
        through_z(tmp_a, tmp_b, zfwd_m)
        scale(a, eig_m, eig_m)
        through_z(tmp_b, tmp_c, zback_m)

        def put(j, value):
            work[a, j] = value

        y_back(tmp_c, pick_m, put)
        return 0

    lax.fori_loop(0, 10, main_step, 0)

    def x_back(j, _):
        column = [work[a, j] for a in range(10)]
        first = dot_rows([(row(pick_m, a), column[a]) for a in range(10)])
        last = dot_rows([(row(pick_m, 90 + a), column[a]) for a in range(10)])
        side = edge[j]
        for i in range(1, 9):
            total = dot_rows([(row(pick_m, 10 * i + a), column[a]) for a in range(10)])
            if i == 1:
                total = total + jnp.where(wide >= 32, pltpu.roll(last, 32, 1), side)
            if i == 8:
                total = total + jnp.where(wide < 96, pltpu.roll(first, 96, 1), side)
            main = total[0:8]
            tail = pltpu.roll(total[8:16], 7, 0)
            main = main + jnp.where(
                sub == 7,
                jnp.where(kz == 15, 0.0, pltpu.roll(tail, 127, 1)),
                jnp.where((sub == 0) & (kz != 0), pltpu.roll(tail, 1, 1), 0.0),
            )
            win_m[i, j, 0:8, :] = main
        return 0

    lax.fori_loop(0, 10, x_back, 0)

    back_a = (((lane - sub) & 7) << 4) | (lane >> 3)
    back_c = (lane & ~7) | ((lane + sub) & 7)
    upper = (lane & 16) != 0

    def unplace(i, _):
        first = win_m[i + 1, 0, 0:8, :]
        last = win_m[i + 1, 9, 0:8, :]
        for j in range(8):
            tile = win_m[i + 1, j + 1, 0:8, :]
            if j == 0:
                tile = tile + jnp.where(upper, pltpu.roll(last, 16, 1), 0.0)
            if j == 7:
                tile = tile + jnp.where(upper, 0.0, pltpu.roll(first, 112, 1))
            out_rows[pl.ds(pl.multiple_of((i * 8 + j) * 8, 8), 8), :] = shuffled(tile, back_a, turn_b, back_c)
        tile = jnp.where(upper, last, first)
        rim_rows[pl.ds(pl.multiple_of(i * 8, 8), 8), :] = shuffled(tile, back_a, turn_b, back_c)
        return 0

    lax.fori_loop(0, 8, unplace, 0)

    for ix in range(4):
        for jy in range(2):
            r = 2 * ix + jy
            for i in range(8):
                fine_ref[pl.ds(128 * ix + 16 * i + 8 * jy, 8), :] = out_rows[pl.ds(64 * i + r, 8, stride=8), :]
            rim_ref[pl.ds(32 * jy + 8 * ix, 8), :] = rim_rows[pl.ds(r, 8, stride=8), :]


def tree_kernel(got_ref, rim_ref, pay_ref):
    p = lax.axis_index("gx")
    q = lax.axis_index("gy")
    bits = q + 1
    total = jnp.zeros((1, 384), F32)
    for t in range(64):
        inside = (t >> bits) == (p >> bits)
        total = total + jnp.where(inside, got_ref[t], 0.0)
    for peer in range(8):
        pay_ref[peer, 0:32, :] = jnp.where(peer < q, rim_ref[0:32, :], rim_ref[32:64, :])
        for n in range(3):
            pay_ref[peer, 32 + n : 33 + n, :] = total[:, LANES * n : LANES * (n + 1)]
        pay_ref[peer, 35:40, :] = jnp.zeros((5, LANES), F32)


def up_kernel(first_ref, own_ref, got_ref, pan_ref, num_ref, fine_ref, out_ref, line_ref, value_ref, vertex_ref):
    q = lax.axis_index("gy")
    line_ref[...] = jnp.zeros((32, LANES), F32)
    line_ref[0:2, :] = own_ref[0:2, :]
    for level in range(1, 4):
        total = jnp.zeros((1, LANES), F32)
        for peer in range(8):
            inside = (peer >> level) == (q >> level)
            total = total + jnp.where(inside, first_ref[peer, 31 + level : 32 + level, :], 0.0)
        line_ref[1 + level : 2 + level, :] = total
    for peer in range(6):
        line_ref[5 + 3 * peer : 8 + 3 * peer, :] = got_ref[peer, 32:35, :]
    here = pltpu.roll(line_ref[0:24], 127, 1)
    after = pltpu.roll(line_ref[1:25], 127, 1)
    coeff = jnp.where(iota((24, LANES), 1) == 127, after, here)
    for low in range(0, 255, 64):
        high = min(low + 64, 255)
        total = pan_ref[low:high, 0:LANES] * coeff[0:1]
        for c in range(1, 22):
            total = total + pan_ref[low:high, c * LANES : (c + 1) * LANES] * coeff[c : c + 1]
        value = jnp.sum(total, axis=1, keepdims=True)
        value = value + jnp.sum(pan_ref[low:high, 2816:2943] * coeff[22:23, 0:127], axis=1, keepdims=True)
        value_ref[low:high, :] = jnp.broadcast_to(value, (high - low, LANES))
    value_ref[255:256, :] = jnp.zeros((1, LANES), F32)
    vertex_ref[...] = jnp.zeros((16, LANES), F32)
    rows = iota((256, 17), 0)
    values = value_ref[:, 0:17]
    for i in range(5):
        for j in range(3):
            k = 3 * i + j
            vertex_ref[k : k + 1, 0:17] = jnp.sum(jnp.where(num_ref[i, j : j + 1, :] == rows, values, 0.0), axis=0, keepdims=True)
    depth = hat(iota((LANES, LANES), 1), iota((LANES, LANES), 0))
    plane = plane_hat(iota((512, 16), 0), iota((512, 16), 1))
    half = jnp.dot(vertex_ref[...], depth, precision=exact)
    out_ref[...] = fine_ref[...] + jnp.dot(plane, half, precision=exact)
    low_face = jnp.where(q > 0, got_ref[jnp.maximum(q - 1, 0), 0:32, :], 0.0)
    high_face = jnp.where(q < 7, got_ref[jnp.minimum(q + 1, 7), 0:32, :], 0.0)
    out_ref[pl.ds(0, 32, stride=16), :] = out_ref[pl.ds(0, 32, stride=16), :] + low_face
    out_ref[pl.ds(15, 32, stride=16), :] = out_ref[pl.ds(15, 32, stride=16), :] + high_face


def call(kernel, outs, scratch=(), flops=0, bytes_accessed=0, limit=40):
    shapes = [jax.ShapeDtypeStruct(s, F32) for s in outs]
    return pl.pallas_call(
        kernel,
        out_shape=shapes,
        scratch_shapes=[pltpu.VMEM(s, F32) for s in scratch],
        compiler_params=pltpu.CompilerParams(vmem_limit_bytes=limit << 20),
        cost_estimate=pl.CostEstimate(flops=flops, bytes_accessed=bytes_accessed, transcendentals=0),
    )


def spread_to(block, axis):
    return lax.all_to_all(block, axis, 0, 0, tiled=True)


FINE_SCRATCH = (
    (576, 128), (648, 128), (10, 11, 16, 128), (10, 11, 16, 128),
    (304, 128), (304, 128), (40, 128), (40, 128),
    (10, 16, 128), (10, 16, 128), (10, 16, 128), (10, 16, 128),
    (56, 128), (8, 128), (10, 10, 16, 128),
    (10, 16, 128), (10, 16, 128), (10, 16, 128), (10, 16, 128),
    (512, 128), (64, 128),
)


def shards(residual, elem_class, basis, eigenvalues, vertex_number, panels):
    field = residual.reshape(512, LANES)
    table = basis.reshape(NCLASS, 3 * NEXT * NEXT)
    values = eigenvalues.reshape(NCLASS, 3 * NEXT)
    pay, own = call(down_kernel, [(8, 40, 128), (24, 128)], [(40, 128)])(field, vertex_number, panels)
    first = spread_to(pay, "gy")
    right, left, tree, face = call(
        share_kernel, [(168, 128), (168, 128), (64, 1, 384), (64, 128)]
    )(first, field, elem_class)
    from_left = lax.ppermute(right, "gx", [(i, i + 1) for i in range(63)])
    from_right = lax.ppermute(left, "gx", [(i + 1, i) for i in range(63)])
    summed = spread_to(tree, "gx")
    fine, rim = call(fine_kernel, [(512, 128), (64, 128)], FINE_SCRATCH, flops=8_000_000_000, bytes_accessed=20_000_000)(
        field, face, from_left, from_right, elem_class, table, values
    )
    (pay,) = call(tree_kernel, [(8, 40, 128)])(summed, rim)
    second = spread_to(pay, "gy")
    (out,) = call(up_kernel, [(512, 128)], [(32, 128), (256, 128), (16, 128)])(
        first, own, second, panels, vertex_number, fine
    )
    return out.reshape(residual.shape)


def solution(mesh):
    return jax.shard_map(
        shards,
        mesh=mesh,
        in_specs=(
            P(None, "gx", "gy", None),
            P("gx", "gy", None),
            P(),
            P(),
            P("gx", "gy", None),
            P("gx", "gy"),
        ),
        out_specs=P(None, "gx", "gy", None),
        check_vma=False,
    )
```

profile of v0, /device:TPU:1, one launch (start us, length us, event | category | flops | bytes accessed | tf_op | source)
XLA Modules:
  0.0 78.2 jit_solution(811617895636515934)
XLA Ops:
  0.0 0.0 copy-start
  0.0 1.9 %copy-done = f32[255,2943]{1,0:T(8,128)S(1)} copy-done((f32[255,2943]{1,0:T(8,128)S(1)}, f32[255,2943]{1,0:T(8,128)}, u32[]{:S(2)}) %copy-start) | copy-done | bytes 3001884
  1.9 0.0 copy-start.2
  1.9 0.9 %copy-done.2 = f32[1,32,16,128]{3,2,1,0:T(8,128)S(1)} copy-done((f32[1,32,16,128]{3,2,1,0:T(8,128)S(1)}, f32[1,32,16,128]{3,2,1,0:T(8,128)}, u32[]{:S(2)}) %copy-start.2) | copy-done | bytes 262168
  2.8 0.0 copy-start.6
  2.8 0.7 copy-done.6
  3.5 0.0 copy-start.13
  3.5 0.0 copy-start.22
  3.5 0.0 copy-start.21
  3.5 0.0 copy-start.3
  3.5 1.1 %shard_map.64 = (f32[8,40,128]{2,1,0:T(8,128)S(1)}, f32[24,128]{1,0:T(8,128)S(1)}) custom-call(f32[512,128]{1,0:T(8,128)S(1)} %bitcast.2, s32[5,3,17]{2,1,0:T(4,128)S(1)} %copy-done.6, f32[255,2943]{1,0:T(8,128)S(1)} %copy-done), custom_call_target="tpu_custom_call" | custom-call | tf_op jit(solution)/shard_map/pallas_call | solution.py:412
  4.6 0.0 copy-start.11
  4.6 14.8 %all_to_all.15.got_ref.first_ref = f32[8,40,128]{2,1,0:T(8,128)S(1)} all-to-all(f32[8,40,128]{2,1,0:T(8,128)S(1)} %get-tuple-element.13), channel_id=1, replica_groups=mesh['gx'=64,'gy'=8] {'gy'}, dimensions={0} | all-to-all | bytes 327680 | tf_op jit(solution)/shard_map/all_to_all | solution.py:395
  19.5 0.0 copy-done.13
  19.5 0.7 shard_map.65
  20.1 0.0 copy-done.11
  20.2 0.6 copy-done.19
  20.8 1.3 %collective-permute-start = (f32[168,128]{1,0:T(8,128)S(1)}, f32[168,128]{1,0:T(8,128)S(1)}, u32[]{:S(2)}, u32[]{:S(2)}) collective-permute-start(f32[168,128]{1,0:T(8,128)S(1)} %get-tuple-element.17), channel_id=1, source_target_pairs={{0,8},{8,16},{16,24},{24,32},{32,40},{40,48},{48,56},{56,64},{64,7... | collective-permute-start | bytes 258056 | tf_op jit(solution)/shard_map/ppermute | solution.py:417
  22.0 1.3 %collective-permute-start.1 = (f32[168,128]{1,0:T(8,128)S(1)}, f32[168,128]{1,0:T(8,128)S(1)}, u32[]{:S(2)}, u32[]{:S(2)}) collective-permute-start(f32[168,128]{1,0:T(8,128)S(1)} %get-tuple-element.18), channel_id=1, source_target_pairs={{8,0},{16,8},{24,16},{32,24},{40,32},{48,40},{56,48},{64,56},{72,6... | collective-permute-start | bytes 258056 | tf_op jit(solution)/shard_map/ppermute | solution.py:418
  23.3 0.0 copy-done.22
  23.4 0.7 reshape.14.value_ref
  24.0 0.0 copy-done.21
  24.1 0.7 reshape.13.basis_ref
  24.8 18.7 %all-to-all-start.1 = ((f32[64,1,384]{2,1,0:T(1,128)}), f32[64,1,384]{2,1,0:T(1,128)S(1)}, u32[]{:S(2)}, u32[]{:S(2)}) async-start(f32[64,1,384]{2,1,0:T(1,128)} %get-tuple-element.15), calls=%async_computation.1 | async-start | bytes 196608 | tf_op jit(solution)/shard_map/all_to_all | solution.py:395
  43.5 0.0 collective-permute-done.from_left
  43.5 0.0 copy-start.15
  43.5 0.6 copy-done.15
  44.1 0.0 collective-permute-done.1.from_right
  44.1 0.6 copy-done.17
  44.8 0.0 copy-done.3
  44.8 0.7 copy-done.10
  45.5 0.7 copy-done.14
  46.1 0.9 %copy-done.16 = f32[168,128]{1,0:T(8,128)S(1)} copy-done((f32[168,128]{1,0:T(8,128)S(1)}, f32[168,128]{1,0:T(8,128)}, u32[]{:S(2)}) %copy-start.16) | copy-done | bytes 86040
  47.0 0.9 %copy-done.18 = f32[168,128]{1,0:T(8,128)S(1)} copy-done((f32[168,128]{1,0:T(8,128)S(1)}, f32[168,128]{1,0:T(8,128)}, u32[]{:S(2)}) %copy-start.18) | copy-done | bytes 86040
  47.9 0.8 copy-done.20
  48.7 13.9 %shard_map.66 = (f32[512,128]{1,0:T(8,128)S(1)}, f32[64,128]{1,0:T(8,128)S(1)}) custom-call(f32[512,128]{1,0:T(8,128)S(1)} %bitcast.4, f32[64,128]{1,0:T(8,128)S(1)} %copy-done.20, f32[168,128]{1,0:T(8,128)S(1)} %copy-done.16, f32[168,128]{1,0:T(8,128)S(1)} %copy-done.18, s32[4,2,16]{2,1,0:T(2,128)S(1)} %copy-done.13, f32[8,300]{1,0:T(8,128)S(1)} %copy-done.10, ...), custom_call_target="tpu_custom_call" | custom-call | flops 8000000000 | bytes 20000000 | tf_op jit(solution)/shard_map/pallas_call | solution.py:420
  62.6 0.0 copy-start.4
  62.6 0.7 copy-done.4
  63.3 0.6 copy-done.8
  63.9 0.0 all-to-all-done.1.got_ref
  63.9 0.8 copy-done.9
  64.6 0.1 shard_map.67
  64.7 9.7 %all_to_all.16.got_ref = f32[8,40,128]{2,1,0:T(8,128)S(1)} all-to-all(f32[8,40,128]{2,1,0:T(8,128)S(1)} %shard_map.67), channel_id=1, replica_groups=mesh['gx'=64,'gy'=8] {'gy'}, dimensions={0} | all-to-all | bytes 327680 | tf_op jit(solution)/shard_map/all_to_all | solution.py:395
  74.5 0.0 copy-done.1
  74.5 0.0 copy-done.7
  74.5 0.9 %copy-done.5 = f32[512,128]{1,0:T(8,128)S(1)} copy-done((f32[512,128]{1,0:T(8,128)S(1)}, f32[512,128]{1,0:T(8,128)}, u32[]{:S(2)}) %copy-start.5) | copy-done | bytes 262168
  75.4 0.7 copy-done.12
  76.1 2.1 %shard_map.68 = f32[512,128]{1,0:T(8,128)} custom-call(f32[8,40,128]{2,1,0:T(8,128)S(1)} %all_to_all.15.got_ref.first_ref, f32[24,128]{1,0:T(8,128)S(1)} %copy-done.12, f32[8,40,128]{2,1,0:T(8,128)S(1)} %all_to_all.16.got_ref, f32[255,2943]{1,0:T(8,128)S(1)} %copy-done.1, s32[5,3,17]{2,1,0:T(4,128)S(1)} %copy-done.7, f32[512,128]{1,0:T(8,128)S(1)} %copy-done.5), custom_call_target="tpu_custom_call" | custom-call | tf_op jit(solution)/shard_map/pallas_call | solution.py:425
  (15 shorter events, 0.1 us)
Async XLA Ops:
  0.0 1.9 %copy-start = (f32[255,2943]{1,0:T(8,128)S(1)}, f32[255,2943]{1,0:T(8,128)}, u32[]{:S(2)}) copy-start(f32[255,2943]{1,0:T(8,128)} %pan_ref.3) | copy-start | bytes 9005584
  1.9 0.9 %copy-start.2 = (f32[1,32,16,128]{3,2,1,0:T(8,128)S(1)}, f32[1,32,16,128]{3,2,1,0:T(8,128)}, u32[]{:S(2)}) copy-start(f32[1,32,16,128]{3,2,1,0:T(8,128)} %param.6) | copy-start | bytes 786436
  2.8 0.7 copy-start.6
  3.5 16.0 %copy-start.13 = (s32[4,2,16]{2,1,0:T(2,128)S(1)}, s32[4,2,16]{2,1,0:T(2,128)}, u32[]{:S(2)}) copy-start(s32[4,2,16]{2,1,0:T(2,128)} %cls_ref.3) | copy-start | bytes 1540
  3.5 19.8 %copy-start.22 = (f32[8,3,10]{2,0,1:T(8,128)S(1)}, f32[8,3,10]{2,0,1:T(8,128)}, u32[]{:S(2)}) copy-start(f32[8,3,10]{2,0,1:T(8,128)} %param.9) | copy-start | bytes 2884
  3.5 20.5 %copy-start.21 = (f32[8,3,10,10]{3,0,2,1:T(8,128)S(1)}, f32[8,3,10,10]{3,0,2,1:T(8,128)}, u32[]{:S(2)}) copy-start(f32[8,3,10,10]{3,0,2,1:T(8,128)} %param.8) | copy-start | bytes 28804
  3.5 41.2 %copy-start.3 = (f32[1,32,16,128]{3,2,1,0:T(8,128)S(1)}, f32[1,32,16,128]{3,2,1,0:T(8,128)}, u32[]{:S(2)}) copy-start(f32[1,32,16,128]{3,2,1,0:T(8,128)} %param.6) | copy-start | bytes 786436
  4.6 15.5 %copy-start.11 = (f32[24,128]{1,0:T(8,128)}, f32[24,128]{1,0:T(8,128)S(1)}, u32[]{:S(2)}) copy-start(f32[24,128]{1,0:T(8,128)S(1)} %get-tuple-element.14.own_ref) | copy-start | bytes 36868
  20.1 0.6 copy-start.19
  20.8 22.7 %collective-permute-start = (f32[168,128]{1,0:T(8,128)S(1)}, f32[168,128]{1,0:T(8,128)S(1)}, u32[]{:S(2)}, u32[]{:S(2)}) collective-permute-start(f32[168,128]{1,0:T(8,128)S(1)} %get-tuple-element.17), channel_id=1, source_target_pairs={{0,8},{8,16},{16,24},{24,32},{32,40},{40,48},{48,56},{56,64},{64,7... | collective-permute-start | bytes 258056 | tf_op jit(solution)/shard_map/ppermute | solution.py:417
  22.0 22.1 %collective-permute-start.1 = (f32[168,128]{1,0:T(8,128)S(1)}, f32[168,128]{1,0:T(8,128)S(1)}, u32[]{:S(2)}, u32[]{:S(2)}) collective-permute-start(f32[168,128]{1,0:T(8,128)S(1)} %get-tuple-element.18), channel_id=1, source_target_pairs={{8,0},{16,8},{24,16},{32,24},{40,32},{48,40},{56,48},{64,56},{72,6... | collective-permute-start | bytes 258056 | tf_op jit(solution)/shard_map/ppermute | solution.py:418
  24.8 39.1 %all-to-all-start.1 = ((f32[64,1,384]{2,1,0:T(1,128)}), f32[64,1,384]{2,1,0:T(1,128)S(1)}, u32[]{:S(2)}, u32[]{:S(2)}) async-start(f32[64,1,384]{2,1,0:T(1,128)} %get-tuple-element.15), calls=%async_computation.1 | async-start | bytes 196608 | tf_op jit(solution)/shard_map/all_to_all | solution.py:395
  43.5 0.6 copy-start.15
  44.1 0.6 copy-start.17
  44.8 0.7 copy-start.10
  45.5 0.7 copy-start.14
  46.1 0.9 %copy-start.16 = (f32[168,128]{1,0:T(8,128)S(1)}, f32[168,128]{1,0:T(8,128)}, u32[]{:S(2)}) copy-start(f32[168,128]{1,0:T(8,128)} %copy-done.15) | copy-start | bytes 258052
  47.0 0.9 %copy-start.18 = (f32[168,128]{1,0:T(8,128)S(1)}, f32[168,128]{1,0:T(8,128)}, u32[]{:S(2)}) copy-start(f32[168,128]{1,0:T(8,128)} %copy-done.17) | copy-start | bytes 258052
  47.9 0.8 copy-start.20
  48.7 25.8 %copy-start.1 = (f32[255,2943]{1,0:T(8,128)S(1)}, f32[255,2943]{1,0:T(8,128)}, u32[]{:S(2)}) copy-start(f32[255,2943]{1,0:T(8,128)} %pan_ref.3) | copy-start | bytes 9005584
  48.7 25.8 %copy-start.7 = (s32[5,3,17]{2,1,0:T(4,128)S(1)}, s32[5,3,17]{2,1,0:T(4,128)}, u32[]{:S(2)}) copy-start(s32[5,3,17]{2,1,0:T(4,128)} %num_ref.3) | copy-start | bytes 3064
  62.6 0.7 copy-start.4
  63.3 0.6 copy-start.8
  63.9 0.8 copy-start.9
  74.5 1.0 %copy-start.5 = (f32[512,128]{1,0:T(8,128)S(1)}, f32[512,128]{1,0:T(8,128)}, u32[]{:S(2)}) copy-start(f32[512,128]{1,0:T(8,128)} %copy-done.4) | copy-start | bytes 786436
  75.4 0.7 copy-start.12
where the time goes:
time: 78.9 us; the launch traced here: 78.2 us
  blocking collectives  24.6 us (31%)
  starting transfers between devices  21.3 us (27%)
  Pallas kernels  17.8 us (23%)
  local copies, waits for them, and re-layouts  14.4 us (18%)
    all_to_all x2, blocking collectives, spread_to(): return lax.all_to_all(block, axis, 0, 0, tiled=True)  24.6 us
    all_to_all x1, starting transfers between devices, spread_to(): return lax.all_to_all(block, axis, 0, 0, tiled=True)  18.7 us
    pallas_call x1, Pallas kernels, shards(): call(fine_kernel, [(512, 128), (64, 128)], FINE_SCRATCH, flops=8000000000...  13.9 us
    unnamed x48, local copies, waits for them, and re-layouts  13.1 us
    pallas_call x1, Pallas kernels, shards(): call(up_kernel, [(512, 128)], [(32, 128), (256, 128), (16, 128)])  2.07 us
  transfers between devices with their start and end apart: 3, of which 0 were waited for; matrix products, arithmetic and copies ran while one was open for 2% of the time, Pallas kernels for 18%

commit v1 on v0

v1 whole, which is shorter than its diff:
```python
import functools

import jax
import jax.numpy as jnp
from jax import lax
from jax.experimental import pallas as pl
from jax.experimental.pallas import tpu as pltpu
from jax.sharding import PartitionSpec as P

NPR = 8
NEXT = 10
NCLASS = 8
LANES = 128
HALO = NPR + 1
F32 = jnp.float32
exact = lax.Precision.HIGHEST
ORDER = (1, 2, 3, 4, 5, 6, 7, 8, 0, 9)


def iota(shape, axis):
    return lax.broadcasted_iota(jnp.int32, shape, axis)


def hat(point, vertex):
    place = (point.astype(F32) + 0.5) / NPR
    return jnp.maximum(0.0, 1.0 - jnp.abs(place - vertex.astype(F32)))


def plane_hat(point, vertex):
    third = (vertex.astype(F32) + 0.5) / 3.0
    big = third.astype(jnp.int32)
    return hat(point >> 4, big) * hat(point & 15, vertex - 3 * big)


def down_kernel(
    res_hbm, num_hbm, pan_hbm, cls_hbm, basis_hbm, value_hbm,
    pay_ref, own_ref, res_ref, num_ref, cls_ref, basis_ref, value_ref,
    line_ref, pan_ref, sems,
):
    q = lax.axis_index("gy")
    pairs = (
        (res_hbm, res_ref), (num_hbm, num_ref), (pan_hbm, pan_ref),
        (cls_hbm, cls_ref), (basis_hbm, basis_ref), (value_hbm, value_ref),
    )
    copies = [pltpu.make_async_copy(source, target, sems.at[n]) for n, (source, target) in enumerate(pairs)]
    for copy in copies:
        copy.start()
    plane = plane_hat(iota((16, 512), 1), iota((16, 512), 0))
    depth = hat(iota((128, 17), 0), iota((128, 17), 1))
    line_ref[...] = jnp.zeros((40, LANES), F32)
    copies[0].wait()
    half = jnp.dot(plane, res_ref[...], precision=exact)
    vertex = jnp.dot(half, depth, precision=exact)
    low_face = res_ref[pl.ds(0, 32, stride=16), :]
    high_face = res_ref[pl.ds(15, 32, stride=16), :]
    for peer in range(8):
        pay_ref[peer, 0:32, :] = jnp.where(peer < q, low_face, high_face)
    copies[1].wait()
    rows = iota((256, 17), 0)
    spread = jnp.zeros((256, 17), F32)
    for i in range(5):
        for j in range(3):
            k = 3 * i + j
            spread = spread + jnp.where(num_ref[i, j : j + 1, :] == rows, vertex[k : k + 1, :], 0.0)
    ordered = jnp.broadcast_to(jnp.sum(spread, axis=1, keepdims=True), (256, LANES))
    for copy in copies[2:]:
        copy.wait()
    for c in range(23):
        low = c * LANES
        width = min(LANES, 2943 - low)
        piece = jnp.sum(pan_ref[:, low : low + width] * ordered[:255, :width], axis=0, keepdims=True)
        line_ref[8 + c : 9 + c, :width] = piece
    here = pltpu.roll(line_ref[8:32], 1, 1)
    before = pltpu.roll(line_ref[7:31], 1, 1)
    own_ref[...] = jnp.where(iota((24, LANES), 1) == 0, before, here)
    for peer in range(8):
        pay_ref[peer, 32:35, :] = own_ref[2:5, :]
        if peer < 6:
            pay_ref[peer, 35:38, :] = own_ref[5 + 3 * peer : 8 + 3 * peer, :]
            pay_ref[peer, 38:40, :] = jnp.zeros((2, LANES), F32)
        else:
            pay_ref[peer, 35:40, :] = jnp.zeros((5, LANES), F32)


def share_kernel(got_ref, res_ref, cls_ref, right_ref, left_ref, tree_ref, face_ref):
    q = lax.axis_index("gy")
    face_ref[0:32, :] = jnp.where(q > 0, got_ref[jnp.maximum(q - 1, 0), 0:32, :], 0.0)
    face_ref[32:64, :] = jnp.where(q < 7, got_ref[jnp.minimum(q + 1, 7), 0:32, :], 0.0)
    for ref, column, first in ((right_ref, 3, 23), (left_ref, 0, 0)):
        ref[0:144, :] = res_ref[16 * first : 16 * first + 144, :]
        ref[144:153, :] = face_ref[first : first + 9, :]
        ref[153:162, :] = face_ref[32 + first : 41 + first, :]
        ref[162:168, :] = jnp.zeros((6, LANES), F32)
        ref[162:164, 0:16] = (cls_ref[column] + 1).astype(F32)
    total = got_ref[0, 35:38, :]
    for peer in range(1, 8):
        total = total + got_ref[peer, 35:38, :]
    line = jnp.concatenate([total[0:1], total[1:2], total[2:3]], axis=1)
    for t in range(64):
        tree_ref[t] = line


def shuffled(tile, first, second, third):
    tile = jnp.take_along_axis(tile, first, axis=1, mode="promise_in_bounds")
    tile = jnp.take_along_axis(tile, second, axis=0, mode="promise_in_bounds")
    return jnp.take_along_axis(tile, third, axis=1, mode="promise_in_bounds")


def grids():
    sub = iota((8, LANES), 0)
    lane = iota((8, LANES), 1)
    return sub, lane, lane & 15


def place(tile, sub, lane, kz):
    turn_a = (lane & ~7) | ((lane - sub) & 7)
    turn_b = (lane - sub) & 7
    turn_c = ((lane & 15) << 3) | ((sub + (lane >> 4)) & 7)
    main = shuffled(tile, turn_a, turn_b, turn_c)
    before = jnp.where(kz == 0, 0.0, pltpu.roll(main, 1, 1))
    after = jnp.where(kz == 15, 0.0, pltpu.roll(main, 127, 1))
    tail = pltpu.roll(jnp.where(sub == 7, before, after), 1, 0)
    return main, jnp.where(sub < 2, tail, 0.0)


def unplace(tile, sub, lane):
    back_a = (((lane - sub) & 7) << 4) | (lane >> 3)
    back_c = (lane & ~7) | ((lane + sub) & 7)
    return shuffled(tile, back_a, (lane - sub) & 7, back_c)


def join_z(total, sub, kz):
    main = total[0:8]
    tail = pltpu.roll(total[8:16], 7, 0)
    return main + jnp.where(
        sub == 7,
        jnp.where(kz == 15, 0.0, pltpu.roll(tail, 127, 1)),
        jnp.where((sub == 0) & (kz != 0), pltpu.roll(tail, 1, 1), 0.0),
    )


def row(ref, n):
    return jnp.broadcast_to(ref[pl.ds(n, 1), :], (16, LANES))


def dot_rows(pairs):
    total = None
    for a, b in pairs:
        total = a * b if total is None else total + a * b
    return total


def pick_tables(kind, table_ref, eigen_ref, pick, eig, zfwd, zback):
    group = iota((8, LANES), 0)
    lane = iota((8, LANES), 1)
    spread = (iota((16, LANES), 0) == (iota((16, LANES), 1) & 15)).astype(F32)
    laid = jnp.dot(kind, spread, precision=exact)
    laid = jnp.sum(jnp.where(group == (lane >> 4), laid, 0.0), axis=0, keepdims=True)
    onehot = (laid == (group + 1).astype(F32)).astype(F32)
    dims = (((0,), (0,)), ((), ()))
    pick[0:300, :] = lax.dot_general(table_ref[:, 0:300], onehot, dims, precision=exact, preferred_element_type=F32)
    eig[0:30, :] = lax.dot_general(eigen_ref[:, 0:30], onehot, dims, precision=exact, preferred_element_type=F32)
    eig[20:30, :] = eig[20:30, :] + jnp.where(laid == 0.0, 1.0, 0.0)
    eig[30:40, :] = jnp.ones((10, LANES), F32)
    for n, k in enumerate(ORDER):
        zfwd[n, 0:10, :] = pick[200 + 10 * k : 210 + 10 * k, :]
        zfwd[n, 10:16, :] = jnp.zeros((6, LANES), F32)
    for c in range(10):
        zback[c, 0:8, :] = pick[pl.ds(210 + c, 8, stride=10), :]
        zback[c, 8:16, :] = jnp.zeros((8, LANES), F32)
        zback[c, 8:9, :] = pick[200 + c : 201 + c, :]
        zback[c, 9:10, :] = pick[290 + c : 291 + c, :]


def tile_kernel(
    res_ref, cls_ref, basis_ref, value_ref,
    win, table_ref, eigen_ref, pick, eig, zfwd, zback,
    rows_m,
):
    sub, lane, kz = grids()
    for d in range(3):
        eigen_ref[:, 10 * d : 10 * d + 10] = value_ref[d]
        for i in range(10):
            low = 100 * d + 10 * i
            table_ref[:, low : low + 10] = basis_ref[d, i]
    kind = jnp.concatenate([cls_ref[ix].astype(F32) + 1.0 for ix in range(4)], axis=0)
    pick_tables(kind, table_ref, eigen_ref, pick, eig, zfwd, zback)
    for ix in range(4):
        for jy in range(2):
            r = 2 * ix + jy
            for i in range(8):
                rows_m[pl.ds(i * 8 + r, 8, stride=64), :] = res_ref[pl.ds(128 * ix + 16 * i + 8 * jy, 8), :]

    def step(j, _):
        for i in range(8):
            main, tail = place(rows_m[pl.ds(pl.multiple_of((j * 8 + i) * 8, 8), 8), :], sub, lane, kz)
            win[i + 1, j + 1, 0:8, :] = main
            win[i + 1, j + 1, 8:16, :] = tail
        return 0

    lax.fori_loop(0, 8, step, 0)


def solve_kernel(
    win_in, table_ref, eigen_ref, pick_m, eig_m, zfwd_m, zback_m, face_ref, from_left, from_right,
    win_m, work, edge, ends, rim_ref,
    rows_e, rows_f, win_e, pick_e, eig_e, zfwd_e, zback_e, half_e, lxe, work_e, tmp_a, tmp_b, tmp_c, rim_rows,
):
    del win_in
    sub, lane, kz = grids()
    wide = iota((16, LANES), 1)
    upper = (wide & 16) != 0

    for ix in range(4):
        for jy in range(2):
            rows_f[pl.ds(2 * ix + jy, 8, stride=8), :] = face_ref[pl.ds(32 * jy + 8 * ix, 8), :]
    for side, ref in ((0, from_left), (1, from_right)):
        for layer in range(9):
            i = (layer + 8) % 9 if side == 0 else layer
            for jy in range(2):
                part = ref[pl.ds(16 * layer + 8 * jy, 8), :]
                outer = ref[pl.ds(144 + 9 * jy + layer, 1), :]
                for r in (2 * side + jy, 4 + 2 * side + jy):
                    rows_e[pl.ds(i * 8 + r, 8, stride=72), :] = part
                    rows_e[pl.ds((72 + i) * 8 + r, 1), :] = outer
    near = [from_left[162:164, 0:16], from_right[162:164, 0:16]]
    pick_tables(jnp.concatenate(near + near, axis=0), table_ref, eigen_ref, pick_e, eig_e, zfwd_e, zback_e)
    low_half = iota((5, LANES), 1) < 64
    for i in range(10):
        half_e[5 * i : 5 * i + 5, :] = jnp.where(low_half, pick_e[10 * i : 10 * i + 5, :], pick_e[10 * i + 5 : 10 * i + 10, :])
    half_e[50:55, :] = jnp.where((iota((5, LANES), 1) & 32) == 0, half_e[45:50, :], half_e[0:5, :])
    lxe[0:5, :] = jnp.where(low_half, eig_e[0:5, :], eig_e[5:10, :])

    for i in range(8):
        main, tail = place(rows_f[8 * i : 8 * i + 8, :], sub, lane, kz)
        win_m[i + 1, 10, 0:8, :] = main
        win_m[i + 1, 10, 8:16, :] = tail

    def fill(j, _):
        for i in range(9):
            main, tail = place(rows_e[pl.ds(pl.multiple_of((j * 9 + i) * 8, 8), 8), :], sub, lane, kz)
            dest = jnp.where(j == 8, 10, j + 1)
            win_e[i + 1, dest, 0:8, :] = main
            win_e[i + 1, dest, 8:16, :] = tail
        return 0

    lax.fori_loop(0, 9, fill, 0)

    def x_halo(j):
        ahead = win_m[8, j]
        back = win_m[1, j]
        extra = win_e[9, j]
        win_m[0, j] = jnp.where(wide >= 32, pltpu.roll(ahead, 32, 1), win_e[8, j])
        win_m[9, j] = jnp.where(wide < 96, pltpu.roll(back, 96, 1), win_e[1, j])
        ahead = jnp.where(wide >= 64, ahead, pltpu.roll(ahead, 64, 1))
        back = jnp.where(wide < 64, back, pltpu.roll(back, 64, 1))
        second = (wide & 32) != 0
        win_e[0, j] = jnp.where(second, ahead, extra)
        win_e[9, j] = jnp.where(second, extra, back)

    for j in (1, 2, 3, 4, 5, 6, 7, 8, 10):
        x_halo(j)

    def y_halo(i, _):
        for win in (win_m, win_e):
            outer = win[i, 10]
            win[i, 0] = jnp.where(upper, pltpu.roll(win[i, 8], 16, 1), outer)
            win[i, 9] = jnp.where(upper, outer, pltpu.roll(win[i, 1], 112, 1))
        return 0

    lax.fori_loop(0, 10, y_halo, 0)

    def x_forward(win, table, target, count):
        def step(j, _):
            column = [win[i, j] for i in range(10)]
            for a in range(count):
                target[a, j] = dot_rows([(row(table, count * i + a), column[i]) for i in range(10)])
            return 0
        lax.fori_loop(0, 10, step, 0)

    def through_z(source, target, zfwd):
        table = [zfwd[k] for k in range(10)]
        for b in range(10):
            target[b] = dot_rows([(table[k], jnp.broadcast_to(source[b, k : k + 1, :], (16, LANES))) for k in range(10)])

    def y_forward(a, source, pick):
        column = [source[a, j] for j in range(10)]
        for b in range(10):
            tmp_a[b] = dot_rows([(row(pick, 100 + 10 * j + b), column[j]) for j in range(10)])

    def scale(a, eig, lx):
        level = row(lx, a) + eig[20:36, :]
        for b in range(10):
            tmp_b[b] = tmp_b[b] / (level + row(eig, 10 + b))

    def y_back(source, pick, store):
        column = [source[b] for b in range(10)]
        for j in range(10):
            store(j, dot_rows([(row(pick, 100 + 10 * j + b), column[b]) for b in range(10)]))

    x_forward(win_e, half_e, work_e, 5)
    for b in range(10):
        edge[b] = jnp.zeros((16, LANES), F32)

    def edge_step(a, _):
        y_forward(a, work_e, pick_e)
        through_z(tmp_a, tmp_b, zfwd_e)
        scale(a, eig_e, lxe)
        weight = row(half_e, 50 + a)
        for b in range(10):
            edge[b] = edge[b] + weight * tmp_b[b]
        return 0

    lax.fori_loop(0, 5, edge_step, 0)
    for b in range(10):
        tmp_b[b] = edge[b] + pltpu.roll(edge[b], 64, 1)
    through_z(tmp_b, tmp_c, zback_e)

    def put_edge(j, value):
        edge[j] = value

    y_back(tmp_c, pick_e, put_edge)

    x_forward(win_m, pick_m, work, 10)

    def main_step(a, _):
        y_forward(a, work, pick_m)
        through_z(tmp_a, tmp_b, zfwd_m)
        scale(a, eig_m, eig_m)
        through_z(tmp_b, tmp_c, zback_m)

        def put(j, value):
            work[a, j] = value

        y_back(tmp_c, pick_m, put)
        return 0

    lax.fori_loop(0, 10, main_step, 0)

    for n, j in ((0, 0), (1, 9)):
        def put_end(i, main, n=n):
            ends[n, i - 1] = main

        x_back(work, edge, pick_m, j, put_end)
    for i in range(8):
        tile = jnp.where(upper[0:8], ends[1, i], ends[0, i])
        rim_rows[8 * i : 8 * i + 8, :] = unplace(tile, sub, lane)
    for ix in range(4):
        for jy in range(2):
            rim_ref[pl.ds(32 * jy + 8 * ix, 8), :] = rim_rows[pl.ds(2 * ix + jy, 8, stride=8), :]


def x_back(work, edge, pick, j, put):
    sub, lane, kz = grids()
    wide = iota((16, LANES), 1)
    column = [work[a, j] for a in range(10)]
    first = dot_rows([(row(pick, a), column[a]) for a in range(10)])
    last = dot_rows([(row(pick, 90 + a), column[a]) for a in range(10)])
    side = edge[j]
    for i in range(1, 9):
        total = dot_rows([(row(pick, 10 * i + a), column[a]) for a in range(10)])
        if i == 1:
            total = total + jnp.where(wide >= 32, pltpu.roll(last, 32, 1), side)
        if i == 8:
            total = total + jnp.where(wide < 96, pltpu.roll(first, 96, 1), side)
        put(i, join_z(total, sub, kz))


def back_kernel(work, edge, ends, pick, fine_ref, out_rows):
    sub, lane, kz = grids()
    upper = (lane & 16) != 0

    def step(j, _):
        def put(i, tile):
            tile = tile + jnp.where(upper & (j == 1), pltpu.roll(ends[1, i - 1], 16, 1), 0.0)
            tile = tile + jnp.where(upper | (j != 8), 0.0, pltpu.roll(ends[0, i - 1], 112, 1))
            out_rows[pl.ds(pl.multiple_of(((i - 1) * 8 + j - 1) * 8, 8), 8), :] = unplace(tile, sub, lane)

        x_back(work, edge, pick, j, put)
        return 0

    lax.fori_loop(1, 9, step, 0)
    for ix in range(4):
        for jy in range(2):
            r = 2 * ix + jy
            for i in range(8):
                fine_ref[pl.ds(128 * ix + 16 * i + 8 * jy, 8), :] = out_rows[pl.ds(64 * i + r, 8, stride=8), :]


def tree_kernel(got_ref, rim_ref, pay_ref):
    p = lax.axis_index("gx")
    q = lax.axis_index("gy")
    bits = q + 1
    total = jnp.zeros((1, 384), F32)
    for t in range(64):
        inside = (t >> bits) == (p >> bits)
        total = total + jnp.where(inside, got_ref[t], 0.0)
    for peer in range(8):
        pay_ref[peer, 0:32, :] = jnp.where(peer < q, rim_ref[0:32, :], rim_ref[32:64, :])
        for n in range(3):
            pay_ref[peer, 32 + n : 33 + n, :] = total[:, LANES * n : LANES * (n + 1)]
        pay_ref[peer, 35:40, :] = jnp.zeros((5, LANES), F32)


def up_kernel(
    first_ref, own_ref, got_ref, pan_hbm, num_ref, fine_ref, out_ref, line_ref, value_ref, vertex_ref, pan_ref, sems
):
    q = lax.axis_index("gy")
    copies = []
    for n, low in enumerate(range(0, 255, 64)):
        part = pl.ds(low, min(64, 255 - low))
        copies.append(pltpu.make_async_copy(pan_hbm.at[part, :], pan_ref.at[part, :], sems.at[n]))
        copies[n].start()
    line_ref[...] = jnp.zeros((32, LANES), F32)
    line_ref[0:2, :] = own_ref[0:2, :]
    for level in range(1, 4):
        total = jnp.zeros((1, LANES), F32)
        for peer in range(8):
            inside = (peer >> level) == (q >> level)
            total = total + jnp.where(inside, first_ref[peer, 31 + level : 32 + level, :], 0.0)
        line_ref[1 + level : 2 + level, :] = total
    for peer in range(6):
        line_ref[5 + 3 * peer : 8 + 3 * peer, :] = got_ref[peer, 32:35, :]
    here = pltpu.roll(line_ref[0:24], 127, 1)
    after = pltpu.roll(line_ref[1:25], 127, 1)
    coeff = jnp.where(iota((24, LANES), 1) == 127, after, here)
    for n, low in enumerate(range(0, 255, 64)):
        high = min(low + 64, 255)
        copies[n].wait()
        total = pan_ref[low:high, 0:LANES] * coeff[0:1]
        for c in range(1, 22):
            total = total + pan_ref[low:high, c * LANES : (c + 1) * LANES] * coeff[c : c + 1]
        value = jnp.sum(total, axis=1, keepdims=True)
        value = value + jnp.sum(pan_ref[low:high, 2816:2943] * coeff[22:23, 0:127], axis=1, keepdims=True)
        value_ref[low:high, :] = jnp.broadcast_to(value, (high - low, LANES))
    value_ref[255:256, :] = jnp.zeros((1, LANES), F32)
    vertex_ref[...] = jnp.zeros((16, LANES), F32)
    rows = iota((256, 17), 0)
    values = value_ref[:, 0:17]
    for i in range(5):
        for j in range(3):
            k = 3 * i + j
            vertex_ref[k : k + 1, 0:17] = jnp.sum(jnp.where(num_ref[i, j : j + 1, :] == rows, values, 0.0), axis=0, keepdims=True)
    depth = hat(iota((LANES, LANES), 1), iota((LANES, LANES), 0))
    plane = plane_hat(iota((512, 16), 0), iota((512, 16), 1))
    half = jnp.dot(vertex_ref[...], depth, precision=exact)
    out_ref[...] = fine_ref[...] + jnp.dot(plane, half, precision=exact)
    low_face = jnp.where(q > 0, got_ref[jnp.maximum(q - 1, 0), 0:32, :], 0.0)
    high_face = jnp.where(q < 7, got_ref[jnp.minimum(q + 1, 7), 0:32, :], 0.0)
    out_ref[pl.ds(0, 32, stride=16), :] = out_ref[pl.ds(0, 32, stride=16), :] + low_face
    out_ref[pl.ds(15, 32, stride=16), :] = out_ref[pl.ds(15, 32, stride=16), :] + high_face


VM = pltpu.VMEM
ANYWHERE = None


def call(kernel, outs, scratch=(), ins=None, sems=0, cost=0, limit=24, aliases=None):
    shapes = [
        jax.ShapeDtypeStruct(o[0], o[2] if len(o) > 2 else F32) if o[1] is None else o[1](o[0], o[2] if len(o) > 2 else F32)
        for o in outs
    ]
    spaces = [pltpu.VMEM(s, F32) for s in scratch]
    if sems:
        spaces.append(pltpu.SemaphoreType.DMA((sems,)))
    run = pl.pallas_call(
        kernel,
        out_shape=shapes,
        in_specs=[pl.BlockSpec(memory_space=m or pltpu.VMEM) for m in ins],
        out_specs=[pl.BlockSpec(memory_space=pltpu.VMEM) for _ in outs],
        scratch_shapes=spaces,
        input_output_aliases=aliases or {},
        compiler_params=pltpu.CompilerParams(vmem_limit_bytes=limit << 20),
        cost_estimate=pl.CostEstimate(flops=cost, bytes_accessed=cost // 400, transcendentals=0),
    )

    def apply(*operands):
        held = [x if m is None else pltpu.with_memory_space_constraint(x, m) for x, m in zip(operands, ins, strict=True)]
        return run(*held)

    return apply


def spread_to(block, axis):
    return lax.all_to_all(block, axis, 0, 0, tiled=True)


def shards(residual, elem_class, basis, eigenvalues, vertex_number, panels):
    field = residual.reshape(512, LANES)
    I32 = jnp.int32
    pay, own, res, num, cls, table, eigen = call(
        down_kernel,
        [
            ((8, 40, 128), None), ((24, 128), VM), ((512, 128), VM), ((5, 3, 17), VM, I32),
            ((4, 2, 16), VM, I32), ((3, 10, 8, 10), VM), ((3, 8, 10), VM),
        ],
        [(40, 128), (255, 2943)], ins=[pltpu.HBM] * 6, sems=6,
    )(field, vertex_number, panels, elem_class, basis.transpose(1, 2, 0, 3), eigenvalues.transpose(1, 0, 2))
    first = spread_to(pay, "gy")
    win, basis2, eigen2, pick, eig, zfwd, zback = call(
        tile_kernel,
        [
            ((10, 11, 16, 128), VM), ((8, 300), VM), ((8, 30), VM), ((304, 128), VM), ((40, 128), VM),
            ((10, 16, 128), VM), ((10, 16, 128), VM),
        ],
        [(512, 128)], ins=[VM] * 4, cost=2_000_000_000,
    )(res, cls, table, eigen)
    right, left, tree, face = call(
        share_kernel, [((168, 128), None), ((168, 128), None), ((64, 1, 384), None), ((64, 128), VM)], ins=[None, VM, VM]
    )(first, res, cls)
    from_left = lax.ppermute(right, "gx", [(i, i + 1) for i in range(63)])
    from_right = lax.ppermute(left, "gx", [(i + 1, i) for i in range(63)])
    summed = spread_to(tree, "gx")
    win, work, edge, ends, rim = call(
        solve_kernel,
        [((10, 11, 16, 128), VM), ((10, 10, 16, 128), VM), ((10, 16, 128), VM), ((2, 8, 8, 128), VM), ((64, 128), VM)],
        [
            (648, 128), (64, 128), (10, 11, 16, 128), (304, 128), (40, 128), (10, 16, 128), (10, 16, 128),
            (56, 128), (8, 128), (5, 10, 16, 128), (10, 16, 128), (10, 16, 128), (10, 16, 128), (64, 128),
        ],
        ins=[VM] * 8 + [None, None], cost=8_000_000_000, aliases={0: 0},
    )(win, basis2, eigen2, pick, eig, zfwd, zback, face, from_left, from_right)
    (pay,) = call(tree_kernel, [((8, 40, 128), None)], ins=[None, VM])(summed, rim)
    second = spread_to(pay, "gy")
    (fine,) = call(back_kernel, [((512, 128), VM)], [(512, 128)], ins=[VM] * 4, cost=3_000_000_000)(work, edge, ends, pick)
    (out,) = call(up_kernel, [((512, 128), None)], [(32, 128), (256, 128), (16, 128), (255, 2943)], ins=[None, VM, None, pltpu.HBM, VM, VM], sems=4)(
        first, own, second, panels, num, fine
    )
    return out.reshape(residual.shape)


def solution(mesh):
    return jax.shard_map(
        shards,
        mesh=mesh,
        in_specs=(
            P(None, "gx", "gy", None),
            P("gx", "gy", None),
            P(),
            P(),
            P("gx", "gy", None),
            P("gx", "gy"),
        ),
        out_specs=P(None, "gx", "gy", None),
        check_vma=False,
    )
```

time: 78.9 us -> 72 us (0.913)
  local copies, waits for them, and re-layouts: 14.4 us -> 0 us
  blocking collectives: 24.6 us -> 14.8 us
  waiting for transfers between devices: 0.01 us -> 9.08 us
  starting transfers between devices: 21.3 us -> 27.5 us
  Pallas kernels: 17.8 us -> 20.1 us
    unnamed x48 -> x0, local copies, waits for them, and re-layouts: 13.1 us -> none
    all_to_all x2 -> x1, blocking collectives: 24.6 us -> 14.8 us  [spread_to(): return lax.all_to_all(block, axis, 0, 0, tiled=True)]
    all_to_all x1 -> x2, waiting for transfers between devices: 0.01 us -> 9.07 us  [spread_to(): return lax.all_to_all(block, axis, 0, 0, tiled=True)]
    all_to_all x1 -> x2, starting transfers between devices: 18.7 us -> 25 us  [spread_to(): return lax.all_to_all(block, axis, 0, 0, tiled=True)]
    pallas_call x5 -> x7, Pallas kernels: 17.8 us -> 20.1 us  [apply(): return run(*held)]
    reshape x2 -> x0, local copies, waits for them, and re-layouts: 1.36 us -> none  [the longest x1 0.7 us: shards(): table = basis.reshape(NCLASS, 3 * NEXT * NEXT)]
  transfers between devices with their start and end apart: 3 -> 4, of which waited for: 0 -> 2; matrix products, arithmetic and copies ran while one was open for 2% -> 0% of each run, Pallas kernels for 18% -> 18%
where the time goes in v1:
time: 72 us; the launch traced here: 71.6 us
  starting transfers between devices  27.5 us (38%)
  Pallas kernels  20.1 us (28%)
  blocking collectives  14.8 us (21%)
  waiting for transfers between devices  9.08 us (13%)
    all_to_all x2, starting transfers between devices, spread_to(): return lax.all_to_all(block, axis, 0, 0, tiled=True)  25 us
    pallas_call x7, Pallas kernels, apply(): return run(*held)  20.1 us
    all_to_all x1, blocking collectives, spread_to(): return lax.all_to_all(block, axis, 0, 0, tiled=True)  14.8 us
    all_to_all x2, waiting for transfers between devices, spread_to(): return lax.all_to_all(block, axis, 0, 0, tiled=True)  9.07 us
  transfers between devices with their start and end apart: 4, of which 2 were waited for; matrix products, arithmetic and copies ran while one was open for 0% of the time, Pallas kernels for 18%

profile of v1, /device:TPU:1, one launch (start us, length us, event | category | flops | bytes accessed | tf_op | source)
XLA Modules:
  0.0 71.6 jit_solution(4777796327023132609)
XLA Ops:
  0.0 2.4 %shard_map.64 = (f32[8,40,128]{2,1,0:T(8,128)S(1)}, f32[24,128]{1,0:T(8,128)S(1)}, f32[512,128]{1,0:T(8,128)S(1)}, s32[5,3,17]{2,1,0:T(4,128)S(1)}, s32[4,2,16]{...) custom-call(f32[512,128]{1,0:T(8,128)} %bitcast.4, s32[5,3,17]{2,1,0:T(4,128)} %num_hbm.1, ...), custom_call_target="tpu_custom_call" | custom-call | tf_op jit(solution)/shard_map/pallas_call | solution.py:479
  2.4 14.8 %all_to_all.15.got_ref.first_ref = f32[8,40,128]{2,1,0:T(8,128)S(1)} all-to-all(f32[8,40,128]{2,1,0:T(8,128)S(1)} %get-tuple-element.27), channel_id=1, replica_groups=mesh['gx'=64,'gy'=8] {'gy'}, dimensions={0} | all-to-all | bytes 327680 | tf_op jit(solution)/shard_map/all_to_all | solution.py:485
  17.2 0.7 shard_map.65
  17.9 1.3 %collective-permute-start = (f32[168,128]{1,0:T(8,128)S(1)}, f32[168,128]{1,0:T(8,128)S(1)}, u32[]{:S(2)}, u32[]{:S(2)}) collective-permute-start(f32[168,128]{1,0:T(8,128)S(1)} %get-tuple-element.42), channel_id=1, source_target_pairs={{0,8},{8,16},{16,24},{24,32},{32,40},{40,48},{48,56},{56,64},{64,7... | collective-permute-start | bytes 258056 | tf_op jit(solution)/shard_map/ppermute | solution.py:511
  19.2 1.3 %collective-permute-start.1 = (f32[168,128]{1,0:T(8,128)S(1)}, f32[168,128]{1,0:T(8,128)S(1)}, u32[]{:S(2)}, u32[]{:S(2)}) collective-permute-start(f32[168,128]{1,0:T(8,128)S(1)} %get-tuple-element.43), channel_id=1, source_target_pairs={{8,0},{16,8},{24,16},{32,24},{40,32},{48,40},{56,48},{64,56},{72,6... | collective-permute-start | bytes 258056 | tf_op jit(solution)/shard_map/ppermute | solution.py:512
  20.5 2.4 %shard_map.66 = (f32[10,11,16,128]{3,2,1,0:T(8,128)S(1)}, f32[8,300]{1,0:T(8,128)S(1)}, f32[8,30]{1,0:T(8,128)S(1)}, f32[304,128]{1,0:T(8,128)S(1)}, f32[40,128]...) custom-call(f32[512,128]{1,0:T(8,128)S(1)} %get-tuple-element.29.res_ref, ...), custom_call_target="tpu_custom_call" | custom-call | flops 2000000000 | bytes 5000000 | tf_op jit(solution)/shard_map/pallas_call | solution.py:479
  22.9 18.7 %all-to-all-start.1 = ((f32[64,1,384]{2,1,0:T(1,128)}), f32[64,1,384]{2,1,0:T(1,128)S(1)}, u32[]{:S(2)}, u32[]{:S(2)}) async-start(f32[64,1,384]{2,1,0:T(1,128)} %get-tuple-element.31), calls=%async_computation.1 | async-start | bytes 196608 | tf_op jit(solution)/shard_map/all_to_all | solution.py:485
  41.6 0.0 collective-permute-done.from_left
  41.6 0.0 collective-permute-done.1.from_right
  41.6 7.8 %shard_map.67 = (f32[10,11,16,128]{3,2,1,0:T(8,128)S(1)}, f32[10,10,16,128]{3,2,1,0:T(8,128)S(1)}, f32[10,16,128]{2,1,0:T(8,128)S(1)}, f32[2,8,8,128]{3,2,1,0:T(8,128)S(1)}, f32[64,128]{1,0:T(8,128)S(1)}) custom-call(f32[10,11,16,128]{3,2,1,0:T(8,128)S(1)} %get-tuple-element.34.win_in, ...), custom_call_target="tpu_custom_call", output_to_operand_aliasing={{0}: (0, {})} | custom-call | flops 8000000000 | bytes 20000000 | tf_op jit(solution)/shard_map/pallas_call | solution.py:479
  49.4 5.9 %all-to-all-done.1.got_ref = f32[64,1,384]{2,1,0:T(1,128)S(1)} async-done(((f32[64,1,384]{2,1,0:T(1,128)}), f32[64,1,384]{2,1,0:T(1,128)S(1)}, u32[]{:S(2)}, u32[]{:S(2)}) %all-to-all-start.1) | async-done | bytes 98336 | tf_op jit(solution)/shard_map/all_to_all | solution.py:485
  55.3 0.8 %shard_map.68 = f32[8,40,128]{2,1,0:T(8,128)} custom-call(f32[64,1,384]{2,1,0:T(1,128)S(1)} %all-to-all-done.1.got_ref, f32[64,128]{1,0:T(8,128)S(1)} %get-tuple-element.44.rim_ref), custom_call_target="tpu_custom_call" | custom-call | tf_op jit(solution)/shard_map/pallas_call | solution.py:479
  56.1 6.3 %all-to-all-start.2 = ((f32[8,40,128]{2,1,0:T(8,128)}), f32[8,40,128]{2,1,0:T(8,128)S(1)}, u32[]{:S(2)}, u32[]{:S(2)}) async-start(f32[8,40,128]{2,1,0:T(8,128)} %shard_map.68), calls=%async_computation.2 | async-start | bytes 327680 | tf_op jit(solution)/shard_map/all_to_all | solution.py:485
  62.4 2.4 %shard_map.69.fine_ref = f32[512,128]{1,0:T(8,128)S(1)} custom-call(f32[10,10,16,128]{3,2,1,0:T(8,128)S(1)} %get-tuple-element.46.work, f32[10,16,128]{2,1,0:T(8,128)S(1)} %get-tuple-element.47.edge, f32[2,8,8,128]{3,2,1,0:T(8,128)S(1)} %get-tuple-element.48.ends, f32[304,128]{1,0:T(8,128)S(1)} %get-tuple-element.37.pick_m.pick), custom_call_target="tpu_custom_call" | custom-call | flops 3000000000 | bytes 7500000 | tf_op jit(solution)/shard_map/pallas_call | solution.py:479
  64.8 3.2 %all-to-all-done.2.got_ref = f32[8,40,128]{2,1,0:T(8,128)S(1)} async-done(((f32[8,40,128]{2,1,0:T(8,128)}), f32[8,40,128]{2,1,0:T(8,128)S(1)}, u32[]{:S(2)}, u32[]{:S(2)}) %all-to-all-start.2) | async-done | bytes 163872 | tf_op jit(solution)/shard_map/all_to_all | solution.py:485
  68.0 3.7 %shard_map.70 = f32[512,128]{1,0:T(8,128)} custom-call(f32[8,40,128]{2,1,0:T(8,128)S(1)} %all_to_all.15.got_ref.first_ref, f32[24,128]{1,0:T(8,128)S(1)} %get-tuple-element.28.own_ref, f32[8,40,128]{2,1,0:T(8,128)S(1)} %all-to-all-done.2.got_ref, f32[255,2943]{1,0:T(8,128)} %pan_hbm.3, s32[5,3,17]{2,1,0:T(4,128)S(1)} %get-tuple-element.45.num_ref, ...), custom_call_target="tpu_custom_call" | custom-call | tf_op jit(solution)/shard_map/pallas_call | solution.py:479
Async XLA Ops:
  17.9 23.7 %collective-permute-start = (f32[168,128]{1,0:T(8,128)S(1)}, f32[168,128]{1,0:T(8,128)S(1)}, u32[]{:S(2)}, u32[]{:S(2)}) collective-permute-start(f32[168,128]{1,0:T(8,128)S(1)} %get-tuple-element.42), channel_id=1, source_target_pairs={{0,8},{8,16},{16,24},{24,32},{32,40},{40,48},{48,56},{56,64},{64,7... | collective-permute-start | bytes 258056 | tf_op jit(solution)/shard_map/ppermute | solution.py:511
  19.2 22.4 %collective-permute-start.1 = (f32[168,128]{1,0:T(8,128)S(1)}, f32[168,128]{1,0:T(8,128)S(1)}, u32[]{:S(2)}, u32[]{:S(2)}) collective-permute-start(f32[168,128]{1,0:T(8,128)S(1)} %get-tuple-element.43), channel_id=1, source_target_pairs={{8,0},{16,8},{24,16},{32,24},{40,32},{48,40},{56,48},{64,56},{72,6... | collective-permute-start | bytes 258056 | tf_op jit(solution)/shard_map/ppermute | solution.py:512
  22.9 32.5 %all-to-all-start.1 = ((f32[64,1,384]{2,1,0:T(1,128)}), f32[64,1,384]{2,1,0:T(1,128)S(1)}, u32[]{:S(2)}, u32[]{:S(2)}) async-start(f32[64,1,384]{2,1,0:T(1,128)} %get-tuple-element.31), calls=%async_computation.1 | async-start | bytes 196608 | tf_op jit(solution)/shard_map/all_to_all | solution.py:485
  56.1 11.9 %all-to-all-start.2 = ((f32[8,40,128]{2,1,0:T(8,128)}), f32[8,40,128]{2,1,0:T(8,128)S(1)}, u32[]{:S(2)}, u32[]{:S(2)}) async-start(f32[8,40,128]{2,1,0:T(8,128)} %shard_map.68), calls=%async_computation.2 | async-start | bytes 327680 | tf_op jit(solution)/shard_map/all_to_all | solution.py:485

commit v2 on v1

v2 whole, which is shorter than its diff:
```python
import functools

import jax
import jax.numpy as jnp
from jax import lax
from jax.experimental import pallas as pl
from jax.experimental.pallas import tpu as pltpu
from jax.sharding import PartitionSpec as P

NPR = 8
NEXT = 10
NCLASS = 8
LANES = 128
TOP = 128
CUTS = [(slice(low, min(low + 128, 2943)), min(128, 2943 - low)) for low in range(0, 2943, 128)]
HALO = NPR + 1
F32 = jnp.float32
exact = lax.Precision.HIGHEST
ORDER = (1, 2, 3, 4, 5, 6, 7, 8, 0, 9)


def iota(shape, axis):
    return lax.broadcasted_iota(jnp.int32, shape, axis)


def hat(point, vertex):
    place = (point.astype(F32) + 0.5) / NPR
    return jnp.maximum(0.0, 1.0 - jnp.abs(place - vertex.astype(F32)))


def moved(rows, table):
    high = rows.astype(jnp.bfloat16)
    rest = rows - high.astype(F32)
    middle = rest.astype(jnp.bfloat16)
    low = (rest - middle.astype(F32)).astype(jnp.bfloat16)
    total = jnp.dot(low, table, preferred_element_type=F32)
    total = total + jnp.dot(middle, table, preferred_element_type=F32)
    return total + jnp.dot(high, table, preferred_element_type=F32)


def plane_hat(point, vertex):
    third = (vertex.astype(F32) + 0.5) / 3.0
    big = third.astype(jnp.int32)
    return hat(point >> 4, big) * hat(point & 15, vertex - 3 * big)


def down_kernel(
    res_hbm, num_hbm, pan_hbm, cls_hbm, basis_hbm, value_hbm,
    pay_ref, own_ref, num_ref, cls_ref, top_ref, win, table_ref, eigen_ref, pick, eig, zfwd, zback, rows_ref,
    res_ref, basis_ref, value_ref, line_ref, low_ref, sems,
):
    q = lax.axis_index("gy")
    pairs = [
        (res_hbm, res_ref), (num_hbm, num_ref), (cls_hbm, cls_ref), (basis_hbm, basis_ref), (value_hbm, value_ref),
        (pan_hbm.at[pl.ds(0, TOP), :], top_ref), (pan_hbm.at[pl.ds(TOP, 255 - TOP), :], low_ref),
    ]
    copies = [pltpu.make_async_copy(source, target, sems.at[n]) for n, (source, target) in enumerate(pairs)]
    for copy in copies:
        copy.start()
    plane = plane_hat(iota((16, 512), 1), iota((16, 512), 0))
    depth = hat(iota((128, 17), 0), iota((128, 17), 1))
    line_ref[...] = jnp.zeros((40, LANES), F32)
    copies[0].wait()
    half = jnp.dot(plane, res_ref[...], precision=exact)
    vertex = jnp.dot(half, depth, precision=exact)
    low_face = res_ref[pl.ds(0, 32, stride=16), :]
    high_face = res_ref[pl.ds(15, 32, stride=16), :]
    for peer in range(8):
        pay_ref[peer, 0:32, :] = jnp.where(peer < q, low_face, high_face)
    copies[1].wait()
    rows = iota((256, 17), 0)
    spread = jnp.zeros((256, 17), F32)
    for i in range(5):
        for j in range(3):
            k = 3 * i + j
            spread = spread + jnp.where(num_ref[i, j : j + 1, :] == rows, vertex[k : k + 1, :], 0.0)
    ordered = jnp.broadcast_to(jnp.sum(spread, axis=1, keepdims=True), (256, LANES))

    rows_ref[...] = split_z(res_ref[...])
    for copy in copies[2:5]:
        copy.wait()
    for d in range(3):
        eigen_ref[:, 10 * d : 10 * d + 10] = value_ref[d]
        for i in range(10):
            low = 100 * d + 10 * i
            table_ref[:, low : low + 10] = basis_ref[d, i]
    kind = jnp.concatenate([cls_ref[ix].astype(F32) + 1.0 for ix in range(4)], axis=0)
    pick_tables(kind, table_ref, eigen_ref, pick, eig, zfwd, zback)
    columns = range(8)
    groups = [[rows_ref[128 * (r // 2) + 16 * i + 8 * (r % 2) : 128 * (r // 2) + 16 * i + 8 * (r % 2) + 8, :] for r in range(8)] for i in columns]
    for i, parts in zip(columns, with_outer(exchange(groups)), strict=True):
        for k, part in enumerate(parts):
            win[pl.ds((i * 11 + 12) * 16 + k, 8, stride=16), :] = part

    for copy in copies[5:]:
        copy.wait()
    for c, (cut, width) in enumerate(CUTS):
        piece = jnp.sum(top_ref[:, cut] * ordered[:TOP, :width], axis=0, keepdims=True)
        piece = piece + jnp.sum(low_ref[:, cut] * ordered[TOP:255, :width], axis=0, keepdims=True)
        line_ref[8 + c : 9 + c, :width] = piece
    here = pltpu.roll(line_ref[8:32], 1, 1)
    before = pltpu.roll(line_ref[7:31], 1, 1)
    own_ref[...] = jnp.where(iota((24, LANES), 1) == 0, before, here)
    for peer in range(8):
        pay_ref[peer, 32:35, :] = own_ref[2:5, :]
        pay_ref[peer, 35:37, :] = own_ref[8 + 2 * peer : 10 + 2 * peer, :]
        pay_ref[peer, 37:40, :] = own_ref[5:8, :] if peer == 7 else jnp.zeros((3, LANES), F32)


def share_kernel(got_ref, rows_ref, cls_ref, right_ref, left_ref, tree_ref, face_ref, four_ref):
    q = lax.axis_index("gy")
    face_ref[0:32, :] = jnp.where(q > 0, got_ref[jnp.maximum(q - 1, 0), 0:32, :], 0.0)
    face_ref[32:64, :] = jnp.where(q < 7, got_ref[jnp.minimum(q + 1, 7), 0:32, :], 0.0)
    total = got_ref[0, 35:40, :]
    for peer in range(1, 8):
        total = total + got_ref[peer, 35:40, :]
    four_ref[...] = jnp.zeros((8, LANES), F32)
    four_ref[0:3, :] = total[2:5]
    for level in range(1, 4):
        low = jnp.zeros((1, LANES), F32)
        for peer in range(8):
            inside = (peer >> level) == (q >> level)
            low = low + jnp.where(inside, got_ref[peer, 31 + level : 32 + level, :], 0.0)
        four_ref[2 + level : 3 + level, :] = low
    for ref, column, first in ((right_ref, 3, 23), (left_ref, 0, 0)):
        ref[0:144, :] = rows_ref[16 * first : 16 * first + 144, :]
        ref[144:153, :] = face_ref[first : first + 9, :]
        ref[153:162, :] = face_ref[32 + first : 41 + first, :]
        ref[162:168, :] = jnp.zeros((6, LANES), F32)
        ref[162:164, 0:16] = (cls_ref[column] + 1).astype(F32)
        ref[164:167, :] = total[2:5]
    line = jnp.concatenate([total[0:1], total[1:2]], axis=1)
    for t in range(64):
        tree_ref[t] = line


def grids():
    sub = iota((8, LANES), 0)
    lane = iota((8, LANES), 1)
    return sub, lane, lane & 15


def split_z(rows):
    lane = iota((LANES, LANES), 1)
    return moved(rows, (iota((LANES, LANES), 0) == (((lane & 15) << 3) | (lane >> 4))).astype(jnp.bfloat16))


def join_rows(rows):
    lane = iota((LANES, LANES), 0)
    return moved(rows, (iota((LANES, LANES), 1) == (((lane & 15) << 3) | (lane >> 4))).astype(jnp.bfloat16))


def exchange(groups):
    lane = iota((8, LANES), 1)
    groups = [list(parts) for parts in groups]
    for bit in (4, 2, 1):
        inside = (lane & (16 * bit)) != 0
        for parts in groups:
            for n in range(8):
                if n & bit:
                    continue
                low, high = parts[n], parts[n | bit]
                if bit == 4:
                    swap = pltpu.roll(jnp.where(inside, low, high), 64, 1)
                    parts[n] = jnp.where(inside, swap, low)
                    parts[n | bit] = jnp.where(inside, high, swap)
                else:
                    parts[n] = jnp.where(inside, pltpu.roll(high, 16 * bit, 1), low)
                    parts[n | bit] = jnp.where(inside, high, pltpu.roll(low, LANES - 16 * bit, 1))
    return groups


def with_outer(groups):
    kz = iota((8, LANES), 1) & 15
    before = [jnp.where(kz == 0, 0.0, pltpu.roll(parts[7], 1, 1)) for parts in groups]
    after = [jnp.where(kz == 15, 0.0, pltpu.roll(parts[0], 127, 1)) for parts in groups]
    return [parts + [b, a] for parts, b, a in zip(groups, before, after, strict=True)]


def at(i, j):
    return pl.ds(pl.multiple_of((i * 11 + j) * 16, 16), 16)


def join_z(total, sub, kz):
    main = total[0:8]
    tail = pltpu.roll(total[8:16], 7, 0)
    return main + jnp.where(
        sub == 7,
        jnp.where(kz == 15, 0.0, pltpu.roll(tail, 127, 1)),
        jnp.where((sub == 0) & (kz != 0), pltpu.roll(tail, 1, 1), 0.0),
    )


def row(ref, n):
    return jnp.broadcast_to(ref[pl.ds(n, 1), :], (16, LANES))


def dot_rows(pairs):
    total = None
    for a, b in pairs:
        total = a * b if total is None else total + a * b
    return total


def pick_tables(kind, table_ref, eigen_ref, pick, eig, zfwd, zback):
    group = iota((8, LANES), 0)
    lane = iota((8, LANES), 1)
    spread = (iota((16, LANES), 0) == (iota((16, LANES), 1) & 15)).astype(F32)
    laid = jnp.dot(kind, spread, precision=exact)
    laid = jnp.sum(jnp.where(group == (lane >> 4), laid, 0.0), axis=0, keepdims=True)
    onehot = (laid == (group + 1).astype(F32)).astype(F32)
    dims = (((0,), (0,)), ((), ()))
    pick[0:300, :] = lax.dot_general(table_ref[:, 0:300], onehot, dims, precision=exact, preferred_element_type=F32)
    eig[0:30, :] = lax.dot_general(eigen_ref[:, 0:30], onehot, dims, precision=exact, preferred_element_type=F32)
    eig[20:30, :] = eig[20:30, :] + jnp.where(laid == 0.0, 1.0, 0.0)
    eig[30:40, :] = jnp.ones((10, LANES), F32)
    for n, k in enumerate(ORDER):
        zfwd[n, 0:10, :] = pick[200 + 10 * k : 210 + 10 * k, :]
        zfwd[n, 10:16, :] = jnp.zeros((6, LANES), F32)
    for c in range(10):
        zback[c, 0:8, :] = pick[pl.ds(210 + c, 8, stride=10), :]
        zback[c, 8:16, :] = jnp.zeros((8, LANES), F32)
        zback[c, 8:9, :] = pick[200 + c : 201 + c, :]
        zback[c, 9:10, :] = pick[290 + c : 291 + c, :]


def solve_kernel(
    win_in, table_ref, eigen_ref, pick_m, eig_m, zfwd_m, zback_m, face_ref, from_left, from_right,
    win_m, fine_ref, rim_ref,
    work, edge, ends, tiles, rows_ref, rows_f, win_e, pick_e, eig_e, zfwd_e, zback_e, half_e, lxe, work_e, tmp_a, tmp_b, tmp_c, rim_rows,
):
    del win_in
    sub, lane, kz = grids()
    wide = iota((16, LANES), 1)
    upper = (wide & 16) != 0

    rows_f[0:64, :] = face_ref[...]
    rows_f[64:88, :] = from_left[144:168, :]
    rows_f[88:112, :] = from_right[144:168, :]
    rows_f[...] = split_z(rows_f[...])
    outer = [rows_f[32 * (r % 2) + 8 * (r // 2) : 32 * (r % 2) + 8 * (r // 2) + 8, :] for r in range(8)]
    beside = [rows_f[first : first + 8, :] for first in (65, 74, 88, 97)]
    corner = [jnp.broadcast_to(rows_f[n : n + 1, :], (8, LANES)) for n in (64, 73, 96, 105)]
    outer, beside, corner = with_outer(exchange([outer, beside + beside, corner + corner]))
    for k in range(10):
        win_m[pl.ds(21 * 16 + k, 8, stride=176), :] = outer[k]
        win_e[pl.ds(21 * 16 + k, 8, stride=176), :] = beside[k]
        win_e[109 * 16 + k : 109 * 16 + k + 1, :] = corner[k][0:1]

    def fill(n, _):
        columns = [9 * n + m for m in range(9)]
        groups = []
        for i in columns:
            layer = jnp.where(i == 8, 0, i + 1)
            parts = [from_left[pl.ds(pl.multiple_of(16 * layer + 8 * jy, 8), 8), :] for jy in range(2)]
            parts += [from_right[pl.ds(pl.multiple_of(16 * i + 8 * jy, 8), 8), :] for jy in range(2)]
            groups.append(parts + parts)
        for i, parts in zip(columns, with_outer(exchange(groups)), strict=True):
            for k, part in enumerate(parts):
                win_e[pl.ds((i * 11 + 12) * 16 + k, 8, stride=16), :] = part
        return 0

    lax.fori_loop(0, 1, fill, 0)

    near = [from_left[162:164, 0:16], from_right[162:164, 0:16]]
    pick_tables(jnp.concatenate(near + near, axis=0), table_ref, eigen_ref, pick_e, eig_e, zfwd_e, zback_e)
    low_half = iota((5, LANES), 1) < 64
    for i in range(10):
        half_e[5 * i : 5 * i + 5, :] = jnp.where(low_half, pick_e[10 * i : 10 * i + 5, :], pick_e[10 * i + 5 : 10 * i + 10, :])
    half_e[50:55, :] = jnp.where((iota((5, LANES), 1) & 32) == 0, half_e[45:50, :], half_e[0:5, :])
    lxe[0:5, :] = jnp.where(low_half, eig_e[0:5, :], eig_e[5:10, :])

    second = (wide & 32) != 0

    def x_halo(lines):
        ahead = [win_m[at(8, j), :] for j in lines]
        back = [win_m[at(1, j), :] for j in lines]
        extra = [win_e[at(9, j), :] for j in lines]
        near = [win_e[at(8, j), :] for j in lines]
        far = [win_e[at(1, j), :] for j in lines]
        for n, j in enumerate(lines):
            win_m[at(0, j), :] = jnp.where(wide >= 32, pltpu.roll(ahead[n], 32, 1), near[n])
            win_m[at(9, j), :] = jnp.where(wide < 96, pltpu.roll(back[n], 96, 1), far[n])
            both = pltpu.roll(jnp.where(wide < 64, back[n], ahead[n]), 64, 1)
            win_e[at(0, j), :] = jnp.where(second, jnp.where(wide >= 64, ahead[n], both), extra[n])
            win_e[at(9, j), :] = jnp.where(second, extra[n], jnp.where(wide < 64, back[n], both))

    def x_halos(n, _):
        x_halo([1 + 8 * n + m for m in range(8)])
        return 0

    lax.fori_loop(0, 1, x_halos, 0)
    x_halo([10])

    def y_halo(n, _):
        columns = [(win, 10 * n + m) for m in range(10) for win in (win_m, win_e)]
        outer = [win[at(i, 10), :] for win, i in columns]
        last = [pltpu.roll(win[at(i, 8), :], 16, 1) for win, i in columns]
        first = [pltpu.roll(win[at(i, 1), :], 112, 1) for win, i in columns]
        for m, (win, i) in enumerate(columns):
            win[at(i, 0), :] = jnp.where(upper, last[m], outer[m])
            win[at(i, 9), :] = jnp.where(upper, outer[m], first[m])
        return 0

    lax.fori_loop(0, 1, y_halo, 0)

    def x_forward(win, table, target, count):
        def step(j, _):
            column = [win[at(i, j), :] for i in range(10)]
            for a in range(count):
                target[a, j] = dot_rows([(row(table, count * i + a), column[i]) for i in range(10)])
            return 0
        lax.fori_loop(0, 10, step, 0)

    def through_z(source, target, zfwd):
        table = [zfwd[k] for k in range(10)]
        for b in range(10):
            target[b] = dot_rows([(table[k], jnp.broadcast_to(source[b, k : k + 1, :], (16, LANES))) for k in range(10)])

    def y_forward(a, source, pick):
        column = [source[a, j] for j in range(10)]
        for b in range(10):
            tmp_a[b] = dot_rows([(row(pick, 100 + 10 * j + b), column[j]) for j in range(10)])

    def scale(a, eig, lx):
        level = row(lx, a) + eig[20:36, :]
        for b in range(10):
            tmp_b[b] = tmp_b[b] / (level + row(eig, 10 + b))

    def y_back(source, pick, store):
        column = [source[b] for b in range(10)]
        for j in range(10):
            store(j, dot_rows([(row(pick, 100 + 10 * j + b), column[b]) for b in range(10)]))

    x_forward(win_e, half_e, work_e, 5)
    for b in range(10):
        edge[b] = jnp.zeros((16, LANES), F32)

    def edge_step(a, _):
        y_forward(a, work_e, pick_e)
        through_z(tmp_a, tmp_b, zfwd_e)
        scale(a, eig_e, lxe)
        weight = row(half_e, 50 + a)
        for b in range(10):
            edge[b] = edge[b] + weight * tmp_b[b]
        return 0

    lax.fori_loop(0, 5, edge_step, 0)
    for b in range(10):
        tmp_b[b] = edge[b] + pltpu.roll(edge[b], 64, 1)
    through_z(tmp_b, tmp_c, zback_e)

    def put_edge(j, value):
        edge[j] = value

    y_back(tmp_c, pick_e, put_edge)

    x_forward(win_m, pick_m, work, 10)

    def main_step(a, _):
        y_forward(a, work, pick_m)
        through_z(tmp_a, tmp_b, zfwd_m)
        scale(a, eig_m, eig_m)
        through_z(tmp_b, tmp_c, zback_m)

        def put(j, value):
            work[a, j] = value

        y_back(tmp_c, pick_m, put)
        return 0

    lax.fori_loop(0, 10, main_step, 0)

    for n, j in ((0, 0), (1, 9)):
        def put_end(i, main, n=n):
            ends[n, i - 1] = main

        x_back(work, edge, pick_m, j, put_end)
    for i in range(8):
        rim_rows[8 * i : 8 * i + 8, :] = jnp.where(upper[0:8], ends[1, i], ends[0, i])
    (parts,) = exchange([[rim_rows[pl.ds(k, 8, stride=8), :] for k in range(8)]])
    for r in range(8):
        rows_f[32 * (r % 2) + 8 * (r // 2) : 32 * (r % 2) + 8 * (r // 2) + 8, :] = parts[r]
    rim_ref[...] = join_rows(rows_f[0:64, :])
    inner = upper[0:8]

    def solve(j, _):
        def put(i, tile):
            tile = tile + jnp.where(inner & (j == 1), pltpu.roll(ends[1, i - 1], 16, 1), 0.0)
            tile = tile + jnp.where(inner | (j != 8), 0.0, pltpu.roll(ends[0, i - 1], 112, 1))
            tiles[pl.ds(pl.multiple_of(((i - 1) * 8 + j - 1) * 8, 8), 8), :] = tile

        x_back(work, edge, pick_m, j, put)
        return 0

    lax.fori_loop(1, 9, solve, 0)

    def step(n, _):
        columns = [8 * n + m for m in range(8)]
        groups = exchange([[tiles[pl.ds(i * 64 + k, 8, stride=8), :] for k in range(8)] for i in columns])
        for i, parts in zip(columns, groups, strict=True):
            for r in range(8):
                rows_ref[pl.ds(pl.multiple_of(128 * (r // 2) + 16 * i + 8 * (r % 2), 8), 8), :] = parts[r]
        return 0

    lax.fori_loop(0, 1, step, 0)
    fine_ref[...] = join_rows(rows_ref[...])


def x_back(work, edge, pick, j, put):
    sub, lane, kz = grids()
    wide = iota((16, LANES), 1)
    column = [work[a, j] for a in range(10)]
    first = dot_rows([(row(pick, a), column[a]) for a in range(10)])
    last = dot_rows([(row(pick, 90 + a), column[a]) for a in range(10)])
    side = edge[j]
    for i in range(1, 9):
        total = dot_rows([(row(pick, 10 * i + a), column[a]) for a in range(10)])
        if i == 1:
            total = total + jnp.where(wide >= 32, pltpu.roll(last, 32, 1), side)
        if i == 8:
            total = total + jnp.where(wide < 96, pltpu.roll(first, 96, 1), side)
        put(i, join_z(total, sub, kz))


def tree_kernel(got_ref, rim_ref, four_ref, from_left, from_right, pay_ref):
    p = lax.axis_index("gx")
    q = lax.axis_index("gy")
    totals = []
    for n in range(2):
        bits = 2 + (2 * q + n) // 3
        total = jnp.zeros((1, LANES), F32)
        for t in range(64):
            inside = (t >> bits) == (p >> bits)
            total = total + jnp.where(inside, got_ref[t, :, LANES * n : LANES * (n + 1)], 0.0)
        totals.append(total)
    four = four_ref[0:3, :] + jnp.where((p & 1) == 0, from_right[164:167, :], from_left[164:167, :])
    for peer in range(8):
        pay_ref[peer, 0:32, :] = jnp.where(peer < q, rim_ref[0:32, :], rim_ref[32:64, :])
        pay_ref[peer, 32:33, :] = totals[0]
        pay_ref[peer, 33:34, :] = totals[1]
        pay_ref[peer, 34:37, :] = four
        pay_ref[peer, 37:40, :] = jnp.zeros((3, LANES), F32)


def up_kernel(
    four_ref, own_ref, got_ref, pan_hbm, num_ref, top_ref, fine_ref, out_ref, line_ref, coeff_ref, sums_ref, vertex_ref, low_ref, sems
):
    q = lax.axis_index("gy")
    copies = []
    for n, (low, high) in enumerate(((0, 64), (64, 255 - TOP))):
        part = pl.ds(low, high - low)
        copies.append(pltpu.make_async_copy(pan_hbm.at[pl.ds(TOP + low, high - low), :], low_ref.at[part, :], sems.at[n]))
        copies[n].start()
    line_ref[...] = jnp.zeros((32, LANES), F32)
    line_ref[0:2, :] = own_ref[0:2, :]
    line_ref[2:5, :] = four_ref[3:6, :]
    line_ref[5:8, :] = got_ref[7, 34:37, :]
    for peer in range(8):
        line_ref[8 + 2 * peer : 10 + 2 * peer, :] = got_ref[peer, 32:34, :]
    here = pltpu.roll(line_ref[0:24], 127, 1)
    after = pltpu.roll(line_ref[1:25], 127, 1)
    coeff_ref[...] = jnp.where(iota((24, LANES), 1) == 127, after, here)
    weights = [jnp.broadcast_to(coeff_ref[c : c + 1, :width], (8, width)) for c, (_, width) in enumerate(CUTS)]

    def product(ref, first, place, count):
        total = ref[place, CUTS[0][0]] * weights[0][:count]
        for weight, (cut, _) in zip(weights[1:22], CUTS[1:22], strict=True):
            total = total + ref[place, cut] * weight[:count]
        end = ref[place, CUTS[22][0]] * weights[22][:count]
        sums_ref[pl.ds(first, count), :] = total
        sums_ref[pl.ds(first, count), 0:127] = total[:, 0:127] + end

    def top_step(g, _):
        first = pl.multiple_of(8 * g, 8)
        product(top_ref, first, pl.ds(first, 8), 8)
        return 0

    def low_step(g, _):
        first = pl.multiple_of(8 * g, 8)
        product(low_ref, TOP + first, pl.ds(first, 8), 8)
        return 0

    lax.fori_loop(0, TOP // 8, top_step, 0, unroll=4)
    copies[0].wait()
    lax.fori_loop(0, 8, low_step, 0, unroll=4)
    copies[1].wait()
    lax.fori_loop(8, (255 - TOP) // 8, low_step, 0, unroll=7)
    product(low_ref, 248, pl.ds(248 - TOP, 7), 7)
    sums_ref[255:256, :] = jnp.zeros((1, LANES), F32)
    values = jnp.broadcast_to(jnp.sum(sums_ref[...], axis=1, keepdims=True), (256, 17))
    vertex_ref[...] = jnp.zeros((16, LANES), F32)
    rows = iota((256, 17), 0)
    for i in range(5):
        for j in range(3):
            k = 3 * i + j
            vertex_ref[k : k + 1, 0:17] = jnp.sum(jnp.where(num_ref[i, j : j + 1, :] == rows, values, 0.0), axis=0, keepdims=True)
    depth = hat(iota((LANES, LANES), 1), iota((LANES, LANES), 0)).astype(jnp.bfloat16)
    vertex_ref[...] = moved(vertex_ref[...], depth)
    rise = (2.0 * iota((8, LANES), 0).astype(F32) + 1.0) / 16.0
    planes = []
    for i in range(5):
        three = [jnp.broadcast_to(vertex_ref[3 * i + j : 3 * i + j + 1, :], (8, LANES)) for j in range(3)]
        planes.append([three[jy] * (1.0 - rise) + three[jy + 1] * rise for jy in range(2)])
    faces = (
        jnp.where(q > 0, got_ref[jnp.maximum(q - 1, 0), 0:32, :], 0.0),
        jnp.where(q < 7, got_ref[jnp.minimum(q + 1, 7), 0:32, :], 0.0),
    )
    edges = (iota((8, LANES), 0) == 0, iota((8, LANES), 0) == 7)
    for ix in range(4):
        for i in range(8):
            x = 8 * ix + i
            far = (2 * i + 1) / 16.0
            for jy in range(2):
                place = slice(16 * x + 8 * jy, 16 * x + 8 * jy + 8)
                value = fine_ref[place, :] + planes[ix][jy] * (1.0 - far) + planes[ix + 1][jy] * far
                out_ref[place, :] = value + jnp.where(edges[jy], faces[jy][x : x + 1, :], 0.0)


VM = pltpu.VMEM
ANYWHERE = None


def call(kernel, outs, scratch=(), ins=None, sems=0, cost=0, limit=24, aliases=None):
    shapes = [
        jax.ShapeDtypeStruct(o[0], o[2] if len(o) > 2 else F32) if o[1] is None else o[1](o[0], o[2] if len(o) > 2 else F32)
        for o in outs
    ]
    spaces = [pltpu.VMEM(s, F32) for s in scratch]
    if sems:
        spaces.append(pltpu.SemaphoreType.DMA((sems,)))
    run = pl.pallas_call(
        kernel,
        out_shape=shapes,
        in_specs=[pl.BlockSpec(memory_space=m or pltpu.VMEM) for m in ins],
        out_specs=[pl.BlockSpec(memory_space=pltpu.VMEM) for _ in outs],
        scratch_shapes=spaces,
        input_output_aliases=aliases or {},
        compiler_params=pltpu.CompilerParams(vmem_limit_bytes=limit << 20),
        cost_estimate=pl.CostEstimate(flops=cost, bytes_accessed=cost // 400, transcendentals=0),
    )

    def apply(*operands):
        held = [x if m is None else pltpu.with_memory_space_constraint(x, m) for x, m in zip(operands, ins, strict=True)]
        return run(*held)

    return apply


def spread_to(block, axis):
    return lax.all_to_all(block, axis, 0, 0, tiled=True)


def shards(residual, elem_class, basis, eigenvalues, vertex_number, panels):
    field = residual.reshape(512, LANES)
    I32 = jnp.int32
    pay, own, num, cls, top, win, basis2, eigen2, pick, eig, zfwd, zback, rows = call(
        down_kernel,
        [
            ((8, 40, 128), VM), ((24, 128), VM), ((5, 3, 17), VM, I32), ((4, 2, 16), VM, I32), ((TOP, 2943), VM),
            ((1760, 128), VM), ((8, 300), VM), ((8, 30), VM), ((304, 128), VM), ((40, 128), VM),
            ((10, 16, 128), VM), ((10, 16, 128), VM), ((512, 128), VM),
        ],
        [(512, 128), (3, 10, 8, 10), (3, 8, 10), (40, 128), (255 - TOP, 2943)], ins=[pltpu.HBM] * 6, sems=7,
    )(field, vertex_number, panels, elem_class, basis.transpose(1, 2, 0, 3), eigenvalues.transpose(1, 0, 2))
    first = spread_to(pay, "gy")
    right, left, tree, face, four = call(
        share_kernel,
        [((168, 128), VM), ((168, 128), VM), ((64, 1, 256), VM), ((64, 128), VM), ((8, 128), VM)],
        ins=[None, VM, VM],
    )(first, rows, cls)
    from_left = lax.ppermute(right, "gx", [(i, i + 1) for i in range(63)])
    from_right = lax.ppermute(left, "gx", [(i + 1, i) for i in range(63)])
    summed = spread_to(tree, "gx")
    win, fine, rim = call(
        solve_kernel,
        [((1760, 128), VM), ((512, 128), VM), ((64, 128), VM)],
        [
            (10, 10, 16, 128), (10, 16, 128), (2, 8, 8, 128), (512, 128), (512, 128),
            (112, 128), (1760, 128), (304, 128), (40, 128), (10, 16, 128), (10, 16, 128),
            (56, 128), (8, 128), (5, 10, 16, 128), (10, 16, 128), (10, 16, 128), (10, 16, 128), (64, 128),
        ],
        ins=[VM] * 8 + [None, None], cost=8_000_000_000, aliases={0: 0},
    )(win, basis2, eigen2, pick, eig, zfwd, zback, face, from_left, from_right)
    (pay,) = call(tree_kernel, [((8, 40, 128), VM)], ins=[None, VM, VM, None, None])(summed, rim, four, from_left, from_right)
    second = spread_to(pay, "gy")
    (out,) = call(
        up_kernel, [((512, 128), None)], [(32, 128), (24, 128), (256, 128), (16, 128), (255 - TOP, 2943)],
        ins=[VM, VM, None, pltpu.HBM, VM, VM, VM], sems=2,
    )(four, own, second, panels, num, top, fine)
    return out.reshape(residual.shape)


def solution(mesh):
    return jax.shard_map(
        shards,
        mesh=mesh,
        in_specs=(
            P(None, "gx", "gy", None),
            P("gx", "gy", None),
            P(),
            P(),
            P("gx", "gy", None),
            P("gx", "gy"),
        ),
        out_specs=P(None, "gx", "gy", None),
        check_vma=False,
    )
```

time: 72 us -> 67.3 us (0.935)
  blocking collectives: 14.8 us -> 25.8 us
  Pallas kernels: 20.1 us -> 13.6 us
  starting transfers between devices: 27.5 us -> 21.3 us
  waiting for transfers between devices: 9.08 us -> 6.29 us
    all_to_all x1 -> x2, blocking collectives: 14.8 us -> 25.8 us  [spread_to(): return lax.all_to_all(block, axis, 0, 0, tiled=True)]
    pallas_call x7 -> x5, Pallas kernels: 20.1 us -> 13.6 us  [apply(): return run(*held)]
    all_to_all x2 -> x1, starting transfers between devices: 25 us -> 18.7 us  [spread_to(): return lax.all_to_all(block, axis, 0, 0, tiled=True)]
    all_to_all x2 -> x1, waiting for transfers between devices: 9.07 us -> 6.28 us  [spread_to(): return lax.all_to_all(block, axis, 0, 0, tiled=True)]
  transfers between devices with their start and end apart: 4 -> 3, of which waited for: 2 -> 1; matrix products, arithmetic and copies ran while one was open for 0% -> 0% of each run, Pallas kernels for 18% -> 11%
where the time goes in v2:
time: 67.3 us; the launch traced here: 67 us
  blocking collectives  25.8 us (38%)
  starting transfers between devices  21.3 us (32%)
  Pallas kernels  13.6 us (20%)
  waiting for transfers between devices  6.29 us (9%)
    all_to_all x2, blocking collectives, spread_to(): return lax.all_to_all(block, axis, 0, 0, tiled=True)  25.8 us
    all_to_all x1, starting transfers between devices, spread_to(): return lax.all_to_all(block, axis, 0, 0, tiled=True)  18.7 us
    pallas_call x5, Pallas kernels, apply(): return run(*held)  13.6 us
    all_to_all x1, waiting for transfers between devices, spread_to(): return lax.all_to_all(block, axis, 0, 0, tiled=True)  6.28 us
  transfers between devices with their start and end apart: 3, of which 1 were waited for; matrix products, arithmetic and copies ran while one was open for 0% of the time, Pallas kernels for 11%

profile of v2, /device:TPU:1, one launch (start us, length us, event | category | flops | bytes accessed | tf_op | source)
XLA Modules:
  0.0 67.0 jit_solution(14458139472232433192)
XLA Ops:
  0.0 2.9 %shard_map.64 = (f32[8,40,128]{2,1,0:T(8,128)S(1)}, f32[24,128]{1,0:T(8,128)S(1)}, s32[5,3,17]{2,1,0:T(4,128)S(1)}, s32[4,2,16]{2,1,0:T(2,128)S(1)}, f32[128,294...) custom-call(f32[512,128]{1,0:T(8,128)} %bitcast.4, ...), custom_call_target="tpu_custom_call" | custom-call | tf_op jit(solution)/shard_map/pallas_call | solution.py:545
  2.9 14.8 %all_to_all.15.got_ref = f32[8,40,128]{2,1,0:T(8,128)S(1)} all-to-all(f32[8,40,128]{2,1,0:T(8,128)S(1)} %get-tuple-element.25), channel_id=1, replica_groups=mesh['gx'=64,'gy'=8] {'gy'}, dimensions={0} | all-to-all | bytes 327680 | tf_op jit(solution)/shard_map/all_to_all | solution.py:551
  17.8 0.7 shard_map.65
  18.4 1.3 %collective-permute-start = (f32[168,128]{1,0:T(8,128)S(1)}, f32[168,128]{1,0:T(8,128)S(1)}, u32[]{:S(2)}, u32[]{:S(2)}) collective-permute-start(f32[168,128]{1,0:T(8,128)S(1)} %get-tuple-element.39), channel_id=1, source_target_pairs={{0,8},{8,16},{16,24},{24,32},{32,40},{40,48},{48,56},{56,64},{64,7... | collective-permute-start | bytes 258056 | tf_op jit(solution)/shard_map/ppermute | solution.py:572
  19.7 1.3 %collective-permute-start.1 = (f32[168,128]{1,0:T(8,128)S(1)}, f32[168,128]{1,0:T(8,128)S(1)}, u32[]{:S(2)}, u32[]{:S(2)}) collective-permute-start(f32[168,128]{1,0:T(8,128)S(1)} %get-tuple-element.40), channel_id=1, source_target_pairs={{8,0},{16,8},{24,16},{32,24},{40,32},{48,40},{56,48},{64,56},{72,6... | collective-permute-start | bytes 258056 | tf_op jit(solution)/shard_map/ppermute | solution.py:573
  21.0 18.7 %all-to-all-start.1 = ((f32[64,1,256]{2,1,0:T(1,128)}), f32[64,1,256]{2,1,0:T(1,128)S(1)}, u32[]{:S(2)}, u32[]{:S(2)}) async-start(f32[64,1,256]{2,1,0:T(1,128)} %get-tuple-element.30), calls=%async_computation.1 | async-start | bytes 131072 | tf_op jit(solution)/shard_map/all_to_all | solution.py:551
  39.7 0.0 collective-permute-done.from_left
  39.7 0.0 collective-permute-done.1.from_right
  39.7 7.2 %shard_map.66 = (f32[1760,128]{1,0:T(8,128)S(1)}, f32[512,128]{1,0:T(8,128)S(1)}, f32[64,128]{1,0:T(8,128)S(1)}) custom-call(f32[1760,128]{1,0:T(8,128)S(1)} %get-tuple-element.31.win_in, f32[8,300]{1,0:T(8,128)S(1)} %get-tuple-element.32.table_ref, f32[8,30]{1,0:T(8,128)S(1)} %get-tuple-element.33.eigen_ref, ...), custom_call_target="tpu_custom_call", output_to_operand_aliasing={{0}: (0, {})} | custom-call | flops 8000000000 | bytes 20000000 | tf_op jit(solution)/shard_map/pallas_call | solution.py:545
  47.0 6.3 %all-to-all-done.1.got_ref = f32[64,1,256]{2,1,0:T(1,128)S(1)} async-done(((f32[64,1,256]{2,1,0:T(1,128)}), f32[64,1,256]{2,1,0:T(1,128)S(1)}, u32[]{:S(2)}, u32[]{:S(2)}) %all-to-all-start.1) | async-done | bytes 65568 | tf_op jit(solution)/shard_map/all_to_all | solution.py:551
  53.2 0.2 shard_map.67
  53.4 10.9 %all_to_all.16.got_ref = f32[8,40,128]{2,1,0:T(8,128)S(1)} all-to-all(f32[8,40,128]{2,1,0:T(8,128)S(1)} %shard_map.67), channel_id=1, replica_groups=mesh['gx'=64,'gy'=8] {'gy'}, dimensions={0} | all-to-all | bytes 327680 | tf_op jit(solution)/shard_map/all_to_all | solution.py:551
  64.4 2.7 %shard_map.68 = f32[512,128]{1,0:T(8,128)} custom-call(f32[8,128]{1,0:T(8,128)S(1)} %get-tuple-element.28.four_ref, f32[24,128]{1,0:T(8,128)S(1)} %get-tuple-element.29.own_ref, f32[8,40,128]{2,1,0:T(8,128)S(1)} %all_to_all.16.got_ref, f32[255,2943]{1,0:T(8,128)} %pan_hbm.3, s32[5,3,17]{2,1,0:T(4,128)S(1)} %get-tuple-element.42.num_ref, ...), custom_call_target="tpu_custom_call" | custom-call | tf_op jit(solution)/shard_map/pallas_call | solution.py:545
Async XLA Ops:
  18.4 21.3 %collective-permute-start = (f32[168,128]{1,0:T(8,128)S(1)}, f32[168,128]{1,0:T(8,128)S(1)}, u32[]{:S(2)}, u32[]{:S(2)}) collective-permute-start(f32[168,128]{1,0:T(8,128)S(1)} %get-tuple-element.39), channel_id=1, source_target_pairs={{0,8},{8,16},{16,24},{24,32},{32,40},{40,48},{48,56},{56,64},{64,7... | collective-permute-start | bytes 258056 | tf_op jit(solution)/shard_map/ppermute | solution.py:572
  19.7 20.0 %collective-permute-start.1 = (f32[168,128]{1,0:T(8,128)S(1)}, f32[168,128]{1,0:T(8,128)S(1)}, u32[]{:S(2)}, u32[]{:S(2)}) collective-permute-start(f32[168,128]{1,0:T(8,128)S(1)} %get-tuple-element.40), channel_id=1, source_target_pairs={{8,0},{16,8},{24,16},{32,24},{40,32},{48,40},{56,48},{64,56},{72,6... | collective-permute-start | bytes 258056 | tf_op jit(solution)/shard_map/ppermute | solution.py:573
  21.0 32.2 %all-to-all-start.1 = ((f32[64,1,256]{2,1,0:T(1,128)}), f32[64,1,256]{2,1,0:T(1,128)S(1)}, u32[]{:S(2)}, u32[]{:S(2)}) async-start(f32[64,1,256]{2,1,0:T(1,128)} %get-tuple-element.30), calls=%async_computation.1 | async-start | bytes 131072 | tf_op jit(solution)/shard_map/all_to_all | solution.py:551

commit v3 on v2

--- a/solution.py
+++ b/solution.py
@@ -46,8 +46,8 @@
 
 def down_kernel(
     res_hbm, num_hbm, pan_hbm, cls_hbm, basis_hbm, value_hbm,
-    pay_ref, own_ref, num_ref, cls_ref, top_ref, win, table_ref, eigen_ref, pick, eig, zfwd, zback, rows_ref,
-    res_ref, basis_ref, value_ref, line_ref, low_ref, sems,
+    pay_ref, own_ref, num_ref, cls_ref, top_ref, res_ref, basis_ref, value_ref,
+    line_ref, low_ref, sems,
 ):
     q = lax.axis_index("gy")
     pairs = [
@@ -76,23 +76,7 @@
             spread = spread + jnp.where(num_ref[i, j : j + 1, :] == rows, vertex[k : k + 1, :], 0.0)
     ordered = jnp.broadcast_to(jnp.sum(spread, axis=1, keepdims=True), (256, LANES))
 
-    rows_ref[...] = split_z(res_ref[...])
-    for copy in copies[2:5]:
-        copy.wait()
-    for d in range(3):
-        eigen_ref[:, 10 * d : 10 * d + 10] = value_ref[d]
-        for i in range(10):
-            low = 100 * d + 10 * i
-            table_ref[:, low : low + 10] = basis_ref[d, i]
-    kind = jnp.concatenate([cls_ref[ix].astype(F32) + 1.0 for ix in range(4)], axis=0)
-    pick_tables(kind, table_ref, eigen_ref, pick, eig, zfwd, zback)
-    columns = range(8)
-    groups = [[rows_ref[128 * (r // 2) + 16 * i + 8 * (r % 2) : 128 * (r // 2) + 16 * i + 8 * (r % 2) + 8, :] for r in range(8)] for i in columns]
-    for i, parts in zip(columns, with_outer(exchange(groups)), strict=True):
-        for k, part in enumerate(parts):
-            win[pl.ds((i * 11 + 12) * 16 + k, 8, stride=16), :] = part
-
-    for copy in copies[5:]:
+    for copy in copies[2:]:
         copy.wait()
     for c, (cut, width) in enumerate(CUTS):
         piece = jnp.sum(top_ref[:, cut] * ordered[:TOP, :width], axis=0, keepdims=True)
@@ -107,10 +91,8 @@
         pay_ref[peer, 37:40, :] = own_ref[5:8, :] if peer == 7 else jnp.zeros((3, LANES), F32)
 
 
-def share_kernel(got_ref, rows_ref, cls_ref, right_ref, left_ref, tree_ref, face_ref, four_ref):
+def sum_kernel(got_ref, tree_ref, four_ref):
     q = lax.axis_index("gy")
-    face_ref[0:32, :] = jnp.where(q > 0, got_ref[jnp.maximum(q - 1, 0), 0:32, :], 0.0)
-    face_ref[32:64, :] = jnp.where(q < 7, got_ref[jnp.minimum(q + 1, 7), 0:32, :], 0.0)
     total = got_ref[0, 35:40, :]
     for peer in range(1, 8):
         total = total + got_ref[peer, 35:40, :]
@@ -122,16 +104,22 @@
             inside = (peer >> level) == (q >> level)
             low = low + jnp.where(inside, got_ref[peer, 31 + level : 32 + level, :], 0.0)
         four_ref[2 + level : 3 + level, :] = low
+    line = jnp.concatenate([total[0:1], total[1:2]], axis=1)
+    for t in range(64):
+        tree_ref[t] = line
+
+
+def pack_kernel(got_ref, res_ref, cls_ref, four_ref, right_ref, left_ref, face_ref):
+    q = lax.axis_index("gy")
+    face_ref[0:32, :] = jnp.where(q > 0, got_ref[jnp.maximum(q - 1, 0), 0:32, :], 0.0)
+    face_ref[32:64, :] = jnp.where(q < 7, got_ref[jnp.minimum(q + 1, 7), 0:32, :], 0.0)
     for ref, column, first in ((right_ref, 3, 23), (left_ref, 0, 0)):
-        ref[0:144, :] = rows_ref[16 * first : 16 * first + 144, :]
+        ref[0:144, :] = res_ref[16 * first : 16 * first + 144, :]
         ref[144:153, :] = face_ref[first : first + 9, :]
         ref[153:162, :] = face_ref[32 + first : 41 + first, :]
         ref[162:168, :] = jnp.zeros((6, LANES), F32)
         ref[162:164, 0:16] = (cls_ref[column] + 1).astype(F32)
-        ref[164:167, :] = total[2:5]
-    line = jnp.concatenate([total[0:1], total[1:2]], axis=1)
-    for t in range(64):
-        tree_ref[t] = line
+        ref[164:167, :] = four_ref[0:3, :]
 
 
 def grids():
@@ -224,10 +212,33 @@
         zback[c, 9:10, :] = pick[290 + c : 291 + c, :]
 
 
+def tile_kernel(
+    res_ref, cls_ref, basis_ref, value_ref,
+    win, table_ref, eigen_ref, pick, eig, zfwd, zback,
+    rows_ref,
+):
+    rows_ref[...] = split_z(res_ref[...])
+    for d in range(3):
+        eigen_ref[:, 10 * d : 10 * d + 10] = value_ref[d]
+        for i in range(10):
+            low = 100 * d + 10 * i
+            table_ref[:, low : low + 10] = basis_ref[d, i]
+    kind = jnp.concatenate([cls_ref[ix].astype(F32) + 1.0 for ix in range(4)], axis=0)
+    pick_tables(kind, table_ref, eigen_ref, pick, eig, zfwd, zback)
+    columns = range(8)
+    groups = [
+        [rows_ref[128 * (r // 2) + 16 * i + 8 * (r % 2) : 128 * (r // 2) + 16 * i + 8 * (r % 2) + 8, :] for r in range(8)]
+        for i in columns
+    ]
+    for i, parts in zip(columns, with_outer(exchange(groups)), strict=True):
+        for k, part in enumerate(parts):
+            win[pl.ds((i * 11 + 12) * 16 + k, 8, stride=16), :] = part
+
+
 def solve_kernel(
     win_in, table_ref, eigen_ref, pick_m, eig_m, zfwd_m, zback_m, face_ref, from_left, from_right,
     win_m, fine_ref, rim_ref,
-    work, edge, ends, tiles, rows_ref, rows_f, win_e, pick_e, eig_e, zfwd_e, zback_e, half_e, lxe, work_e, tmp_a, tmp_b, tmp_c, rim_rows,
+    work, edge, ends, tiles, rows_ref, rows_f, rows_e, win_e, pick_e, eig_e, zfwd_e, zback_e, half_e, lxe, work_e, tmp_a, tmp_b, tmp_c, rim_rows,
 ):
     del win_in
     sub, lane, kz = grids()
@@ -238,6 +249,9 @@
     rows_f[64:88, :] = from_left[144:168, :]
     rows_f[88:112, :] = from_right[144:168, :]
     rows_f[...] = split_z(rows_f[...])
+    rows_e[0:144, :] = from_left[0:144, :]
+    rows_e[144:288, :] = from_right[0:144, :]
+    rows_e[...] = split_z(rows_e[...])
     outer = [rows_f[32 * (r % 2) + 8 * (r // 2) : 32 * (r % 2) + 8 * (r // 2) + 8, :] for r in range(8)]
     beside = [rows_f[first : first + 8, :] for first in (65, 74, 88, 97)]
     corner = [jnp.broadcast_to(rows_f[n : n + 1, :], (8, LANES)) for n in (64, 73, 96, 105)]
@@ -252,8 +266,8 @@
         groups = []
         for i in columns:
             layer = jnp.where(i == 8, 0, i + 1)
-            parts = [from_left[pl.ds(pl.multiple_of(16 * layer + 8 * jy, 8), 8), :] for jy in range(2)]
-            parts += [from_right[pl.ds(pl.multiple_of(16 * i + 8 * jy, 8), 8), :] for jy in range(2)]
+            parts = [rows_e[pl.ds(pl.multiple_of(16 * layer + 8 * jy, 8), 8), :] for jy in range(2)]
+            parts += [rows_e[pl.ds(pl.multiple_of(144 + 16 * i + 8 * jy, 8), 8), :] for jy in range(2)]
             groups.append(parts + parts)
         for i, parts in zip(columns, with_outer(exchange(groups)), strict=True):
             for k, part in enumerate(parts):
@@ -554,33 +568,39 @@
 def shards(residual, elem_class, basis, eigenvalues, vertex_number, panels):
     field = residual.reshape(512, LANES)
     I32 = jnp.int32
-    pay, own, num, cls, top, win, basis2, eigen2, pick, eig, zfwd, zback, rows = call(
+    pay, own, num, cls, top, res, table, eigen = call(
         down_kernel,
         [
             ((8, 40, 128), VM), ((24, 128), VM), ((5, 3, 17), VM, I32), ((4, 2, 16), VM, I32), ((TOP, 2943), VM),
-            ((1760, 128), VM), ((8, 300), VM), ((8, 30), VM), ((304, 128), VM), ((40, 128), VM),
-            ((10, 16, 128), VM), ((10, 16, 128), VM), ((512, 128), VM),
+            ((512, 128), VM), ((3, 10, 8, 10), VM), ((3, 8, 10), VM),
         ],
-        [(512, 128), (3, 10, 8, 10), (3, 8, 10), (40, 128), (255 - TOP, 2943)], ins=[pltpu.HBM] * 6, sems=7,
+        [(40, 128), (255 - TOP, 2943)], ins=[pltpu.HBM] * 6, sems=7,
     )(field, vertex_number, panels, elem_class, basis.transpose(1, 2, 0, 3), eigenvalues.transpose(1, 0, 2))
     first = spread_to(pay, "gy")
-    right, left, tree, face, four = call(
-        share_kernel,
-        [((168, 128), VM), ((168, 128), VM), ((64, 1, 256), VM), ((64, 128), VM), ((8, 128), VM)],
-        ins=[None, VM, VM],
-    )(first, rows, cls)
+    tree, four = call(sum_kernel, [((64, 1, 256), VM), ((8, 128), VM)], ins=[None])(first)
+    summed = spread_to(tree, "gx")
+    right, left, face = call(
+        pack_kernel, [((168, 128), VM), ((168, 128), VM), ((64, 128), VM)], ins=[None, VM, VM, VM], cost=2_000_000_000
+    )(first, res, cls, four)
     from_left = lax.ppermute(right, "gx", [(i, i + 1) for i in range(63)])
     from_right = lax.ppermute(left, "gx", [(i + 1, i) for i in range(63)])
-    summed = spread_to(tree, "gx")
+    win, basis2, eigen2, pick, eig, zfwd, zback = call(
+        tile_kernel,
+        [
+            ((1760, 128), VM), ((8, 300), VM), ((8, 30), VM), ((304, 128), VM), ((40, 128), VM),
+            ((10, 16, 128), VM), ((10, 16, 128), VM),
+        ],
+        [(512, 128)], ins=[VM] * 4, cost=2_000_000_000,
+    )(res, cls, table, eigen)
     win, fine, rim = call(
         solve_kernel,
         [((1760, 128), VM), ((512, 128), VM), ((64, 128), VM)],
         [
             (10, 10, 16, 128), (10, 16, 128), (2, 8, 8, 128), (512, 128), (512, 128),
-            (112, 128), (1760, 128), (304, 128), (40, 128), (10, 16, 128), (10, 16, 128),
+            (112, 128), (288, 128), (1760, 128), (304, 128), (40, 128), (10, 16, 128), (10, 16, 128),
             (56, 128), (8, 128), (5, 10, 16, 128), (10, 16, 128), (10, 16, 128), (10, 16, 128), (64, 128),
         ],
-        ins=[VM] * 8 + [None, None], cost=8_000_000_000, aliases={0: 0},
+        ins=[VM] * 8 + [None, None], cost=1_000_000_000, aliases={0: 0},
     )(win, basis2, eigen2, pick, eig, zfwd, zback, face, from_left, from_right)
     (pay,) = call(tree_kernel, [((8, 40, 128), VM)], ins=[None, VM, VM, None, None])(summed, rim, four, from_left, from_right)
     second = spread_to(pay, "gy")

time: 67.3 us -> 62.8 us (0.933)
  waiting for transfers between devices: 6.29 us -> 3.92 us
  starting transfers between devices: 21.3 us -> 19 us
  blocking collectives: 25.8 us -> 25.1 us
    all_to_all x1, waiting for transfers between devices: 6.28 us -> 0.01 us  [spread_to(): return lax.all_to_all(block, axis, 0, 0, tiled=True)]
    all_to_all x1, starting transfers between devices: 18.7 us -> 14.8 us  [spread_to(): return lax.all_to_all(block, axis, 0, 0, tiled=True)]
    ppermute x1, waiting for transfers between devices: 0.01 us -> 3.91 us  [shards(): from_right = lax.ppermute(left, 'gx', [(i + 1, i) for i in range(63)])]
    ppermute x1, starting transfers between devices: 1.28 us -> 2.92 us  [shards(): from_left = lax.ppermute(right, 'gx', [(i, i + 1) for i in range(63)])]
    pallas_call x5 -> x7, Pallas kernels: 13.6 us -> 13.9 us  [apply(): return run(*held)]
  transfers between devices with their start and end apart: 3 -> 3, of which waited for: 1 -> 1; matrix products, arithmetic and copies ran while one was open for 0% -> 0% of each run, Pallas kernels for 11% -> 13%
where the time goes in v3:
time: 62.8 us; the launch traced here: 62 us
  blocking collectives  25.1 us (40%)
  starting transfers between devices  19 us (30%)
  Pallas kernels  13.9 us (22%)
  waiting for transfers between devices  3.92 us (6%)
    all_to_all x2, blocking collectives, spread_to(): return lax.all_to_all(block, axis, 0, 0, tiled=True)  25.1 us
    all_to_all x1, starting transfers between devices, spread_to(): return lax.all_to_all(block, axis, 0, 0, tiled=True)  14.8 us
    pallas_call x7, Pallas kernels, apply(): return run(*held)  13.9 us
    ppermute x1, waiting for transfers between devices, shards(): from_right = lax.ppermute(left, 'gx', [(i + 1, i) for i in range(63)])  3.91 us
    ppermute x1, starting transfers between devices, shards(): from_left = lax.ppermute(right, 'gx', [(i, i + 1) for i in range(63)])  2.92 us
    ppermute x1, starting transfers between devices, shards(): from_right = lax.ppermute(left, 'gx', [(i + 1, i) for i in range(63)])  1.29 us
  transfers between devices with their start and end apart: 3, of which 1 were waited for; matrix products, arithmetic and copies ran while one was open for 0% of the time, Pallas kernels for 13%

profile of v3, /device:TPU:1, one launch (start us, length us, event | category | flops | bytes accessed | tf_op | source)
XLA Modules:
  0.0 62.0 jit_solution(6489493137852200397)
XLA Ops:
  0.0 2.4 %shard_map.64 = (f32[8,40,128]{2,1,0:T(8,128)S(1)}, f32[24,128]{1,0:T(8,128)S(1)}, s32[5,3,17]{2,1,0:T(4,128)S(1)}, s32[4,2,16]{2,1,0:T(2,128)S(1)}, f32[128,294...) custom-call(f32[512,128]{1,0:T(8,128)} %bitcast.4, ...), custom_call_target="tpu_custom_call" | custom-call | tf_op jit(solution)/shard_map/pallas_call | solution.py:559
  2.4 14.8 %all_to_all.15.got_ref = f32[8,40,128]{2,1,0:T(8,128)S(1)} all-to-all(f32[8,40,128]{2,1,0:T(8,128)S(1)} %get-tuple-element.27), channel_id=1, replica_groups=mesh['gx'=64,'gy'=8] {'gy'}, dimensions={0} | all-to-all | bytes 327680 | tf_op jit(solution)/shard_map/all_to_all | solution.py:565
  17.3 0.7 %shard_map.65 = (f32[64,1,256]{2,1,0:T(1,128)}, f32[8,128]{1,0:T(8,128)S(1)}) custom-call(f32[8,40,128]{2,1,0:T(8,128)S(1)} %all_to_all.15.got_ref), custom_call_target="tpu_custom_call" | custom-call | tf_op jit(solution)/shard_map/pallas_call | solution.py:559
  18.0 14.8 %all-to-all-start.1 = ((f32[64,1,256]{2,1,0:T(1,128)}), f32[64,1,256]{2,1,0:T(1,128)S(1)}, u32[]{:S(2)}, u32[]{:S(2)}) async-start(f32[64,1,256]{2,1,0:T(1,128)} %get-tuple-element.30), calls=%async_computation.1 | async-start | bytes 131072 | tf_op jit(solution)/shard_map/all_to_all | solution.py:565
  32.8 2.9 %collective-permute-start = (f32[168,128]{1,0:T(8,128)S(1)}, f32[168,128]{1,0:T(8,128)S(1)}, u32[]{:S(2)}, u32[]{:S(2)}) collective-permute-start(f32[168,128]{1,0:T(8,128)S(1)} %get-tuple-element.43), channel_id=1, source_target_pairs={{0,8},{8,16},{16,24},{24,32},{32,40},{40,48},{48,56},{56,64},{64,7... | collective-permute-start | bytes 258056 | tf_op jit(solution)/shard_map/ppermute | solution.py:585
  35.7 1.3 %collective-permute-start.1 = (f32[168,128]{1,0:T(8,128)S(1)}, f32[168,128]{1,0:T(8,128)S(1)}, u32[]{:S(2)}, u32[]{:S(2)}) collective-permute-start(f32[168,128]{1,0:T(8,128)S(1)} %get-tuple-element.44), channel_id=1, source_target_pairs={{8,0},{16,8},{24,16},{32,24},{40,32},{48,40},{56,48},{64,56},{72,6... | collective-permute-start | bytes 258056 | tf_op jit(solution)/shard_map/ppermute | solution.py:586
  37.0 0.7 %shard_map.66 = (f32[1760,128]{1,0:T(8,128)S(1)}, f32[8,300]{1,0:T(8,128)S(1)}, f32[8,30]{1,0:T(8,128)S(1)}, f32[304,128]{1,0:T(8,128)S(1)}, f32[40,128]{1,0:T(8...) custom-call(f32[512,128]{1,0:T(8,128)S(1)} %get-tuple-element.31.res_ref, ...), custom_call_target="tpu_custom_call" | custom-call | flops 2000000000 | bytes 5000000 | tf_op jit(solution)/shard_map/pallas_call | solution.py:559
  37.7 0.0 collective-permute-done.from_left
  37.7 3.9 %collective-permute-done.1.from_right = f32[168,128]{1,0:T(8,128)S(1)} collective-permute-done((f32[168,128]{1,0:T(8,128)S(1)}, f32[168,128]{1,0:T(8,128)S(1)}, u32[]{:S(2)}, u32[]{:S(2)}) %collective-permute-start.1) | collective-permute-done | bytes 86048 | tf_op jit(solution)/shard_map/ppermute | solution.py:586
  41.6 7.2 %shard_map.68 = (f32[1760,128]{1,0:T(8,128)S(1)}, f32[512,128]{1,0:T(8,128)S(1)}, f32[64,128]{1,0:T(8,128)S(1)}) custom-call(f32[1760,128]{1,0:T(8,128)S(1)} %get-tuple-element.35.win_in, f32[8,300]{1,0:T(8,128)S(1)} %get-tuple-element.36.table_ref, f32[8,30]{1,0:T(8,128)S(1)} %get-tuple-element.37.eigen_ref, ...), custom_call_target="tpu_custom_call", output_to_operand_aliasing={{0}: (0, {})} | custom-call | flops 1000000000 | bytes 2500000 | tf_op jit(solution)/shard_map/pallas_call | solution.py:559
  48.9 0.0 all-to-all-done.1.got_ref
  48.9 0.2 shard_map.69
  49.1 10.3 %all_to_all.16.got_ref = f32[8,40,128]{2,1,0:T(8,128)S(1)} all-to-all(f32[8,40,128]{2,1,0:T(8,128)S(1)} %shard_map.69), channel_id=1, replica_groups=mesh['gx'=64,'gy'=8] {'gy'}, dimensions={0} | all-to-all | bytes 327680 | tf_op jit(solution)/shard_map/all_to_all | solution.py:565
  59.3 2.7 %shard_map.70 = f32[512,128]{1,0:T(8,128)} custom-call(f32[8,128]{1,0:T(8,128)S(1)} %get-tuple-element.28.four_ref, f32[24,128]{1,0:T(8,128)S(1)} %get-tuple-element.29.own_ref, f32[8,40,128]{2,1,0:T(8,128)S(1)} %all_to_all.16.got_ref, f32[255,2943]{1,0:T(8,128)} %pan_hbm.3, s32[5,3,17]{2,1,0:T(4,128)S(1)} %get-tuple-element.46.num_ref, ...), custom_call_target="tpu_custom_call" | custom-call | tf_op jit(solution)/shard_map/pallas_call | solution.py:559
  (1 shorter events, 0.0 us)
Async XLA Ops:
  18.0 30.9 %all-to-all-start.1 = ((f32[64,1,256]{2,1,0:T(1,128)}), f32[64,1,256]{2,1,0:T(1,128)S(1)}, u32[]{:S(2)}, u32[]{:S(2)}) async-start(f32[64,1,256]{2,1,0:T(1,128)} %get-tuple-element.30), calls=%async_computation.1 | async-start | bytes 131072 | tf_op jit(solution)/shard_map/all_to_all | solution.py:565
  32.8 4.9 %collective-permute-start = (f32[168,128]{1,0:T(8,128)S(1)}, f32[168,128]{1,0:T(8,128)S(1)}, u32[]{:S(2)}, u32[]{:S(2)}) collective-permute-start(f32[168,128]{1,0:T(8,128)S(1)} %get-tuple-element.43), channel_id=1, source_target_pairs={{0,8},{8,16},{16,24},{24,32},{32,40},{40,48},{48,56},{56,64},{64,7... | collective-permute-start | bytes 258056 | tf_op jit(solution)/shard_map/ppermute | solution.py:585
  35.7 5.9 %collective-permute-start.1 = (f32[168,128]{1,0:T(8,128)S(1)}, f32[168,128]{1,0:T(8,128)S(1)}, u32[]{:S(2)}, u32[]{:S(2)}) collective-permute-start(f32[168,128]{1,0:T(8,128)S(1)} %get-tuple-element.44), channel_id=1, source_target_pairs={{8,0},{16,8},{24,16},{32,24},{40,32},{48,40},{56,48},{64,56},{72,6... | collective-permute-start | bytes 258056 | tf_op jit(solution)/shard_map/ppermute | solution.py:586

commit v4 on v3

--- a/solution.py
+++ b/solution.py
@@ -11,7 +11,7 @@
 NEXT = 10
 NCLASS = 8
 LANES = 128
-TOP = 128
+TOP = 208
 CUTS = [(slice(low, min(low + 128, 2943)), min(128, 2943 - low)) for low in range(0, 2943, 128)]
 HALO = NPR + 1
 F32 = jnp.float32
@@ -46,8 +46,8 @@
 
 def down_kernel(
     res_hbm, num_hbm, pan_hbm, cls_hbm, basis_hbm, value_hbm,
-    pay_ref, own_ref, num_ref, cls_ref, top_ref, res_ref, basis_ref, value_ref,
-    line_ref, low_ref, sems,
+    pay_ref, own_ref, cls_ref, top_ref, res_ref, table_ref, eigen_ref,
+    line_ref, basis_ref, value_ref, low_ref, num_ref, sems,
 ):
     q = lax.axis_index("gy")
     pairs = [
@@ -76,7 +76,14 @@
             spread = spread + jnp.where(num_ref[i, j : j + 1, :] == rows, vertex[k : k + 1, :], 0.0)
     ordered = jnp.broadcast_to(jnp.sum(spread, axis=1, keepdims=True), (256, LANES))
 
-    for copy in copies[2:]:
+    for copy in copies[2:5]:
+        copy.wait()
+    for d in range(3):
+        eigen_ref[:, 10 * d : 10 * d + 10] = value_ref[d]
+        for i in range(10):
+            low = 100 * d + 10 * i
+            table_ref[:, low : low + 10] = basis_ref[d, i]
+    for copy in copies[5:]:
         copy.wait()
     for c, (cut, width) in enumerate(CUTS):
         piece = jnp.sum(top_ref[:, cut] * ordered[:TOP, :width], axis=0, keepdims=True)
@@ -91,13 +98,13 @@
         pay_ref[peer, 37:40, :] = own_ref[5:8, :] if peer == 7 else jnp.zeros((3, LANES), F32)
 
 
-def sum_kernel(got_ref, tree_ref, four_ref):
+def sum_kernel(got_ref, own_ref, tree_ref, four_ref):
     q = lax.axis_index("gy")
     total = got_ref[0, 35:40, :]
     for peer in range(1, 8):
         total = total + got_ref[peer, 35:40, :]
-    four_ref[...] = jnp.zeros((8, LANES), F32)
     four_ref[0:3, :] = total[2:5]
+    four_ref[6:8, :] = own_ref[0:2, :]
     for level in range(1, 4):
         low = jnp.zeros((1, LANES), F32)
         for peer in range(8):
@@ -190,21 +197,37 @@
     return total
 
 
-def pick_tables(kind, table_ref, eigen_ref, pick, eig, zfwd, zback):
+def chosen(table, onehot):
+    high = table.astype(jnp.bfloat16)
+    rest = table - high.astype(F32)
+    middle = rest.astype(jnp.bfloat16)
+    low = (rest - middle.astype(F32)).astype(jnp.bfloat16)
+    dims = (((0,), (0,)), ((), ()))
+    total = lax.dot_general(low, onehot, dims, preferred_element_type=F32)
+    total = total + lax.dot_general(middle, onehot, dims, preferred_element_type=F32)
+    return total + lax.dot_general(high, onehot, dims, preferred_element_type=F32)
+
+
+def pick_tables(kind, table_ref, eigen_ref, pick, eig):
     group = iota((8, LANES), 0)
     lane = iota((8, LANES), 1)
     spread = (iota((16, LANES), 0) == (iota((16, LANES), 1) & 15)).astype(F32)
     laid = jnp.dot(kind, spread, precision=exact)
     laid = jnp.sum(jnp.where(group == (lane >> 4), laid, 0.0), axis=0, keepdims=True)
-    onehot = (laid == (group + 1).astype(F32)).astype(F32)
-    dims = (((0,), (0,)), ((), ()))
-    pick[0:300, :] = lax.dot_general(table_ref[:, 0:300], onehot, dims, precision=exact, preferred_element_type=F32)
-    eig[0:30, :] = lax.dot_general(eigen_ref[:, 0:30], onehot, dims, precision=exact, preferred_element_type=F32)
+    onehot = (laid == (group + 1).astype(F32)).astype(jnp.bfloat16)
+    pick[0:300, :] = chosen(table_ref[:, 0:300], onehot)
+    eig[0:30, :] = chosen(eigen_ref[:, 0:30], onehot)
     eig[20:30, :] = eig[20:30, :] + jnp.where(laid == 0.0, 1.0, 0.0)
     eig[30:40, :] = jnp.ones((10, LANES), F32)
+
+
+def forward_z(pick, zfwd):
     for n, k in enumerate(ORDER):
         zfwd[n, 0:10, :] = pick[200 + 10 * k : 210 + 10 * k, :]
         zfwd[n, 10:16, :] = jnp.zeros((6, LANES), F32)
+
+
+def backward_z(pick, zback):
     for c in range(10):
         zback[c, 0:8, :] = pick[pl.ds(210 + c, 8, stride=10), :]
         zback[c, 8:16, :] = jnp.zeros((8, LANES), F32)
@@ -212,52 +235,117 @@
         zback[c, 9:10, :] = pick[290 + c : 291 + c, :]
 
 
-def tile_kernel(
-    res_ref, cls_ref, basis_ref, value_ref,
-    win, table_ref, eigen_ref, pick, eig, zfwd, zback,
-    rows_ref,
+def x_forward(win, table, target, count):
+    def step(j, _):
+        column = [win[at(i, j), :] for i in range(10)]
+        for a in range(count):
+            target[a, j] = dot_rows([(row(table, count * i + a), column[i]) for i in range(10)])
+        return 0
+
+    lax.fori_loop(0, 10, step, 0, unroll=2)
+
+
+def through_z(source, zfwd, store):
+    table = [zfwd[k] for k in range(10)]
+    for b in range(10):
+        store(b, dot_rows([(table[k], jnp.broadcast_to(source[b, k : k + 1, :], (16, LANES))) for k in range(10)]))
+
+
+def y_forward(column, pick, target):
+    for b in range(10):
+        target[b] = dot_rows([(row(pick, 100 + 10 * j + b), column[j]) for j in range(10)])
+
+
+def y_back(source, pick, store):
+    column = [source[b] for b in range(10)]
+    for j in range(10):
+        store(j, dot_rows([(row(pick, 100 + 10 * j + b), column[b]) for b in range(10)]))
+
+
+def into(ref, *place):
+    def store(n, value):
+        ref[(*place, n)] = value
+
+    return store
+
+
+def spectral_kernel(
+    res_ref, face_ref, cls_ref, table_ref, eigen_ref,
+    spec, sides, pick, eig, table_out,
+    zfwd, rows_ref, rows_f, win, work, tmp,
 ):
+    wide = iota((16, LANES), 1)
+    upper = (wide & 16) != 0
     rows_ref[...] = split_z(res_ref[...])
-    for d in range(3):
-        eigen_ref[:, 10 * d : 10 * d + 10] = value_ref[d]
-        for i in range(10):
-            low = 100 * d + 10 * i
-            table_ref[:, low : low + 10] = basis_ref[d, i]
+    rows_f[...] = split_z(face_ref[...])
     kind = jnp.concatenate([cls_ref[ix].astype(F32) + 1.0 for ix in range(4)], axis=0)
-    pick_tables(kind, table_ref, eigen_ref, pick, eig, zfwd, zback)
+    table_out[...] = table_ref[...]
+    pick_tables(kind, table_ref, eigen_ref, pick, eig)
+    forward_z(pick, zfwd)
     columns = range(8)
     groups = [
         [rows_ref[128 * (r // 2) + 16 * i + 8 * (r % 2) : 128 * (r // 2) + 16 * i + 8 * (r % 2) + 8, :] for r in range(8)]
         for i in columns
     ]
-    for i, parts in zip(columns, with_outer(exchange(groups)), strict=True):
-        for k, part in enumerate(parts):
+    groups.append([rows_f[32 * (r % 2) + 8 * (r // 2) : 32 * (r % 2) + 8 * (r // 2) + 8, :] for r in range(8)])
+    groups = with_outer(exchange(groups))
+    for k in range(10):
+        win[pl.ds(21 * 16 + k, 8, stride=176), :] = groups[8][k]
+    for i in columns:
+        for k, part in enumerate(groups[i]):
             win[pl.ds((i * 11 + 12) * 16 + k, 8, stride=16), :] = part
+    lines = (1, 2, 3, 4, 5, 6, 7, 8, 10)
+    ahead = [win[at(8, j), :] for j in lines]
+    back = [win[at(1, j), :] for j in lines]
+    for n, j in enumerate(lines):
+        sides[0, j] = back[n]
+        sides[1, j] = ahead[n]
+        win[at(0, j), :] = jnp.where(wide >= 32, pltpu.roll(ahead[n], 32, 1), 0.0)
+        win[at(9, j), :] = jnp.where(wide < 96, pltpu.roll(back[n], 96, 1), 0.0)
+
+    def y_halo(n, _):
+        columns = [5 * n + m for m in range(5)]
+        outer = [win[at(i, 10), :] for i in columns]
+        last = [pltpu.roll(win[at(i, 8), :], 16, 1) for i in columns]
+        first = [pltpu.roll(win[at(i, 1), :], 112, 1) for i in columns]
+        for m, i in enumerate(columns):
+            win[at(i, 0), :] = jnp.where(upper, last[m], outer[m])
+            win[at(i, 9), :] = jnp.where(upper, outer[m], first[m])
+        return 0
+
+    lax.fori_loop(0, 2, y_halo, 0)
+    x_forward(win, pick, work, 10)
+
+    def step(a, _):
+        y_forward([work[a, j] for j in range(10)], pick, tmp)
+        through_z(tmp, zfwd, into(spec, a))
+        return 0
+
+    lax.fori_loop(0, 10, step, 0, unroll=2)
 
 
 def solve_kernel(
-    win_in, table_ref, eigen_ref, pick_m, eig_m, zfwd_m, zback_m, face_ref, from_left, from_right,
-    win_m, fine_ref, rim_ref,
-    work, edge, ends, tiles, rows_ref, rows_f, rows_e, win_e, pick_e, eig_e, zfwd_e, zback_e, half_e, lxe, work_e, tmp_a, tmp_b, tmp_c, rim_rows,
+    spec, sides, table_ref, eigen_ref, pick_m, eig_m, from_left, from_right, pan_hbm,
+    fine_ref, rim_ref, low_ref,
+    work, edge, ends, tiles, rows_ref, rows_f, rows_e, win_e, pick_e, eig_e, zfwd_e, zback_e, zfwd_m, zback_m,
+    half_e, lxe, work_e, tmp_a, tmp_b, tmp_c, rim_rows, late, sems,
 ):
-    del win_in
+    copy = pltpu.make_async_copy(pan_hbm.at[pl.ds(TOP, 255 - TOP), :], low_ref, sems.at[0])
+    copy.start()
     sub, lane, kz = grids()
     wide = iota((16, LANES), 1)
     upper = (wide & 16) != 0
 
-    rows_f[0:64, :] = face_ref[...]
-    rows_f[64:88, :] = from_left[144:168, :]
-    rows_f[88:112, :] = from_right[144:168, :]
-    rows_f[...] = split_z(rows_f[...])
+    rows_f[0:24, :] = from_left[144:168, :]
+    rows_f[24:48, :] = from_right[144:168, :]
+    rows_f[0:48, :] = split_z(rows_f[0:48, :])
     rows_e[0:144, :] = from_left[0:144, :]
     rows_e[144:288, :] = from_right[0:144, :]
     rows_e[...] = split_z(rows_e[...])
-    outer = [rows_f[32 * (r % 2) + 8 * (r // 2) : 32 * (r % 2) + 8 * (r // 2) + 8, :] for r in range(8)]
-    beside = [rows_f[first : first + 8, :] for first in (65, 74, 88, 97)]
-    corner = [jnp.broadcast_to(rows_f[n : n + 1, :], (8, LANES)) for n in (64, 73, 96, 105)]
-    outer, beside, corner = with_outer(exchange([outer, beside + beside, corner + corner]))
+    beside = [rows_f[first : first + 8, :] for first in (1, 10, 24, 33)]
+    corner = [jnp.broadcast_to(rows_f[n : n + 1, :], (8, LANES)) for n in (0, 9, 32, 41)]
+    beside, corner = with_outer(exchange([beside + beside, corner + corner]))
     for k in range(10):
-        win_m[pl.ds(21 * 16 + k, 8, stride=176), :] = outer[k]
         win_e[pl.ds(21 * 16 + k, 8, stride=176), :] = beside[k]
         win_e[109 * 16 + k : 109 * 16 + k + 1, :] = corner[k][0:1]
 
@@ -277,7 +365,10 @@
     lax.fori_loop(0, 1, fill, 0)
 
     near = [from_left[162:164, 0:16], from_right[162:164, 0:16]]
-    pick_tables(jnp.concatenate(near + near, axis=0), table_ref, eigen_ref, pick_e, eig_e, zfwd_e, zback_e)
+    pick_tables(jnp.concatenate(near + near, axis=0), table_ref, eigen_ref, pick_e, eig_e)
+    for pick, zfwd, zback in ((pick_e, zfwd_e, zback_e), (pick_m, zfwd_m, zback_m)):
+        forward_z(pick, zfwd)
+        backward_z(pick, zback)
     low_half = iota((5, LANES), 1) < 64
     for i in range(10):
         half_e[5 * i : 5 * i + 5, :] = jnp.where(low_half, pick_e[10 * i : 10 * i + 5, :], pick_e[10 * i + 5 : 10 * i + 10, :])
@@ -285,102 +376,56 @@
     lxe[0:5, :] = jnp.where(low_half, eig_e[0:5, :], eig_e[5:10, :])
 
     second = (wide & 32) != 0
-
-    def x_halo(lines):
-        ahead = [win_m[at(8, j), :] for j in lines]
-        back = [win_m[at(1, j), :] for j in lines]
-        extra = [win_e[at(9, j), :] for j in lines]
-        near = [win_e[at(8, j), :] for j in lines]
-        far = [win_e[at(1, j), :] for j in lines]
-        for n, j in enumerate(lines):
-            win_m[at(0, j), :] = jnp.where(wide >= 32, pltpu.roll(ahead[n], 32, 1), near[n])
-            win_m[at(9, j), :] = jnp.where(wide < 96, pltpu.roll(back[n], 96, 1), far[n])
-            both = pltpu.roll(jnp.where(wide < 64, back[n], ahead[n]), 64, 1)
-            win_e[at(0, j), :] = jnp.where(second, jnp.where(wide >= 64, ahead[n], both), extra[n])
-            win_e[at(9, j), :] = jnp.where(second, extra[n], jnp.where(wide < 64, back[n], both))
-
-    def x_halos(n, _):
-        x_halo([1 + 8 * n + m for m in range(8)])
-        return 0
-
-    lax.fori_loop(0, 1, x_halos, 0)
-    x_halo([10])
-
-    def y_halo(n, _):
-        columns = [(win, 10 * n + m) for m in range(10) for win in (win_m, win_e)]
-        outer = [win[at(i, 10), :] for win, i in columns]
-        last = [pltpu.roll(win[at(i, 8), :], 16, 1) for win, i in columns]
-        first = [pltpu.roll(win[at(i, 1), :], 112, 1) for win, i in columns]
-        for m, (win, i) in enumerate(columns):
-            win[at(i, 0), :] = jnp.where(upper, last[m], outer[m])
-            win[at(i, 9), :] = jnp.where(upper, outer[m], first[m])
-        return 0
-
-    lax.fori_loop(0, 1, y_halo, 0)
-
-    def x_forward(win, table, target, count):
-        def step(j, _):
-            column = [win[at(i, j), :] for i in range(10)]
-            for a in range(count):
-                target[a, j] = dot_rows([(row(table, count * i + a), column[i]) for i in range(10)])
-            return 0
-        lax.fori_loop(0, 10, step, 0)
-
-    def through_z(source, target, zfwd):
-        table = [zfwd[k] for k in range(10)]
-        for b in range(10):
-            target[b] = dot_rows([(table[k], jnp.broadcast_to(source[b, k : k + 1, :], (16, LANES))) for k in range(10)])
-
-    def y_forward(a, source, pick):
-        column = [source[a, j] for j in range(10)]
-        for b in range(10):
-            tmp_a[b] = dot_rows([(row(pick, 100 + 10 * j + b), column[j]) for j in range(10)])
-
-    def scale(a, eig, lx):
-        level = row(lx, a) + eig[20:36, :]
-        for b in range(10):
-            tmp_b[b] = tmp_b[b] / (level + row(eig, 10 + b))
-
-    def y_back(source, pick, store):
-        column = [source[b] for b in range(10)]
-        for j in range(10):
-            store(j, dot_rows([(row(pick, 100 + 10 * j + b), column[b]) for b in range(10)]))
+    lines = (1, 2, 3, 4, 5, 6, 7, 8, 10)
+    both = [pltpu.roll(jnp.where(wide < 64, sides[0, j], sides[1, j]), 64, 1) for j in lines]
+    for n, j in enumerate(lines):
+        extra = win_e[at(9, j), :]
+        win_e[at(0, j), :] = jnp.where(second, jnp.where(wide >= 64, sides[1, j], both[n]), extra)
+        win_e[at(9, j), :] = jnp.where(second, extra, jnp.where(wide < 64, sides[0, j], both[n]))
+    outer = [win_e[at(i, 10), :] for i in range(10)]
+    last = [pltpu.roll(win_e[at(i, 8), :], 16, 1) for i in range(10)]
+    first = [pltpu.roll(win_e[at(i, 1), :], 112, 1) for i in range(10)]
+    for i in range(10):
+        win_e[at(i, 0), :] = jnp.where(upper, last[i], outer[i])
+        win_e[at(i, 9), :] = jnp.where(upper, outer[i], first[i])
+
+    def scale(level, eig, b):
+        return level + row(eig, 10 + b)
 
     x_forward(win_e, half_e, work_e, 5)
     for b in range(10):
         edge[b] = jnp.zeros((16, LANES), F32)
 
     def edge_step(a, _):
-        y_forward(a, work_e, pick_e)
-        through_z(tmp_a, tmp_b, zfwd_e)
-        scale(a, eig_e, lxe)
+        y_forward([work_e[a, j] for j in range(10)], pick_e, tmp_a)
+        level = row(lxe, a) + eig_e[20:36, :]
         weight = row(half_e, 50 + a)
-        for b in range(10):
-            edge[b] = edge[b] + weight * tmp_b[b]
+
+        def add(b, value):
+            edge[b] = edge[b] + weight * (value / scale(level, eig_e, b))
+
+        through_z(tmp_a, zfwd_e, add)
         return 0
 
     lax.fori_loop(0, 5, edge_step, 0)
     for b in range(10):
         tmp_b[b] = edge[b] + pltpu.roll(edge[b], 64, 1)
-    through_z(tmp_b, tmp_c, zback_e)
-
-    def put_edge(j, value):
-        edge[j] = value
-
-    y_back(tmp_c, pick_e, put_edge)
-
-    x_forward(win_m, pick_m, work, 10)
+    through_z(tmp_b, zback_e, into(tmp_c))
+    y_back(tmp_c, pick_e, into(edge))
+
+    inner = (wide >= 32) & (wide < 96)
+    beyond = [jnp.where(inner, 0.0, jnp.where(wide < 32, win_e[at(8, j), :], win_e[at(1, j), :])) for j in range(10)]
+    y_forward(beyond, pick_m, tmp_a)
+    through_z(tmp_a, zfwd_m, into(late))
+    lxe[0:16, :] = jnp.where(iota((16, LANES), 1) < 64, pick_m[0:16, :], pick_m[90:106, :])
 
     def main_step(a, _):
-        y_forward(a, work, pick_m)
-        through_z(tmp_a, tmp_b, zfwd_m)
-        scale(a, eig_m, eig_m)
-        through_z(tmp_b, tmp_c, zback_m)
-
-        def put(j, value):
-            work[a, j] = value
-
-        y_back(tmp_c, pick_m, put)
+        level = row(eig_m, a) + eig_m[20:36, :]
+        weight = row(lxe, a)
+        for b in range(10):
+            tmp_b[b] = (spec[a, b] + weight * late[b]) / scale(level, eig_m, b)
+        through_z(tmp_b, zback_m, into(tmp_c))
+        y_back(tmp_c, pick_m, into(work, a))
         return 0
 
     lax.fori_loop(0, 10, main_step, 0)
@@ -407,7 +452,7 @@
         x_back(work, edge, pick_m, j, put)
         return 0
 
-    lax.fori_loop(1, 9, solve, 0)
+    lax.fori_loop(1, 9, solve, 0, unroll=8)
 
     def step(n, _):
         columns = [8 * n + m for m in range(8)]
@@ -419,6 +464,7 @@
 
     lax.fori_loop(0, 1, step, 0)
     fine_ref[...] = join_rows(rows_ref[...])
+    copy.wait()
 
 
 def x_back(work, edge, pick, j, put):
@@ -458,16 +504,13 @@
 
 
 def up_kernel(
-    four_ref, own_ref, got_ref, pan_hbm, num_ref, top_ref, fine_ref, out_ref, line_ref, coeff_ref, sums_ref, vertex_ref, low_ref, sems
+    four_ref, got_ref, num_hbm, top_ref, low_ref, fine_ref, out_ref, line_ref, coeff_ref, sums_ref, vertex_ref, num_ref, sems
 ):
     q = lax.axis_index("gy")
-    copies = []
-    for n, (low, high) in enumerate(((0, 64), (64, 255 - TOP))):
-        part = pl.ds(low, high - low)
-        copies.append(pltpu.make_async_copy(pan_hbm.at[pl.ds(TOP + low, high - low), :], low_ref.at[part, :], sems.at[n]))
-        copies[n].start()
+    copy = pltpu.make_async_copy(num_hbm, num_ref, sems.at[0])
+    copy.start()
     line_ref[...] = jnp.zeros((32, LANES), F32)
-    line_ref[0:2, :] = own_ref[0:2, :]
+    line_ref[0:2, :] = four_ref[6:8, :]
     line_ref[2:5, :] = four_ref[3:6, :]
     line_ref[5:8, :] = got_ref[7, 34:37, :]
     for peer in range(8):
@@ -485,26 +528,20 @@
         sums_ref[pl.ds(first, count), :] = total
         sums_ref[pl.ds(first, count), 0:127] = total[:, 0:127] + end
 
-    def top_step(g, _):
+    def step(g, _):
         first = pl.multiple_of(8 * g, 8)
         product(top_ref, first, pl.ds(first, 8), 8)
         return 0
 
-    def low_step(g, _):
-        first = pl.multiple_of(8 * g, 8)
-        product(low_ref, TOP + first, pl.ds(first, 8), 8)
-        return 0
-
-    lax.fori_loop(0, TOP // 8, top_step, 0, unroll=4)
-    copies[0].wait()
-    lax.fori_loop(0, 8, low_step, 0, unroll=4)
-    copies[1].wait()
-    lax.fori_loop(8, (255 - TOP) // 8, low_step, 0, unroll=7)
+    lax.fori_loop(0, TOP // 8, step, 0, unroll=TOP // 16)
+    for low in range(0, 248 - TOP, 8):
+        product(low_ref, TOP + low, pl.ds(low, 8), 8)
     product(low_ref, 248, pl.ds(248 - TOP, 7), 7)
     sums_ref[255:256, :] = jnp.zeros((1, LANES), F32)
     values = jnp.broadcast_to(jnp.sum(sums_ref[...], axis=1, keepdims=True), (256, 17))
     vertex_ref[...] = jnp.zeros((16, LANES), F32)
     rows = iota((256, 17), 0)
+    copy.wait()
     for i in range(5):
         for j in range(3):
             k = 3 * i + j
@@ -540,7 +577,7 @@
         jax.ShapeDtypeStruct(o[0], o[2] if len(o) > 2 else F32) if o[1] is None else o[1](o[0], o[2] if len(o) > 2 else F32)
         for o in outs
     ]
-    spaces = [pltpu.VMEM(s, F32) for s in scratch]
+    spaces = [pltpu.VMEM(s, F32) if isinstance(s, tuple) else s for s in scratch]
     if sems:
         spaces.append(pltpu.SemaphoreType.DMA((sems,)))
     run = pl.pallas_call(
@@ -568,46 +605,45 @@
 def shards(residual, elem_class, basis, eigenvalues, vertex_number, panels):
     field = residual.reshape(512, LANES)
     I32 = jnp.int32
-    pay, own, num, cls, top, res, table, eigen = call(
+    pay, own, cls, top, res, table, eigen = call(
         down_kernel,
         [
-            ((8, 40, 128), VM), ((24, 128), VM), ((5, 3, 17), VM, I32), ((4, 2, 16), VM, I32), ((TOP, 2943), VM),
-            ((512, 128), VM), ((3, 10, 8, 10), VM), ((3, 8, 10), VM),
+            ((8, 40, 128), VM), ((24, 128), VM), ((4, 2, 16), VM, I32), ((TOP, 2943), VM),
+            ((512, 128), VM), ((8, 300), VM), ((8, 30), VM),
         ],
-        [(40, 128), (255 - TOP, 2943)], ins=[pltpu.HBM] * 6, sems=7,
+        [(40, 128), (3, 10, 8, 10), (3, 8, 10), (255 - TOP, 2943), VM((5, 3, 17), I32)], ins=[pltpu.HBM] * 6, sems=7,
     )(field, vertex_number, panels, elem_class, basis.transpose(1, 2, 0, 3), eigenvalues.transpose(1, 0, 2))
     first = spread_to(pay, "gy")
-    tree, four = call(sum_kernel, [((64, 1, 256), VM), ((8, 128), VM)], ins=[None])(first)
+    tree, four = call(sum_kernel, [((64, 1, 256), VM), ((8, 128), VM)], ins=[None, VM])(first, own)
     summed = spread_to(tree, "gx")
     right, left, face = call(
         pack_kernel, [((168, 128), VM), ((168, 128), VM), ((64, 128), VM)], ins=[None, VM, VM, VM], cost=2_000_000_000
     )(first, res, cls, four)
     from_left = lax.ppermute(right, "gx", [(i, i + 1) for i in range(63)])
     from_right = lax.ppermute(left, "gx", [(i + 1, i) for i in range(63)])
-    win, basis2, eigen2, pick, eig, zfwd, zback = call(
-        tile_kernel,
+    spec, sides, pick, eig, table_out = call(
+        spectral_kernel,
         [
-            ((1760, 128), VM), ((8, 300), VM), ((8, 30), VM), ((304, 128), VM), ((40, 128), VM),
-            ((10, 16, 128), VM), ((10, 16, 128), VM),
+            ((10, 10, 16, 128), VM), ((2, 11, 16, 128), VM), ((304, 128), VM), ((40, 128), VM), ((8, 300), VM),
         ],
-        [(512, 128)], ins=[VM] * 4, cost=2_000_000_000,
-    )(res, cls, table, eigen)
-    win, fine, rim = call(
+        [(10, 16, 128), (512, 128), (64, 128), (1760, 128), (10, 10, 16, 128), (10, 16, 128)], ins=[VM] * 5, cost=2_000_000_000,
+    )(res, face, cls, table, eigen)
+    fine, rim, low = call(
         solve_kernel,
-        [((1760, 128), VM), ((512, 128), VM), ((64, 128), VM)],
+        [((512, 128), VM), ((64, 128), VM), ((255 - TOP, 2943), VM)],
         [
             (10, 10, 16, 128), (10, 16, 128), (2, 8, 8, 128), (512, 128), (512, 128),
-            (112, 128), (288, 128), (1760, 128), (304, 128), (40, 128), (10, 16, 128), (10, 16, 128),
-            (56, 128), (8, 128), (5, 10, 16, 128), (10, 16, 128), (10, 16, 128), (10, 16, 128), (64, 128),
+            (64, 128), (288, 128), (1760, 128), (304, 128), (40, 128), (10, 16, 128), (10, 16, 128), (10, 16, 128), (10, 16, 128),
+            (56, 128), (16, 128), (5, 10, 16, 128), (10, 16, 128), (10, 16, 128), (10, 16, 128), (64, 128), (10, 16, 128),
         ],
-        ins=[VM] * 8 + [None, None], cost=1_000_000_000, aliases={0: 0},
-    )(win, basis2, eigen2, pick, eig, zfwd, zback, face, from_left, from_right)
+        ins=[VM] * 6 + [None, None, pltpu.HBM], sems=1, cost=1_000_000_000,
+    )(spec, sides, table_out, eigen, pick, eig, from_left, from_right, panels)
     (pay,) = call(tree_kernel, [((8, 40, 128), VM)], ins=[None, VM, VM, None, None])(summed, rim, four, from_left, from_right)
     second = spread_to(pay, "gy")
     (out,) = call(
-        up_kernel, [((512, 128), None)], [(32, 128), (24, 128), (256, 128), (16, 128), (255 - TOP, 2943)],
-        ins=[VM, VM, None, pltpu.HBM, VM, VM, VM], sems=2,
-    )(four, own, second, panels, num, top, fine)
+        up_kernel, [((512, 128), None)], [(32, 128), (24, 128), (256, 128), (16, 128), VM((5, 3, 17), I32)],
+        ins=[VM, None, pltpu.HBM, VM, VM, VM], sems=1,
+    )(four, second, vertex_number, top, low, fine)
     return out.reshape(residual.shape)
 
 

time: 62.8 us -> 59.5 us (0.947)
  waiting for transfers between devices: 3.92 us -> 1.93 us
  Pallas kernels: 13.9 us -> 12.5 us
    ppermute x1, waiting for transfers between devices: 3.91 us -> 1.88 us  [shards(): from_right = lax.ppermute(left, 'gx', [(i + 1, i) for i in range(63)])]
    pallas_call x7, Pallas kernels: 13.9 us -> 12.5 us  [apply(): return run(*held)]
  transfers between devices with their start and end apart: 3 -> 3, of which waited for: 1 -> 1; matrix products, arithmetic and copies ran while one was open for 0% -> 0% of each run, Pallas kernels for 13% -> 12%
where the time goes in v4:
time: 59.5 us; the launch traced here: 58.7 us
  blocking collectives  25.2 us (42%)
  starting transfers between devices  19 us (32%)
  Pallas kernels  12.5 us (21%)
  waiting for transfers between devices  1.93 us (3%)
    all_to_all x2, blocking collectives, spread_to(): return lax.all_to_all(block, axis, 0, 0, tiled=True)  25.2 us
    all_to_all x1, starting transfers between devices, spread_to(): return lax.all_to_all(block, axis, 0, 0, tiled=True)  14.8 us
    pallas_call x7, Pallas kernels, apply(): return run(*held)  12.5 us
    ppermute x1, starting transfers between devices, shards(): from_left = lax.ppermute(right, 'gx', [(i, i + 1) for i in range(63)])  2.92 us
    ppermute x1, waiting for transfers between devices, shards(): from_right = lax.ppermute(left, 'gx', [(i + 1, i) for i in range(63)])  1.88 us
    ppermute x1, starting transfers between devices, shards(): from_right = lax.ppermute(left, 'gx', [(i + 1, i) for i in range(63)])  1.29 us
  transfers between devices with their start and end apart: 3, of which 1 were waited for; matrix products, arithmetic and copies ran while one was open for 0% of the time, Pallas kernels for 12%

profile of v4, /device:TPU:1, one launch (start us, length us, event | category | flops | bytes accessed | tf_op | source)
XLA Modules:
  0.0 58.7 jit_solution(13890441982835242709)
XLA Ops:
  0.0 2.4 %shard_map.64 = (f32[8,40,128]{2,1,0:T(8,128)S(1)}, f32[24,128]{1,0:T(8,128)S(1)}, s32[4,2,16]{2,1,0:T(2,128)S(1)}, f32[208,2943]{1,0:T(8,128)S(1)}, f32[512,128...) custom-call(f32[512,128]{1,0:T(8,128)} %bitcast.4, s32[5,3,17]{2,1,0:T(4,128)} %num_hbm.3, ...), custom_call_target="tpu_custom_call" | custom-call | tf_op jit(solution)/shard_map/pallas_call | solution.py:596
  2.4 14.8 %all_to_all.15.got_ref = f32[8,40,128]{2,1,0:T(8,128)S(1)} all-to-all(f32[8,40,128]{2,1,0:T(8,128)S(1)} %get-tuple-element.25), channel_id=1, replica_groups=mesh['gx'=64,'gy'=8] {'gy'}, dimensions={0} | all-to-all | bytes 327680 | tf_op jit(solution)/shard_map/all_to_all | solution.py:602
  17.2 0.7 %shard_map.65 = (f32[64,1,256]{2,1,0:T(1,128)}, f32[8,128]{1,0:T(8,128)S(1)}) custom-call(f32[8,40,128]{2,1,0:T(8,128)S(1)} %all_to_all.15.got_ref, f32[24,128]{1,0:T(8,128)S(1)} %get-tuple-element.26.own_ref), custom_call_target="tpu_custom_call" | custom-call | tf_op jit(solution)/shard_map/pallas_call | solution.py:596
  17.9 14.8 %all-to-all-start.1 = ((f32[64,1,256]{2,1,0:T(1,128)}), f32[64,1,256]{2,1,0:T(1,128)S(1)}, u32[]{:S(2)}, u32[]{:S(2)}) async-start(f32[64,1,256]{2,1,0:T(1,128)} %get-tuple-element.28), calls=%async_computation.1 | async-start | bytes 131072 | tf_op jit(solution)/shard_map/all_to_all | solution.py:602
  32.7 2.9 %collective-permute-start = (f32[168,128]{1,0:T(8,128)S(1)}, f32[168,128]{1,0:T(8,128)S(1)}, u32[]{:S(2)}, u32[]{:S(2)}) collective-permute-start(f32[168,128]{1,0:T(8,128)S(1)} %get-tuple-element.39), channel_id=1, source_target_pairs={{0,8},{8,16},{16,24},{24,32},{32,40},{40,48},{48,56},{56,64},{64,7... | collective-permute-start | bytes 258056 | tf_op jit(solution)/shard_map/ppermute | solution.py:622
  35.7 1.3 %collective-permute-start.1 = (f32[168,128]{1,0:T(8,128)S(1)}, f32[168,128]{1,0:T(8,128)S(1)}, u32[]{:S(2)}, u32[]{:S(2)}) collective-permute-start(f32[168,128]{1,0:T(8,128)S(1)} %get-tuple-element.40), channel_id=1, source_target_pairs={{8,0},{16,8},{24,16},{32,24},{40,32},{48,40},{56,48},{64,56},{72,6... | collective-permute-start | bytes 258056 | tf_op jit(solution)/shard_map/ppermute | solution.py:623
  37.0 2.7 %shard_map.67 = (f32[10,10,16,128]{3,2,1,0:T(8,128)S(1)}, f32[2,11,16,128]{3,2,1,0:T(8,128)S(1)}, f32[304,128]{1,0:T(8,128)S(1)}, f32[40,128]{1,0:T(8,128)S(1)}, f32[8,300]{1,0:T(8,128)S(1)}) custom-call(f32[512,128]{1,0:T(8,128)S(1)} %get-tuple-element.29.res_ref, f32[64,128]{1,0:T(8,128)S(1)} %get-tuple-element.31.face_ref, ...), custom_call_target="tpu_custom_call" | custom-call | flops 2000000000 | bytes 5000000 | tf_op jit(solution)/shard_map/pallas_call | solution.py:596
  39.7 0.0 collective-permute-done.from_left
  39.7 1.9 %collective-permute-done.1.from_right = f32[168,128]{1,0:T(8,128)S(1)} collective-permute-done((f32[168,128]{1,0:T(8,128)S(1)}, f32[168,128]{1,0:T(8,128)S(1)}, u32[]{:S(2)}, u32[]{:S(2)}) %collective-permute-start.1) | collective-permute-done | bytes 86048 | tf_op jit(solution)/shard_map/ppermute | solution.py:623
  41.6 4.6 %shard_map.68 = (f32[512,128]{1,0:T(8,128)S(1)}, f32[64,128]{1,0:T(8,128)S(1)}, f32[47,2943]{1,0:T(8,128)S(1)}) custom-call(f32[10,10,16,128]{3,2,1,0:T(8,128)S(1)} %get-tuple-element.34.spec, f32[2,11,16,128]{3,2,1,0:T(8,128)S(1)} %get-tuple-element.35.sides, f32[8,300]{1,0:T(8,128)S(1)} %get-tuple-element.36.table_ref, ...), custom_call_target="tpu_custom_call" | custom-call | flops 1000000000 | bytes 2500000 | tf_op jit(solution)/shard_map/pallas_call | solution.py:596
  46.2 0.0 all-to-all-done.1.got_ref
  46.2 0.2 shard_map.69
  46.4 10.3 %all_to_all.16.got_ref = f32[8,40,128]{2,1,0:T(8,128)S(1)} all-to-all(f32[8,40,128]{2,1,0:T(8,128)S(1)} %shard_map.69), channel_id=1, replica_groups=mesh['gx'=64,'gy'=8] {'gy'}, dimensions={0} | all-to-all | bytes 327680 | tf_op jit(solution)/shard_map/all_to_all | solution.py:602
  56.7 2.0 %shard_map.70 = f32[512,128]{1,0:T(8,128)} custom-call(f32[8,128]{1,0:T(8,128)S(1)} %get-tuple-element.27.four_ref, f32[8,40,128]{2,1,0:T(8,128)S(1)} %all_to_all.16.got_ref, s32[5,3,17]{2,1,0:T(4,128)} %num_hbm.3, f32[208,2943]{1,0:T(8,128)S(1)} %get-tuple-element.42.top_ref, f32[47,2943]{1,0:T(8,128)S(1)} %get-tuple-element.43.low_ref, ...), custom_call_target="tpu_custom_call" | custom-call | tf_op jit(solution)/shard_map/pallas_call | solution.py:596
  (1 shorter events, 0.0 us)
Async XLA Ops:
  17.9 28.3 %all-to-all-start.1 = ((f32[64,1,256]{2,1,0:T(1,128)}), f32[64,1,256]{2,1,0:T(1,128)S(1)}, u32[]{:S(2)}, u32[]{:S(2)}) async-start(f32[64,1,256]{2,1,0:T(1,128)} %get-tuple-element.28), calls=%async_computation.1 | async-start | bytes 131072 | tf_op jit(solution)/shard_map/all_to_all | solution.py:602
  32.7 7.0 %collective-permute-start = (f32[168,128]{1,0:T(8,128)S(1)}, f32[168,128]{1,0:T(8,128)S(1)}, u32[]{:S(2)}, u32[]{:S(2)}) collective-permute-start(f32[168,128]{1,0:T(8,128)S(1)} %get-tuple-element.39), channel_id=1, source_target_pairs={{0,8},{8,16},{16,24},{24,32},{32,40},{40,48},{48,56},{56,64},{64,7... | collective-permute-start | bytes 258056 | tf_op jit(solution)/shard_map/ppermute | solution.py:622
  35.7 5.9 %collective-permute-start.1 = (f32[168,128]{1,0:T(8,128)S(1)}, f32[168,128]{1,0:T(8,128)S(1)}, u32[]{:S(2)}, u32[]{:S(2)}) collective-permute-start(f32[168,128]{1,0:T(8,128)S(1)} %get-tuple-element.40), channel_id=1, source_target_pairs={{8,0},{16,8},{24,16},{32,24},{40,32},{48,40},{56,48},{64,56},{72,6... | collective-permute-start | bytes 258056 | tf_op jit(solution)/shard_map/ppermute | solution.py:623

commit v5 on v4

--- a/solution.py
+++ b/solution.py
@@ -83,15 +83,19 @@
         for i in range(10):
             low = 100 * d + 10 * i
             table_ref[:, low : low + 10] = basis_ref[d, i]
-    for copy in copies[5:]:
-        copy.wait()
+    own_ref[24:40, :] = jnp.zeros((16, LANES), F32)
+    for i in range(5):
+        own_ref[24 + 3 * i : 27 + 3 * i, 0:17] = num_ref[i].astype(F32)
+    copies[5].wait()
     for c, (cut, width) in enumerate(CUTS):
-        piece = jnp.sum(top_ref[:, cut] * ordered[:TOP, :width], axis=0, keepdims=True)
-        piece = piece + jnp.sum(low_ref[:, cut] * ordered[TOP:255, :width], axis=0, keepdims=True)
-        line_ref[8 + c : 9 + c, :width] = piece
+        line_ref[8 + c : 9 + c, :width] = jnp.sum(top_ref[:, cut] * ordered[:TOP, :width], axis=0, keepdims=True)
+    copies[6].wait()
+    for c, (cut, width) in enumerate(CUTS):
+        piece = jnp.sum(low_ref[:, cut] * ordered[TOP:255, :width], axis=0, keepdims=True)
+        line_ref[8 + c : 9 + c, :width] = line_ref[8 + c : 9 + c, :width] + piece
     here = pltpu.roll(line_ref[8:32], 1, 1)
     before = pltpu.roll(line_ref[7:31], 1, 1)
-    own_ref[...] = jnp.where(iota((24, LANES), 1) == 0, before, here)
+    own_ref[0:24, :] = jnp.where(iota((24, LANES), 1) == 0, before, here)
     for peer in range(8):
         pay_ref[peer, 32:35, :] = own_ref[2:5, :]
         pay_ref[peer, 35:37, :] = own_ref[8 + 2 * peer : 10 + 2 * peer, :]
@@ -105,6 +109,7 @@
         total = total + got_ref[peer, 35:40, :]
     four_ref[0:3, :] = total[2:5]
     four_ref[6:8, :] = own_ref[0:2, :]
+    four_ref[8:24, :] = own_ref[24:40, :]
     for level in range(1, 4):
         low = jnp.zeros((1, LANES), F32)
         for peer in range(8):
@@ -298,8 +303,8 @@
     ahead = [win[at(8, j), :] for j in lines]
     back = [win[at(1, j), :] for j in lines]
     for n, j in enumerate(lines):
-        sides[0, j] = back[n]
-        sides[1, j] = ahead[n]
+        sides[0, n] = back[n]
+        sides[1, n] = ahead[n]
         win[at(0, j), :] = jnp.where(wide >= 32, pltpu.roll(ahead[n], 32, 1), 0.0)
         win[at(9, j), :] = jnp.where(wide < 96, pltpu.roll(back[n], 96, 1), 0.0)
 
@@ -325,8 +330,8 @@
 
 
 def solve_kernel(
-    spec, sides, table_ref, eigen_ref, pick_m, eig_m, from_left, from_right, pan_hbm,
-    fine_ref, rim_ref, low_ref,
+    spec, sides, table_ref, eigen_ref, pick_m, eig_m, four_ref, from_left, from_right, pan_hbm,
+    fine_ref, low_ref,
     work, edge, ends, tiles, rows_ref, rows_f, rows_e, win_e, pick_e, eig_e, zfwd_e, zback_e, zfwd_m, zback_m,
     half_e, lxe, work_e, tmp_a, tmp_b, tmp_c, rim_rows, late, sems,
 ):
@@ -377,11 +382,11 @@
 
     second = (wide & 32) != 0
     lines = (1, 2, 3, 4, 5, 6, 7, 8, 10)
-    both = [pltpu.roll(jnp.where(wide < 64, sides[0, j], sides[1, j]), 64, 1) for j in lines]
+    both = [pltpu.roll(jnp.where(wide < 64, sides[0, n], sides[1, n]), 64, 1) for n in range(9)]
     for n, j in enumerate(lines):
         extra = win_e[at(9, j), :]
-        win_e[at(0, j), :] = jnp.where(second, jnp.where(wide >= 64, sides[1, j], both[n]), extra)
-        win_e[at(9, j), :] = jnp.where(second, extra, jnp.where(wide < 64, sides[0, j], both[n]))
+        win_e[at(0, j), :] = jnp.where(second, jnp.where(wide >= 64, sides[1, n], both[n]), extra)
+        win_e[at(9, j), :] = jnp.where(second, extra, jnp.where(wide < 64, sides[0, n], both[n]))
     outer = [win_e[at(i, 10), :] for i in range(10)]
     last = [pltpu.roll(win_e[at(i, 8), :], 16, 1) for i in range(10)]
     first = [pltpu.roll(win_e[at(i, 1), :], 112, 1) for i in range(10)]
@@ -440,7 +445,8 @@
     (parts,) = exchange([[rim_rows[pl.ds(k, 8, stride=8), :] for k in range(8)]])
     for r in range(8):
         rows_f[32 * (r % 2) + 8 * (r // 2) : 32 * (r % 2) + 8 * (r // 2) + 8, :] = parts[r]
-    rim_ref[...] = join_rows(rows_f[0:64, :])
+    fine_ref[576:600, :] = four_ref[...]
+    fine_ref[512:576, :] = join_rows(rows_f[0:64, :])
     inner = upper[0:8]
 
     def solve(j, _):
@@ -463,7 +469,7 @@
         return 0
 
     lax.fori_loop(0, 1, step, 0)
-    fine_ref[...] = join_rows(rows_ref[...])
+    fine_ref[0:512, :] = join_rows(rows_ref[...])
     copy.wait()
 
 
@@ -483,7 +489,7 @@
         put(i, join_z(total, sub, kz))
 
 
-def tree_kernel(got_ref, rim_ref, four_ref, from_left, from_right, pay_ref):
+def tree_kernel(got_ref, fine_ref, from_left, from_right, pay_ref):
     p = lax.axis_index("gx")
     q = lax.axis_index("gy")
     totals = []
@@ -494,9 +500,9 @@
             inside = (t >> bits) == (p >> bits)
             total = total + jnp.where(inside, got_ref[t, :, LANES * n : LANES * (n + 1)], 0.0)
         totals.append(total)
-    four = four_ref[0:3, :] + jnp.where((p & 1) == 0, from_right[164:167, :], from_left[164:167, :])
+    four = fine_ref[576:579, :] + jnp.where((p & 1) == 0, from_right[164:167, :], from_left[164:167, :])
     for peer in range(8):
-        pay_ref[peer, 0:32, :] = jnp.where(peer < q, rim_ref[0:32, :], rim_ref[32:64, :])
+        pay_ref[peer, 0:32, :] = jnp.where(peer < q, fine_ref[512:544, :], fine_ref[544:576, :])
         pay_ref[peer, 32:33, :] = totals[0]
         pay_ref[peer, 33:34, :] = totals[1]
         pay_ref[peer, 34:37, :] = four
@@ -504,14 +510,12 @@
 
 
 def up_kernel(
-    four_ref, got_ref, num_hbm, top_ref, low_ref, fine_ref, out_ref, line_ref, coeff_ref, sums_ref, vertex_ref, num_ref, sems
+    got_ref, top_ref, low_ref, fine_ref, out_ref, line_ref, coeff_ref, sums_ref, vertex_ref
 ):
     q = lax.axis_index("gy")
-    copy = pltpu.make_async_copy(num_hbm, num_ref, sems.at[0])
-    copy.start()
     line_ref[...] = jnp.zeros((32, LANES), F32)
-    line_ref[0:2, :] = four_ref[6:8, :]
-    line_ref[2:5, :] = four_ref[3:6, :]
+    line_ref[0:2, :] = fine_ref[582:584, :]
+    line_ref[2:5, :] = fine_ref[579:582, :]
     line_ref[5:8, :] = got_ref[7, 34:37, :]
     for peer in range(8):
         line_ref[8 + 2 * peer : 10 + 2 * peer, :] = got_ref[peer, 32:34, :]
@@ -540,12 +544,13 @@
     sums_ref[255:256, :] = jnp.zeros((1, LANES), F32)
     values = jnp.broadcast_to(jnp.sum(sums_ref[...], axis=1, keepdims=True), (256, 17))
     vertex_ref[...] = jnp.zeros((16, LANES), F32)
-    rows = iota((256, 17), 0)
-    copy.wait()
+    rows = iota((256, 17), 0).astype(F32)
     for i in range(5):
         for j in range(3):
             k = 3 * i + j
-            vertex_ref[k : k + 1, 0:17] = jnp.sum(jnp.where(num_ref[i, j : j + 1, :] == rows, values, 0.0), axis=0, keepdims=True)
+            vertex_ref[k : k + 1, 0:17] = jnp.sum(
+                jnp.where(fine_ref[584 + k : 585 + k, 0:17] == rows, values, 0.0), axis=0, keepdims=True
+            )
     depth = hat(iota((LANES, LANES), 1), iota((LANES, LANES), 0)).astype(jnp.bfloat16)
     vertex_ref[...] = moved(vertex_ref[...], depth)
     rise = (2.0 * iota((8, LANES), 0).astype(F32) + 1.0) / 16.0
@@ -608,13 +613,13 @@
     pay, own, cls, top, res, table, eigen = call(
         down_kernel,
         [
-            ((8, 40, 128), VM), ((24, 128), VM), ((4, 2, 16), VM, I32), ((TOP, 2943), VM),
+            ((8, 40, 128), VM), ((40, 128), VM), ((4, 2, 16), VM, I32), ((TOP, 2943), VM),
             ((512, 128), VM), ((8, 300), VM), ((8, 30), VM),
         ],
         [(40, 128), (3, 10, 8, 10), (3, 8, 10), (255 - TOP, 2943), VM((5, 3, 17), I32)], ins=[pltpu.HBM] * 6, sems=7,
     )(field, vertex_number, panels, elem_class, basis.transpose(1, 2, 0, 3), eigenvalues.transpose(1, 0, 2))
     first = spread_to(pay, "gy")
-    tree, four = call(sum_kernel, [((64, 1, 256), VM), ((8, 128), VM)], ins=[None, VM])(first, own)
+    tree, four = call(sum_kernel, [((64, 1, 256), VM), ((24, 128), VM)], ins=[None, VM])(first, own)
     summed = spread_to(tree, "gx")
     right, left, face = call(
         pack_kernel, [((168, 128), VM), ((168, 128), VM), ((64, 128), VM)], ins=[None, VM, VM, VM], cost=2_000_000_000
@@ -624,26 +629,25 @@
     spec, sides, pick, eig, table_out = call(
         spectral_kernel,
         [
-            ((10, 10, 16, 128), VM), ((2, 11, 16, 128), VM), ((304, 128), VM), ((40, 128), VM), ((8, 300), VM),
+            ((10, 10, 16, 128), VM), ((2, 9, 16, 128), VM), ((304, 128), VM), ((40, 128), VM), ((8, 300), VM),
         ],
         [(10, 16, 128), (512, 128), (64, 128), (1760, 128), (10, 10, 16, 128), (10, 16, 128)], ins=[VM] * 5, cost=2_000_000_000,
     )(res, face, cls, table, eigen)
-    fine, rim, low = call(
+    fine, low = call(
         solve_kernel,
-        [((512, 128), VM), ((64, 128), VM), ((255 - TOP, 2943), VM)],
+        [((600, 128), VM), ((255 - TOP, 2943), VM)],
         [
             (10, 10, 16, 128), (10, 16, 128), (2, 8, 8, 128), (512, 128), (512, 128),
             (64, 128), (288, 128), (1760, 128), (304, 128), (40, 128), (10, 16, 128), (10, 16, 128), (10, 16, 128), (10, 16, 128),
             (56, 128), (16, 128), (5, 10, 16, 128), (10, 16, 128), (10, 16, 128), (10, 16, 128), (64, 128), (10, 16, 128),
         ],
-        ins=[VM] * 6 + [None, None, pltpu.HBM], sems=1, cost=1_000_000_000,
-    )(spec, sides, table_out, eigen, pick, eig, from_left, from_right, panels)
-    (pay,) = call(tree_kernel, [((8, 40, 128), VM)], ins=[None, VM, VM, None, None])(summed, rim, four, from_left, from_right)
+        ins=[VM] * 7 + [None, None, pltpu.HBM], sems=1, cost=1_000_000_000,
+    )(spec, sides, table_out, eigen, pick, eig, four, from_left, from_right, panels)
+    (pay,) = call(tree_kernel, [((8, 40, 128), VM)], ins=[None, VM, None, None])(summed, fine, from_left, from_right)
     second = spread_to(pay, "gy")
     (out,) = call(
-        up_kernel, [((512, 128), None)], [(32, 128), (24, 128), (256, 128), (16, 128), VM((5, 3, 17), I32)],
-        ins=[VM, None, pltpu.HBM, VM, VM, VM], sems=1,
-    )(four, second, vertex_number, top, low, fine)
+        up_kernel, [((512, 128), None)], [(32, 128), (24, 128), (256, 128), (16, 128)], ins=[None, VM, VM, VM]
+    )(second, top, low, fine)
     return out.reshape(residual.shape)
 
 

time: 59.5 us -> 60 us (level)
  no operation moved by 1% of the time
where the time goes in v5:
time: 60 us; the launch traced here: 59.2 us
  blocking collectives  25 us (42%)
  starting transfers between devices  19.2 us (32%)
  Pallas kernels  12.9 us (22%)
  waiting for transfers between devices  2.03 us (3%)
    all_to_all x2, blocking collectives, spread_to(): return lax.all_to_all(block, axis, 0, 0, tiled=True)  25 us
    all_to_all x1, starting transfers between devices, spread_to(): return lax.all_to_all(block, axis, 0, 0, tiled=True)  15 us
    pallas_call x7, Pallas kernels, apply(): return run(*held)  12.9 us
    ppermute x1, starting transfers between devices, shards(): from_left = lax.ppermute(right, 'gx', [(i, i + 1) for i in range(63)])  2.85 us
    ppermute x1, waiting for transfers between devices, shards(): from_right = lax.ppermute(left, 'gx', [(i + 1, i) for i in range(63)])  2.02 us
    ppermute x1, starting transfers between devices, shards(): from_right = lax.ppermute(left, 'gx', [(i + 1, i) for i in range(63)])  1.29 us
  transfers between devices with their start and end apart: 3, of which 1 were waited for; matrix products, arithmetic and copies ran while one was open for 0% of the time, Pallas kernels for 12%

profile of v5, /device:TPU:1, one launch (start us, length us, event | category | flops | bytes accessed | tf_op | source)
XLA Modules:
  0.0 59.2 jit_solution(15845929178398269605)
XLA Ops:
  0.0 2.3 %shard_map.64 = (f32[8,40,128]{2,1,0:T(8,128)S(1)}, f32[40,128]{1,0:T(8,128)S(1)}, s32[4,2,16]{2,1,0:T(2,128)S(1)}, f32[208,2943]{1,0:T(8,128)S(1)}, f32[512,128...) custom-call(f32[512,128]{1,0:T(8,128)} %bitcast.4, s32[5,3,17]{2,1,0:T(4,128)} %num_hbm.1, ...), custom_call_target="tpu_custom_call" | custom-call | tf_op jit(solution)/shard_map/pallas_call | solution.py:601
  2.3 14.8 %all_to_all.15.got_ref = f32[8,40,128]{2,1,0:T(8,128)S(1)} all-to-all(f32[8,40,128]{2,1,0:T(8,128)S(1)} %get-tuple-element.24), channel_id=1, replica_groups=mesh['gx'=64,'gy'=8] {'gy'}, dimensions={0} | all-to-all | bytes 327680 | tf_op jit(solution)/shard_map/all_to_all | solution.py:607
  17.2 0.7 %shard_map.65 = (f32[64,1,256]{2,1,0:T(1,128)}, f32[24,128]{1,0:T(8,128)S(1)}) custom-call(f32[8,40,128]{2,1,0:T(8,128)S(1)} %all_to_all.15.got_ref, f32[40,128]{1,0:T(8,128)S(1)} %get-tuple-element.25.own_ref), custom_call_target="tpu_custom_call" | custom-call | tf_op jit(solution)/shard_map/pallas_call | solution.py:601
  17.8 15.0 %all-to-all-start.1 = ((f32[64,1,256]{2,1,0:T(1,128)}), f32[64,1,256]{2,1,0:T(1,128)}, u32[]{:S(2)}, u32[]{:S(2)}) async-start(f32[64,1,256]{2,1,0:T(1,128)} %get-tuple-element.26), calls=%async_computation.1 | async-start | bytes 131072 | tf_op jit(solution)/shard_map/all_to_all | solution.py:607
  32.9 2.8 %collective-permute-start = (f32[168,128]{1,0:T(8,128)S(1)}, f32[168,128]{1,0:T(8,128)S(1)}, u32[]{:S(2)}, u32[]{:S(2)}) collective-permute-start(f32[168,128]{1,0:T(8,128)S(1)} %get-tuple-element.38), channel_id=1, source_target_pairs={{0,8},{8,16},{16,24},{24,32},{32,40},{40,48},{48,56},{56,64},{64,7... | collective-permute-start | bytes 258056 | tf_op jit(solution)/shard_map/ppermute | solution.py:627
  35.8 1.3 %collective-permute-start.1 = (f32[168,128]{1,0:T(8,128)S(1)}, f32[168,128]{1,0:T(8,128)S(1)}, u32[]{:S(2)}, u32[]{:S(2)}) collective-permute-start(f32[168,128]{1,0:T(8,128)S(1)} %get-tuple-element.39), channel_id=1, source_target_pairs={{8,0},{16,8},{24,16},{32,24},{40,32},{48,40},{56,48},{64,56},{72,6... | collective-permute-start | bytes 258056 | tf_op jit(solution)/shard_map/ppermute | solution.py:628
  37.1 2.7 %shard_map.67 = (f32[10,10,16,128]{3,2,1,0:T(8,128)S(1)}, f32[2,9,16,128]{3,2,1,0:T(8,128)S(1)}, f32[304,128]{1,0:T(8,128)S(1)}, f32[40,128]{1,0:T(8,128)S(1)}, f32[8,300]{1,0:T(8,128)S(1)}) custom-call(f32[512,128]{1,0:T(8,128)S(1)} %get-tuple-element.27.res_ref, f32[64,128]{1,0:T(8,128)S(1)} %get-tuple-element.30.face_ref, ...), custom_call_target="tpu_custom_call" | custom-call | flops 2000000000 | bytes 5000000 | tf_op jit(solution)/shard_map/pallas_call | solution.py:601
  39.8 0.0 collective-permute-done.from_left
  39.8 2.0 %collective-permute-done.1.from_right = f32[168,128]{1,0:T(8,128)S(1)} collective-permute-done((f32[168,128]{1,0:T(8,128)S(1)}, f32[168,128]{1,0:T(8,128)S(1)}, u32[]{:S(2)}, u32[]{:S(2)}) %collective-permute-start.1) | collective-permute-done | bytes 86048 | tf_op jit(solution)/shard_map/ppermute | solution.py:628
  41.8 4.6 %shard_map.68 = (f32[600,128]{1,0:T(8,128)S(1)}, f32[47,2943]{1,0:T(8,128)S(1)}) custom-call(f32[10,10,16,128]{3,2,1,0:T(8,128)S(1)} %get-tuple-element.33.spec, f32[2,9,16,128]{3,2,1,0:T(8,128)S(1)} %get-tuple-element.34.sides, f32[8,300]{1,0:T(8,128)S(1)} %get-tuple-element.35.table_ref, f32[8,30]{1,0:T(8,128)S(1)} %get-tuple-element.32.eigen_ref, ...), custom_call_target="tpu_custom_call" | custom-call | flops 1000000000 | bytes 2500000 | tf_op jit(solution)/shard_map/pallas_call | solution.py:601
  46.4 0.0 all-to-all-done.1.got_ref
  46.4 1.0 %shard_map.69 = f32[8,40,128]{2,1,0:T(8,128)S(1)} custom-call(f32[64,1,256]{2,1,0:T(1,128)} %all-to-all-done.1.got_ref, f32[600,128]{1,0:T(8,128)S(1)} %get-tuple-element.40.fine_ref, f32[168,128]{1,0:T(8,128)S(1)} %collective-permute-done.from_left, f32[168,128]{1,0:T(8,128)S(1)} %collective-permute-done.1.from_right), custom_call_target="tpu_custom_call" | custom-call | tf_op jit(solution)/shard_map/pallas_call | solution.py:601
  47.4 10.1 %all_to_all.16.got_ref = f32[8,40,128]{2,1,0:T(8,128)S(1)} all-to-all(f32[8,40,128]{2,1,0:T(8,128)S(1)} %shard_map.69), channel_id=1, replica_groups=mesh['gx'=64,'gy'=8] {'gy'}, dimensions={0} | all-to-all | bytes 327680 | tf_op jit(solution)/shard_map/all_to_all | solution.py:607
  57.6 1.6 %shard_map.70 = f32[512,128]{1,0:T(8,128)} custom-call(f32[8,40,128]{2,1,0:T(8,128)S(1)} %all_to_all.16.got_ref, f32[208,2943]{1,0:T(8,128)S(1)} %get-tuple-element.41.top_ref, f32[47,2943]{1,0:T(8,128)S(1)} %get-tuple-element.42.low_ref, f32[600,128]{1,0:T(8,128)S(1)} %get-tuple-element.40.fine_ref), custom_call_target="tpu_custom_call" | custom-call | tf_op jit(solution)/shard_map/pallas_call | solution.py:601
  (1 shorter events, 0.0 us)
Async XLA Ops:
  17.8 28.6 %all-to-all-start.1 = ((f32[64,1,256]{2,1,0:T(1,128)}), f32[64,1,256]{2,1,0:T(1,128)}, u32[]{:S(2)}, u32[]{:S(2)}) async-start(f32[64,1,256]{2,1,0:T(1,128)} %get-tuple-element.26), calls=%async_computation.1 | async-start | bytes 131072 | tf_op jit(solution)/shard_map/all_to_all | solution.py:607
  32.9 6.9 %collective-permute-start = (f32[168,128]{1,0:T(8,128)S(1)}, f32[168,128]{1,0:T(8,128)S(1)}, u32[]{:S(2)}, u32[]{:S(2)}) collective-permute-start(f32[168,128]{1,0:T(8,128)S(1)} %get-tuple-element.38), channel_id=1, source_target_pairs={{0,8},{8,16},{16,24},{24,32},{32,40},{40,48},{48,56},{56,64},{64,7... | collective-permute-start | bytes 258056 | tf_op jit(solution)/shard_map/ppermute | solution.py:627
  35.8 6.1 %collective-permute-start.1 = (f32[168,128]{1,0:T(8,128)S(1)}, f32[168,128]{1,0:T(8,128)S(1)}, u32[]{:S(2)}, u32[]{:S(2)}) collective-permute-start(f32[168,128]{1,0:T(8,128)S(1)} %get-tuple-element.39), channel_id=1, source_target_pairs={{8,0},{16,8},{24,16},{32,24},{40,32},{48,40},{56,48},{64,56},{72,6... | collective-permute-start | bytes 258056 | tf_op jit(solution)/shard_map/ppermute | solution.py:628

commit v6 on v5

--- a/solution.py
+++ b/solution.py
@@ -446,6 +446,8 @@
     for r in range(8):
         rows_f[32 * (r % 2) + 8 * (r // 2) : 32 * (r % 2) + 8 * (r // 2) + 8, :] = parts[r]
     fine_ref[576:600, :] = four_ref[...]
+    even = lax.axis_index("gx") % 2 == 0
+    fine_ref[576:579, :] = four_ref[0:3, :] + jnp.where(even, from_right[164:167, :], from_left[164:167, :])
     fine_ref[512:576, :] = join_rows(rows_f[0:64, :])
     inner = upper[0:8]
 
@@ -489,7 +491,7 @@
         put(i, join_z(total, sub, kz))
 
 
-def tree_kernel(got_ref, fine_ref, from_left, from_right, pay_ref):
+def tree_kernel(got_ref, fine_ref, pay_ref):
     p = lax.axis_index("gx")
     q = lax.axis_index("gy")
     totals = []
@@ -500,7 +502,7 @@
             inside = (t >> bits) == (p >> bits)
             total = total + jnp.where(inside, got_ref[t, :, LANES * n : LANES * (n + 1)], 0.0)
         totals.append(total)
-    four = fine_ref[576:579, :] + jnp.where((p & 1) == 0, from_right[164:167, :], from_left[164:167, :])
+    four = fine_ref[576:579, :]
     for peer in range(8):
         pay_ref[peer, 0:32, :] = jnp.where(peer < q, fine_ref[512:544, :], fine_ref[544:576, :])
         pay_ref[peer, 32:33, :] = totals[0]
@@ -643,7 +645,7 @@
         ],
         ins=[VM] * 7 + [None, None, pltpu.HBM], sems=1, cost=1_000_000_000,
     )(spec, sides, table_out, eigen, pick, eig, four, from_left, from_right, panels)
-    (pay,) = call(tree_kernel, [((8, 40, 128), VM)], ins=[None, VM, None, None])(summed, fine, from_left, from_right)
+    (pay,) = call(tree_kernel, [((8, 40, 128), VM)], ins=[None, VM])(summed, fine)
     second = spread_to(pay, "gy")
     (out,) = call(
         up_kernel, [((512, 128), None)], [(32, 128), (24, 128), (256, 128), (16, 128)], ins=[None, VM, VM, VM]

time: 60 us -> 58.9 us (0.982)
  Pallas kernels: 12.9 us -> 12.1 us
    pallas_call x7, Pallas kernels: 12.9 us -> 12.1 us  [apply(): return run(*held)]
  transfers between devices with their start and end apart: 3 -> 3, of which waited for: 1 -> 1; matrix products, arithmetic and copies ran while one was open for 0% -> 0% of each run, Pallas kernels for 12% -> 13%
where the time goes in v6:
time: 58.9 us; the launch traced here: 58.2 us
  blocking collectives  25.2 us (43%)
  starting transfers between devices  19 us (32%)
  Pallas kernels  12.1 us (21%)
  waiting for transfers between devices  1.93 us (3%)
    all_to_all x2, blocking collectives, spread_to(): return lax.all_to_all(block, axis, 0, 0, tiled=True)  25.2 us
    all_to_all x1, starting transfers between devices, spread_to(): return lax.all_to_all(block, axis, 0, 0, tiled=True)  14.8 us
    pallas_call x7, Pallas kernels, apply(): return run(*held)  12.1 us
    ppermute x1, starting transfers between devices, shards(): from_left = lax.ppermute(right, 'gx', [(i, i + 1) for i in range(63)])  2.92 us
    ppermute x1, waiting for transfers between devices, shards(): from_right = lax.ppermute(left, 'gx', [(i + 1, i) for i in range(63)])  1.88 us
    ppermute x1, starting transfers between devices, shards(): from_right = lax.ppermute(left, 'gx', [(i + 1, i) for i in range(63)])  1.29 us
  transfers between devices with their start and end apart: 3, of which 1 were waited for; matrix products, arithmetic and copies ran while one was open for 0% of the time, Pallas kernels for 13%

profile of v6, /device:TPU:1, one launch (start us, length us, event | category | flops | bytes accessed | tf_op | source)
XLA Modules:
  0.0 58.2 jit_solution(8080316343953286602)
XLA Ops:
  0.0 2.3 %shard_map.64 = (f32[8,40,128]{2,1,0:T(8,128)S(1)}, f32[40,128]{1,0:T(8,128)S(1)}, s32[4,2,16]{2,1,0:T(2,128)S(1)}, f32[208,2943]{1,0:T(8,128)S(1)}, f32[512,128...) custom-call(f32[512,128]{1,0:T(8,128)} %bitcast.4, s32[5,3,17]{2,1,0:T(4,128)} %num_hbm.1, ...), custom_call_target="tpu_custom_call" | custom-call | tf_op jit(solution)/shard_map/pallas_call | solution.py:603
  2.3 14.8 %all_to_all.15.got_ref = f32[8,40,128]{2,1,0:T(8,128)S(1)} all-to-all(f32[8,40,128]{2,1,0:T(8,128)S(1)} %get-tuple-element.24), channel_id=1, replica_groups=mesh['gx'=64,'gy'=8] {'gy'}, dimensions={0} | all-to-all | bytes 327680 | tf_op jit(solution)/shard_map/all_to_all | solution.py:609
  17.2 0.7 %shard_map.65 = (f32[64,1,256]{2,1,0:T(1,128)}, f32[24,128]{1,0:T(8,128)S(1)}) custom-call(f32[8,40,128]{2,1,0:T(8,128)S(1)} %all_to_all.15.got_ref, f32[40,128]{1,0:T(8,128)S(1)} %get-tuple-element.25.own_ref), custom_call_target="tpu_custom_call" | custom-call | tf_op jit(solution)/shard_map/pallas_call | solution.py:603
  17.8 14.8 %all-to-all-start.1 = ((f32[64,1,256]{2,1,0:T(1,128)}), f32[64,1,256]{2,1,0:T(1,128)S(1)}, u32[]{:S(2)}, u32[]{:S(2)}) async-start(f32[64,1,256]{2,1,0:T(1,128)} %get-tuple-element.26), calls=%async_computation.1 | async-start | bytes 131072 | tf_op jit(solution)/shard_map/all_to_all | solution.py:609
  32.7 2.9 %collective-permute-start = (f32[168,128]{1,0:T(8,128)S(1)}, f32[168,128]{1,0:T(8,128)S(1)}, u32[]{:S(2)}, u32[]{:S(2)}) collective-permute-start(f32[168,128]{1,0:T(8,128)S(1)} %get-tuple-element.38), channel_id=1, source_target_pairs={{0,8},{8,16},{16,24},{24,32},{32,40},{40,48},{48,56},{56,64},{64,7... | collective-permute-start | bytes 258056 | tf_op jit(solution)/shard_map/ppermute | solution.py:629
  35.6 1.3 %collective-permute-start.1 = (f32[168,128]{1,0:T(8,128)S(1)}, f32[168,128]{1,0:T(8,128)S(1)}, u32[]{:S(2)}, u32[]{:S(2)}) collective-permute-start(f32[168,128]{1,0:T(8,128)S(1)} %get-tuple-element.39), channel_id=1, source_target_pairs={{8,0},{16,8},{24,16},{32,24},{40,32},{48,40},{56,48},{64,56},{72,6... | collective-permute-start | bytes 258056 | tf_op jit(solution)/shard_map/ppermute | solution.py:630
  36.9 2.7 %shard_map.67 = (f32[10,10,16,128]{3,2,1,0:T(8,128)S(1)}, f32[2,9,16,128]{3,2,1,0:T(8,128)S(1)}, f32[304,128]{1,0:T(8,128)S(1)}, f32[40,128]{1,0:T(8,128)S(1)}, f32[8,300]{1,0:T(8,128)S(1)}) custom-call(f32[512,128]{1,0:T(8,128)S(1)} %get-tuple-element.27.res_ref, f32[64,128]{1,0:T(8,128)S(1)} %get-tuple-element.30.face_ref, ...), custom_call_target="tpu_custom_call" | custom-call | flops 2000000000 | bytes 5000000 | tf_op jit(solution)/shard_map/pallas_call | solution.py:603
  39.6 0.0 collective-permute-done.from_left
  39.6 1.9 %collective-permute-done.1.from_right = f32[168,128]{1,0:T(8,128)S(1)} collective-permute-done((f32[168,128]{1,0:T(8,128)S(1)}, f32[168,128]{1,0:T(8,128)S(1)}, u32[]{:S(2)}, u32[]{:S(2)}) %collective-permute-start.1) | collective-permute-done | bytes 86048 | tf_op jit(solution)/shard_map/ppermute | solution.py:630
  41.5 4.6 %shard_map.68 = (f32[600,128]{1,0:T(8,128)S(1)}, f32[47,2943]{1,0:T(8,128)S(1)}) custom-call(f32[10,10,16,128]{3,2,1,0:T(8,128)S(1)} %get-tuple-element.33.spec, f32[2,9,16,128]{3,2,1,0:T(8,128)S(1)} %get-tuple-element.34.sides, f32[8,300]{1,0:T(8,128)S(1)} %get-tuple-element.35.table_ref, f32[8,30]{1,0:T(8,128)S(1)} %get-tuple-element.32.eigen_ref, ...), custom_call_target="tpu_custom_call" | custom-call | flops 1000000000 | bytes 2500000 | tf_op jit(solution)/shard_map/pallas_call | solution.py:603
  46.1 0.0 all-to-all-done.1.got_ref
  46.1 0.2 shard_map.69
  46.3 10.3 %all_to_all.16.got_ref = f32[8,40,128]{2,1,0:T(8,128)S(1)} all-to-all(f32[8,40,128]{2,1,0:T(8,128)S(1)} %shard_map.69), channel_id=1, replica_groups=mesh['gx'=64,'gy'=8] {'gy'}, dimensions={0} | all-to-all | bytes 327680 | tf_op jit(solution)/shard_map/all_to_all | solution.py:609
  56.6 1.6 %shard_map.70 = f32[512,128]{1,0:T(8,128)} custom-call(f32[8,40,128]{2,1,0:T(8,128)S(1)} %all_to_all.16.got_ref, f32[208,2943]{1,0:T(8,128)S(1)} %get-tuple-element.41.top_ref, f32[47,2943]{1,0:T(8,128)S(1)} %get-tuple-element.42.low_ref, f32[600,128]{1,0:T(8,128)S(1)} %get-tuple-element.40.fine_ref), custom_call_target="tpu_custom_call" | custom-call | tf_op jit(solution)/shard_map/pallas_call | solution.py:603
  (1 shorter events, 0.0 us)
Async XLA Ops:
  17.8 28.3 %all-to-all-start.1 = ((f32[64,1,256]{2,1,0:T(1,128)}), f32[64,1,256]{2,1,0:T(1,128)S(1)}, u32[]{:S(2)}, u32[]{:S(2)}) async-start(f32[64,1,256]{2,1,0:T(1,128)} %get-tuple-element.26), calls=%async_computation.1 | async-start | bytes 131072 | tf_op jit(solution)/shard_map/all_to_all | solution.py:609
  32.7 7.0 %collective-permute-start = (f32[168,128]{1,0:T(8,128)S(1)}, f32[168,128]{1,0:T(8,128)S(1)}, u32[]{:S(2)}, u32[]{:S(2)}) collective-permute-start(f32[168,128]{1,0:T(8,128)S(1)} %get-tuple-element.38), channel_id=1, source_target_pairs={{0,8},{8,16},{16,24},{24,32},{32,40},{40,48},{48,56},{56,64},{64,7... | collective-permute-start | bytes 258056 | tf_op jit(solution)/shard_map/ppermute | solution.py:629
  35.6 5.9 %collective-permute-start.1 = (f32[168,128]{1,0:T(8,128)S(1)}, f32[168,128]{1,0:T(8,128)S(1)}, u32[]{:S(2)}, u32[]{:S(2)}) collective-permute-start(f32[168,128]{1,0:T(8,128)S(1)} %get-tuple-element.39), channel_id=1, source_target_pairs={{8,0},{16,8},{24,16},{32,24},{40,32},{48,40},{56,48},{64,56},{72,6... | collective-permute-start | bytes 258056 | tf_op jit(solution)/shard_map/ppermute | solution.py:630

commit v7 on v6

--- a/solution.py
+++ b/solution.py
@@ -83,9 +83,10 @@
         for i in range(10):
             low = 100 * d + 10 * i
             table_ref[:, low : low + 10] = basis_ref[d, i]
-    own_ref[24:40, :] = jnp.zeros((16, LANES), F32)
-    for i in range(5):
-        own_ref[24 + 3 * i : 27 + 3 * i, 0:17] = num_ref[i].astype(F32)
+    own_ref[24:40, :] = jnp.full((16, LANES), -1.0, F32)
+    for k in range(15):
+        low = 17 * (k % 7)
+        own_ref[24 + k // 7 : 25 + k // 7, low : low + 17] = num_ref[k // 3, k % 3 : k % 3 + 1, :].astype(F32)
     copies[5].wait()
     for c, (cut, width) in enumerate(CUTS):
         line_ref[8 + c : 9 + c, :width] = jnp.sum(top_ref[:, cut] * ordered[:TOP, :width], axis=0, keepdims=True)
@@ -544,15 +545,14 @@
         product(low_ref, TOP + low, pl.ds(low, 8), 8)
     product(low_ref, 248, pl.ds(248 - TOP, 7), 7)
     sums_ref[255:256, :] = jnp.zeros((1, LANES), F32)
-    values = jnp.broadcast_to(jnp.sum(sums_ref[...], axis=1, keepdims=True), (256, 17))
+    values = jnp.broadcast_to(jnp.sum(sums_ref[...], axis=1, keepdims=True), (256, LANES))
     vertex_ref[...] = jnp.zeros((16, LANES), F32)
-    rows = iota((256, 17), 0).astype(F32)
-    for i in range(5):
-        for j in range(3):
-            k = 3 * i + j
-            vertex_ref[k : k + 1, 0:17] = jnp.sum(
-                jnp.where(fine_ref[584 + k : 585 + k, 0:17] == rows, values, 0.0), axis=0, keepdims=True
-            )
+    rows = iota((256, LANES), 0).astype(F32)
+    for g in range(3):
+        line = jnp.sum(jnp.where(fine_ref[584 + g : 585 + g, :] == rows, values, 0.0), axis=0, keepdims=True)
+        for k in range(7 * g, min(7 * g + 7, 15)):
+            low = 17 * (k % 7)
+            vertex_ref[k : k + 1, 0:17] = line[:, low : low + 17]
     depth = hat(iota((LANES, LANES), 1), iota((LANES, LANES), 0)).astype(jnp.bfloat16)
     vertex_ref[...] = moved(vertex_ref[...], depth)
     rise = (2.0 * iota((8, LANES), 0).astype(F32) + 1.0) / 16.0

time: 58.9 us -> 58.8 us (level)
  no operation moved by 1% of the time
where the time goes in v7:
time: 58.8 us; the launch traced here: 58.1 us
  blocking collectives  25.2 us (43%)
  starting transfers between devices  19 us (32%)
  Pallas kernels  12 us (20%)
  waiting for transfers between devices  1.93 us (3%)
    all_to_all x2, blocking collectives, spread_to(): return lax.all_to_all(block, axis, 0, 0, tiled=True)  25.2 us
    all_to_all x1, starting transfers between devices, spread_to(): return lax.all_to_all(block, axis, 0, 0, tiled=True)  14.8 us
    pallas_call x7, Pallas kernels, apply(): return run(*held)  12 us
    ppermute x1, starting transfers between devices, shards(): from_left = lax.ppermute(right, 'gx', [(i, i + 1) for i in range(63)])  2.92 us
    ppermute x1, waiting for transfers between devices, shards(): from_right = lax.ppermute(left, 'gx', [(i + 1, i) for i in range(63)])  1.88 us
    ppermute x1, starting transfers between devices, shards(): from_right = lax.ppermute(left, 'gx', [(i + 1, i) for i in range(63)])  1.29 us
  transfers between devices with their start and end apart: 3, of which 1 were waited for; matrix products, arithmetic and copies ran while one was open for 0% of the time, Pallas kernels for 13%

profile of v7, /device:TPU:1, one launch (start us, length us, event | category | flops | bytes accessed | tf_op | source)
XLA Modules:
  0.0 58.1 jit_solution(13204697493173880864)
XLA Ops:
  0.0 2.3 %shard_map.64 = (f32[8,40,128]{2,1,0:T(8,128)S(1)}, f32[40,128]{1,0:T(8,128)S(1)}, s32[4,2,16]{2,1,0:T(2,128)S(1)}, f32[208,2943]{1,0:T(8,128)S(1)}, f32[512,128...) custom-call(f32[512,128]{1,0:T(8,128)} %bitcast.4, s32[5,3,17]{2,1,0:T(4,128)} %num_hbm.1, ...), custom_call_target="tpu_custom_call" | custom-call | tf_op jit(solution)/shard_map/pallas_call | solution.py:603
  2.3 14.8 %all_to_all.15.got_ref = f32[8,40,128]{2,1,0:T(8,128)S(1)} all-to-all(f32[8,40,128]{2,1,0:T(8,128)S(1)} %get-tuple-element.24), channel_id=1, replica_groups=mesh['gx'=64,'gy'=8] {'gy'}, dimensions={0} | all-to-all | bytes 327680 | tf_op jit(solution)/shard_map/all_to_all | solution.py:609
  17.2 0.7 %shard_map.65 = (f32[64,1,256]{2,1,0:T(1,128)}, f32[24,128]{1,0:T(8,128)S(1)}) custom-call(f32[8,40,128]{2,1,0:T(8,128)S(1)} %all_to_all.15.got_ref, f32[40,128]{1,0:T(8,128)S(1)} %get-tuple-element.25.own_ref), custom_call_target="tpu_custom_call" | custom-call | tf_op jit(solution)/shard_map/pallas_call | solution.py:603
  17.8 14.8 %all-to-all-start.1 = ((f32[64,1,256]{2,1,0:T(1,128)}), f32[64,1,256]{2,1,0:T(1,128)S(1)}, u32[]{:S(2)}, u32[]{:S(2)}) async-start(f32[64,1,256]{2,1,0:T(1,128)} %get-tuple-element.26), calls=%async_computation.1 | async-start | bytes 131072 | tf_op jit(solution)/shard_map/all_to_all | solution.py:609
  32.7 2.9 %collective-permute-start = (f32[168,128]{1,0:T(8,128)S(1)}, f32[168,128]{1,0:T(8,128)S(1)}, u32[]{:S(2)}, u32[]{:S(2)}) collective-permute-start(f32[168,128]{1,0:T(8,128)S(1)} %get-tuple-element.38), channel_id=1, source_target_pairs={{0,8},{8,16},{16,24},{24,32},{32,40},{40,48},{48,56},{56,64},{64,7... | collective-permute-start | bytes 258056 | tf_op jit(solution)/shard_map/ppermute | solution.py:629
  35.6 1.3 %collective-permute-start.1 = (f32[168,128]{1,0:T(8,128)S(1)}, f32[168,128]{1,0:T(8,128)S(1)}, u32[]{:S(2)}, u32[]{:S(2)}) collective-permute-start(f32[168,128]{1,0:T(8,128)S(1)} %get-tuple-element.39), channel_id=1, source_target_pairs={{8,0},{16,8},{24,16},{32,24},{40,32},{48,40},{56,48},{64,56},{72,6... | collective-permute-start | bytes 258056 | tf_op jit(solution)/shard_map/ppermute | solution.py:630
  36.9 2.7 %shard_map.67 = (f32[10,10,16,128]{3,2,1,0:T(8,128)S(1)}, f32[2,9,16,128]{3,2,1,0:T(8,128)S(1)}, f32[304,128]{1,0:T(8,128)S(1)}, f32[40,128]{1,0:T(8,128)S(1)}, f32[8,300]{1,0:T(8,128)S(1)}) custom-call(f32[512,128]{1,0:T(8,128)S(1)} %get-tuple-element.27.res_ref, f32[64,128]{1,0:T(8,128)S(1)} %get-tuple-element.30.face_ref, ...), custom_call_target="tpu_custom_call" | custom-call | flops 2000000000 | bytes 5000000 | tf_op jit(solution)/shard_map/pallas_call | solution.py:603
  39.6 0.0 collective-permute-done.from_left
  39.6 1.9 %collective-permute-done.1.from_right = f32[168,128]{1,0:T(8,128)S(1)} collective-permute-done((f32[168,128]{1,0:T(8,128)S(1)}, f32[168,128]{1,0:T(8,128)S(1)}, u32[]{:S(2)}, u32[]{:S(2)}) %collective-permute-start.1) | collective-permute-done | bytes 86048 | tf_op jit(solution)/shard_map/ppermute | solution.py:630
  41.5 4.6 %shard_map.68 = (f32[600,128]{1,0:T(8,128)S(1)}, f32[47,2943]{1,0:T(8,128)S(1)}) custom-call(f32[10,10,16,128]{3,2,1,0:T(8,128)S(1)} %get-tuple-element.33.spec, f32[2,9,16,128]{3,2,1,0:T(8,128)S(1)} %get-tuple-element.34.sides, f32[8,300]{1,0:T(8,128)S(1)} %get-tuple-element.35.table_ref, f32[8,30]{1,0:T(8,128)S(1)} %get-tuple-element.32.eigen_ref, ...), custom_call_target="tpu_custom_call" | custom-call | flops 1000000000 | bytes 2500000 | tf_op jit(solution)/shard_map/pallas_call | solution.py:603
  46.1 0.0 all-to-all-done.1.got_ref
  46.1 0.2 shard_map.69
  46.3 10.3 %all_to_all.16.got_ref = f32[8,40,128]{2,1,0:T(8,128)S(1)} all-to-all(f32[8,40,128]{2,1,0:T(8,128)S(1)} %shard_map.69), channel_id=1, replica_groups=mesh['gx'=64,'gy'=8] {'gy'}, dimensions={0} | all-to-all | bytes 327680 | tf_op jit(solution)/shard_map/all_to_all | solution.py:609
  56.6 1.5 %shard_map.70 = f32[512,128]{1,0:T(8,128)} custom-call(f32[8,40,128]{2,1,0:T(8,128)S(1)} %all_to_all.16.got_ref, f32[208,2943]{1,0:T(8,128)S(1)} %get-tuple-element.41.top_ref, f32[47,2943]{1,0:T(8,128)S(1)} %get-tuple-element.42.low_ref, f32[600,128]{1,0:T(8,128)S(1)} %get-tuple-element.40.fine_ref), custom_call_target="tpu_custom_call" | custom-call | tf_op jit(solution)/shard_map/pallas_call | solution.py:603
  (1 shorter events, 0.0 us)
Async XLA Ops:
  17.8 28.3 %all-to-all-start.1 = ((f32[64,1,256]{2,1,0:T(1,128)}), f32[64,1,256]{2,1,0:T(1,128)S(1)}, u32[]{:S(2)}, u32[]{:S(2)}) async-start(f32[64,1,256]{2,1,0:T(1,128)} %get-tuple-element.26), calls=%async_computation.1 | async-start | bytes 131072 | tf_op jit(solution)/shard_map/all_to_all | solution.py:609
  32.7 7.0 %collective-permute-start = (f32[168,128]{1,0:T(8,128)S(1)}, f32[168,128]{1,0:T(8,128)S(1)}, u32[]{:S(2)}, u32[]{:S(2)}) collective-permute-start(f32[168,128]{1,0:T(8,128)S(1)} %get-tuple-element.38), channel_id=1, source_target_pairs={{0,8},{8,16},{16,24},{24,32},{32,40},{40,48},{48,56},{56,64},{64,7... | collective-permute-start | bytes 258056 | tf_op jit(solution)/shard_map/ppermute | solution.py:629
  35.6 5.9 %collective-permute-start.1 = (f32[168,128]{1,0:T(8,128)S(1)}, f32[168,128]{1,0:T(8,128)S(1)}, u32[]{:S(2)}, u32[]{:S(2)}) collective-permute-start(f32[168,128]{1,0:T(8,128)S(1)} %get-tuple-element.39), channel_id=1, source_target_pairs={{8,0},{16,8},{24,16},{32,24},{40,32},{48,40},{56,48},{64,56},{72,6... | collective-permute-start | bytes 258056 | tf_op jit(solution)/shard_map/ppermute | solution.py:630

commit v8 on v7

--- a/solution.py
+++ b/solution.py
@@ -434,7 +434,7 @@
         y_back(tmp_c, pick_m, into(work, a))
         return 0
 
-    lax.fori_loop(0, 10, main_step, 0)
+    lax.fori_loop(0, 10, main_step, 0, unroll=5)
 
     for n, j in ((0, 0), (1, 9)):
         def put_end(i, main, n=n):

time: 58.8 us -> 58.7 us (level)
  transfers between devices with their start and end apart: 3 -> 3, of which waited for: 1 -> 2; matrix products, arithmetic and copies ran while one was open for 0% -> 0% of each run, Pallas kernels for 13% -> 12%
where the time goes in v8:
time: 58.7 us; the launch traced here: 58.1 us
  blocking collectives  25.2 us (43%)
  starting transfers between devices  19 us (32%)
  Pallas kernels  11.9 us (20%)
  waiting for transfers between devices  2.01 us (3%)
    all_to_all x2, blocking collectives, spread_to(): return lax.all_to_all(block, axis, 0, 0, tiled=True)  25.2 us
    all_to_all x1, starting transfers between devices, spread_to(): return lax.all_to_all(block, axis, 0, 0, tiled=True)  14.8 us
    pallas_call x7, Pallas kernels, apply(): return run(*held)  11.9 us
    ppermute x1, starting transfers between devices, shards(): from_left = lax.ppermute(right, 'gx', [(i, i + 1) for i in range(63)])  2.92 us
    ppermute x1, waiting for transfers between devices, shards(): from_right = lax.ppermute(left, 'gx', [(i + 1, i) for i in range(63)])  1.88 us
    ppermute x1, starting transfers between devices, shards(): from_right = lax.ppermute(left, 'gx', [(i + 1, i) for i in range(63)])  1.29 us
  transfers between devices with their start and end apart: 3, of which 2 were waited for; matrix products, arithmetic and copies ran while one was open for 0% of the time, Pallas kernels for 12%

profile of v8, /device:TPU:1, one launch (start us, length us, event | category | flops | bytes accessed | tf_op | source)
XLA Modules:
  0.0 58.1 jit_solution(15075724987388600786)
XLA Ops:
  0.0 2.3 %shard_map.64 = (f32[8,40,128]{2,1,0:T(8,128)S(1)}, f32[40,128]{1,0:T(8,128)S(1)}, s32[4,2,16]{2,1,0:T(2,128)S(1)}, f32[208,2943]{1,0:T(8,128)S(1)}, f32[512,128...) custom-call(f32[512,128]{1,0:T(8,128)} %bitcast.4, s32[5,3,17]{2,1,0:T(4,128)} %num_hbm.1, ...), custom_call_target="tpu_custom_call" | custom-call | tf_op jit(solution)/shard_map/pallas_call | solution.py:603
  2.3 14.8 %all_to_all.15.got_ref = f32[8,40,128]{2,1,0:T(8,128)S(1)} all-to-all(f32[8,40,128]{2,1,0:T(8,128)S(1)} %get-tuple-element.24), channel_id=1, replica_groups=mesh['gx'=64,'gy'=8] {'gy'}, dimensions={0} | all-to-all | bytes 327680 | tf_op jit(solution)/shard_map/all_to_all | solution.py:609
  17.2 0.7 %shard_map.65 = (f32[64,1,256]{2,1,0:T(1,128)}, f32[24,128]{1,0:T(8,128)S(1)}) custom-call(f32[8,40,128]{2,1,0:T(8,128)S(1)} %all_to_all.15.got_ref, f32[40,128]{1,0:T(8,128)S(1)} %get-tuple-element.25.own_ref), custom_call_target="tpu_custom_call" | custom-call | tf_op jit(solution)/shard_map/pallas_call | solution.py:603
  17.8 14.8 %all-to-all-start.1 = ((f32[64,1,256]{2,1,0:T(1,128)}), f32[64,1,256]{2,1,0:T(1,128)S(1)}, u32[]{:S(2)}, u32[]{:S(2)}) async-start(f32[64,1,256]{2,1,0:T(1,128)} %get-tuple-element.26), calls=%async_computation.1 | async-start | bytes 131072 | tf_op jit(solution)/shard_map/all_to_all | solution.py:609
  32.7 2.9 %collective-permute-start = (f32[168,128]{1,0:T(8,128)S(1)}, f32[168,128]{1,0:T(8,128)S(1)}, u32[]{:S(2)}, u32[]{:S(2)}) collective-permute-start(f32[168,128]{1,0:T(8,128)S(1)} %get-tuple-element.38), channel_id=1, source_target_pairs={{0,8},{8,16},{16,24},{24,32},{32,40},{40,48},{48,56},{56,64},{64,7... | collective-permute-start | bytes 258056 | tf_op jit(solution)/shard_map/ppermute | solution.py:629
  35.6 1.3 %collective-permute-start.1 = (f32[168,128]{1,0:T(8,128)S(1)}, f32[168,128]{1,0:T(8,128)S(1)}, u32[]{:S(2)}, u32[]{:S(2)}) collective-permute-start(f32[168,128]{1,0:T(8,128)S(1)} %get-tuple-element.39), channel_id=1, source_target_pairs={{8,0},{16,8},{24,16},{32,24},{40,32},{48,40},{56,48},{64,56},{72,6... | collective-permute-start | bytes 258056 | tf_op jit(solution)/shard_map/ppermute | solution.py:630
  36.9 2.7 %shard_map.67 = (f32[10,10,16,128]{3,2,1,0:T(8,128)S(1)}, f32[2,9,16,128]{3,2,1,0:T(8,128)S(1)}, f32[304,128]{1,0:T(8,128)S(1)}, f32[40,128]{1,0:T(8,128)S(1)}, f32[8,300]{1,0:T(8,128)S(1)}) custom-call(f32[512,128]{1,0:T(8,128)S(1)} %get-tuple-element.27.res_ref, f32[64,128]{1,0:T(8,128)S(1)} %get-tuple-element.30.face_ref, ...), custom_call_target="tpu_custom_call" | custom-call | flops 2000000000 | bytes 5000000 | tf_op jit(solution)/shard_map/pallas_call | solution.py:603
  39.6 0.0 collective-permute-done.from_left
  39.6 1.9 %collective-permute-done.1.from_right = f32[168,128]{1,0:T(8,128)S(1)} collective-permute-done((f32[168,128]{1,0:T(8,128)S(1)}, f32[168,128]{1,0:T(8,128)S(1)}, u32[]{:S(2)}, u32[]{:S(2)}) %collective-permute-start.1) | collective-permute-done | bytes 86048 | tf_op jit(solution)/shard_map/ppermute | solution.py:630
  41.5 4.5 %shard_map.68 = (f32[600,128]{1,0:T(8,128)S(1)}, f32[47,2943]{1,0:T(8,128)S(1)}) custom-call(f32[10,10,16,128]{3,2,1,0:T(8,128)S(1)} %get-tuple-element.33.spec, f32[2,9,16,128]{3,2,1,0:T(8,128)S(1)} %get-tuple-element.34.sides, f32[8,300]{1,0:T(8,128)S(1)} %get-tuple-element.35.table_ref, f32[8,30]{1,0:T(8,128)S(1)} %get-tuple-element.32.eigen_ref, ...), custom_call_target="tpu_custom_call" | custom-call | flops 1000000000 | bytes 2500000 | tf_op jit(solution)/shard_map/pallas_call | solution.py:603
  46.0 0.1 all-to-all-done.1.got_ref
  46.1 0.2 shard_map.69
  46.3 10.3 %all_to_all.16.got_ref = f32[8,40,128]{2,1,0:T(8,128)S(1)} all-to-all(f32[8,40,128]{2,1,0:T(8,128)S(1)} %shard_map.69), channel_id=1, replica_groups=mesh['gx'=64,'gy'=8] {'gy'}, dimensions={0} | all-to-all | bytes 327680 | tf_op jit(solution)/shard_map/all_to_all | solution.py:609
  56.6 1.5 %shard_map.70 = f32[512,128]{1,0:T(8,128)} custom-call(f32[8,40,128]{2,1,0:T(8,128)S(1)} %all_to_all.16.got_ref, f32[208,2943]{1,0:T(8,128)S(1)} %get-tuple-element.41.top_ref, f32[47,2943]{1,0:T(8,128)S(1)} %get-tuple-element.42.low_ref, f32[600,128]{1,0:T(8,128)S(1)} %get-tuple-element.40.fine_ref), custom_call_target="tpu_custom_call" | custom-call | tf_op jit(solution)/shard_map/pallas_call | solution.py:603
  (1 shorter events, 0.0 us)
Async XLA Ops:
  17.8 28.3 %all-to-all-start.1 = ((f32[64,1,256]{2,1,0:T(1,128)}), f32[64,1,256]{2,1,0:T(1,128)S(1)}, u32[]{:S(2)}, u32[]{:S(2)}) async-start(f32[64,1,256]{2,1,0:T(1,128)} %get-tuple-element.26), calls=%async_computation.1 | async-start | bytes 131072 | tf_op jit(solution)/shard_map/all_to_all | solution.py:609
  32.7 7.0 %collective-permute-start = (f32[168,128]{1,0:T(8,128)S(1)}, f32[168,128]{1,0:T(8,128)S(1)}, u32[]{:S(2)}, u32[]{:S(2)}) collective-permute-start(f32[168,128]{1,0:T(8,128)S(1)} %get-tuple-element.38), channel_id=1, source_target_pairs={{0,8},{8,16},{16,24},{24,32},{32,40},{40,48},{48,56},{56,64},{64,7... | collective-permute-start | bytes 258056 | tf_op jit(solution)/shard_map/ppermute | solution.py:629
  35.6 5.9 %collective-permute-start.1 = (f32[168,128]{1,0:T(8,128)S(1)}, f32[168,128]{1,0:T(8,128)S(1)}, u32[]{:S(2)}, u32[]{:S(2)}) collective-permute-start(f32[168,128]{1,0:T(8,128)S(1)} %get-tuple-element.39), channel_id=1, source_target_pairs={{8,0},{16,8},{24,16},{32,24},{40,32},{48,40},{56,48},{64,56},{72,6... | collective-permute-start | bytes 258056 | tf_op jit(solution)/shard_map/ppermute | solution.py:630
